TPU v7x, 32 devices: a whole 2x2x4 slice. The times are simulated.
32 devices in a mesh: group: 2 (over y), tile: 4 (over z), sect: 2 (over x), sub: 2 (over core).
Axes of the slice: x: 2, y: 2, z: 4, core: 2. Of those that a mesh axis runs over, the one named last changes fastest.
Arguments:
- air_state: float32 [4, 80, 64, 256], P(None, ('sect', 'sub'), ('group', 'tile')), parts along dimension 2, may hold values from -3 to 3
- fire_level: float32 [640, 2560], P(('group', 'tile'), ('sect', 'sub')), parts along dimension 0, may hold values from 0.2 to 3
- fuel_left: float32 [640, 2560], P(('group', 'tile'), ('sect', 'sub')), parts along dimension 0, may hold values from 0.3 to 1
- fuel_class: int32 [640, 2560], P(('group', 'tile'), ('sect', 'sub')), parts along dimension 0, may hold values from 0 to 12
- ignition: int32 [640, 2560], P(('group', 'tile'), ('sect', 'sub')), parts along dimension 0, may hold values from 0 to 4, as said below
- plan: int32 [4], replicated, may hold values from 1 to 3
- spread_rate: float32 [13], replicated, may hold values from 0.05 to 0.3
- burn_time: float32 [13], replicated, may hold values from 0.5 to 8
- heat_content: float32 [13], replicated, may hold values from 1 to 10
- moisture_content: float32 [13], replicated, may hold values from 0.1 to 1
Outputs:
- air_out: float32 [4, 80, 64, 256], P(None, ('sect', 'sub'), ('group', 'tile')), parts along dimension 2
- level_out: float32 [640, 2560], P(('group', 'tile'), ('sect', 'sub')), parts along dimension 0
- fuel_out: float32 [640, 2560], P(('group', 'tile'), ('sect', 'sub')), parts along dimension 0
There are 2 independent parts, one for each index of `group`. A program takes and returns all parts, laid end to end along the dimension named above; an argument that names none is the same for every part. Nothing has to cross between parts.
Inputs may be any that keep to these rules, and one draw needn't show every extreme that they name: `ignition`: A cell with value c is ignited at the start of coupling step c; cells with value 4 are not ignited in the window. Ignited cells lie in scattered atmosphere columns. The plan is shared by all scenarios.
All inputs are finite; a program needn't handle non-finite values.
Results may differ from a plain program's by a relative error of at most 0.0001.
Values sent between devices are 32-bit elements; how exact they have to be, the bound alone decides.
No kernel may reach another device: no remote copies, remote signals or barrier semaphores. Data moves between devices by JAX's collectives and lax.ppermute only.
A program may use at most 128 MiB of HBM per device.

v0:
```python
import jax
import jax.numpy as jnp
from jax import lax
from jax.sharding import PartitionSpec as P

LEVELS = 80
REFINE = 10
STEPS = 4
SUBSTEPS = 4


air_delta = 0.1
diffusion = 0.2
heat_gain = 20.0
vapour_gain = 20.0
lift_gain = 0.3
wind_gain = 0.5
fire_delta = 0.15


def padded_2(block, sides, width):
    for axis, dim in sides:
        count = lax.axis_size(axis)
        forward = [(i, i + 1) for i in range(count - 1)]
        backward = [(target, source) for source, target in forward]
        low = lax.ppermute(
            lax.slice_in_dim(block, block.shape[dim] - width, None, axis=dim), axis, forward
        )
        high = lax.ppermute(lax.slice_in_dim(block, 0, width, axis=dim), axis, backward)
        block = jnp.concatenate([low, block, high], axis=dim)
    return block


def level_weights(layer_count):
    height = jnp.arange(layer_count).astype(jnp.float32)
    profile = jnp.exp(-2.0 * height / layer_count)
    profile = layer_count * profile / jnp.sum(profile)
    column = jnp.exp(-height / layer_count)
    column = column / jnp.sum(column)
    return (profile, column)


def lookup(tables, classes):
    result = jnp.zeros((tables.shape[0],) + classes.shape, jnp.float32)
    for category in range(tables.shape[1]):
        result = jnp.where((classes == category)[None], tables[:, category][:, None, None], result)
    return result


def mend_edges(padded, at_start, at_end, axis_dim):
    extent = padded.shape[axis_dim]
    leading = lax.slice_in_dim(padded, 0, 1, axis=axis_dim)
    following = lax.slice_in_dim(padded, 1, 2, axis=axis_dim)
    interior = lax.slice_in_dim(padded, 1, extent - 1, axis=axis_dim)
    preceding = lax.slice_in_dim(padded, extent - 2, extent - 1, axis=axis_dim)
    trailing = lax.slice_in_dim(padded, extent - 1, extent, axis=axis_dim)
    return jnp.concatenate(
        [jnp.where(at_start, following, leading), interior, jnp.where(at_end, preceding, trailing)],
        axis=axis_dim,
    )


def advance_level(padded, rate_cell, wind_east, wind_north, fire_step):
    at_centre = padded[1:-1, 1:-1]
    at_west = padded[:-2, 1:-1]
    at_east = padded[2:, 1:-1]
    at_south = padded[1:-1, :-2]
    at_north = padded[1:-1, 2:]
    steepness = jnp.sqrt(
        jnp.maximum(at_centre - at_west, 0.0) ** 2
        + jnp.minimum(at_east - at_centre, 0.0) ** 2
        + jnp.maximum(at_centre - at_south, 0.0) ** 2
        + jnp.minimum(at_north - at_centre, 0.0) ** 2
    )
    grad_east = 0.5 * (at_east - at_west)
    grad_north = 0.5 * (at_north - at_south)
    tailwind = (wind_east * grad_east + wind_north * grad_north) / jnp.sqrt(
        grad_east * grad_east + grad_north * grad_north + 1.0
    )
    fire_speed = rate_cell * (1.0 + wind_gain * jnp.maximum(tailwind, 0.0))
    return at_centre - fire_step * fire_speed * steepness


def burn_fuel(level_set, fuel_now, energy, vapour, burnout, heat_cell, moist_cell, fire_step):
    burning = jnp.clip(0.5 - level_set, 0.0, 1.0)
    remain = fuel_now * jnp.exp(-fire_step * burning / burnout)
    consumed = fuel_now - remain
    return (remain, energy + consumed * heat_cell, vapour + consumed * moist_cell)


def fire_core(
    padded,
    fuel_now,
    energy,
    vapour,
    rate_cell,
    burnout,
    heat_cell,
    moist_cell,
    wind_east,
    wind_north,
    fire_step,
):
    level_set = advance_level(padded, rate_cell, wind_east, wind_north, fire_step)
    remain, energy, vapour = burn_fuel(
        level_set, fuel_now, energy, vapour, burnout, heat_cell, moist_cell, fire_step
    )
    return (level_set, remain, energy, vapour)


def air_core(padded, flux_coarse, profile):
    at_centre = padded[:, 1:-1, 1:-1, 1:-1]
    at_below = padded[:, :-2, 1:-1, 1:-1]
    at_above = padded[:, 2:, 1:-1, 1:-1]
    at_west = padded[:, 1:-1, :-2, 1:-1]
    at_east = padded[:, 1:-1, 2:, 1:-1]
    at_south = padded[:, 1:-1, 1:-1, :-2]
    at_north = padded[:, 1:-1, 1:-1, 2:]
    speed_east = at_centre[2]
    speed_north = at_centre[3]
    advect = (
        jnp.maximum(speed_east, 0.0) * (at_centre - at_west)
        + jnp.minimum(speed_east, 0.0) * (at_east - at_centre)
        + jnp.maximum(speed_north, 0.0) * (at_centre - at_south)
        + jnp.minimum(speed_north, 0.0) * (at_north - at_centre)
    )
    diffused = at_west + at_east + at_south + at_north + at_below + at_above - 6.0 * at_centre
    lift_east = at_east[0] + 0.6 * at_east[1] - (at_west[0] + 0.6 * at_west[1])
    lift_north = at_north[0] + 0.6 * at_north[1] - (at_south[0] + 0.6 * at_south[1])
    heights = profile[:, None, None]
    forcing = jnp.stack(
        [
            heat_gain * flux_coarse[0][None] * heights,
            vapour_gain * flux_coarse[1][None] * heights,
            0.5 * lift_gain * lift_east,
            0.5 * lift_gain * lift_north,
        ]
    )
    return at_centre + air_delta * (diffusion * diffused - advect + forcing)


def coarsen(fine_field, refine_by):
    channels, row_count, col_count = fine_field.shape
    blocks = fine_field.reshape(
        channels, row_count // refine_by, refine_by, col_count // refine_by, refine_by
    )
    return jnp.sum(blocks, axis=(2, 4)) / (refine_by * refine_by)


def local(
    air_state,
    fire_level,
    fuel_left,
    fuel_class,
    ignition,
    plan,
    spread_rate,
    burn_time,
    heat_content,
    moisture_content,
):
    tables = jnp.stack([spread_rate, burn_time, heat_content, moisture_content])
    cell_values = lookup(tables, fuel_class)
    rate_cell = cell_values[0]
    burnout = cell_values[1]
    heat_cell = cell_values[2]
    moist_cell = cell_values[3]
    profile, column = level_weights(LEVELS)
    tile_at = lax.axis_index("tile")
    tile_count = lax.axis_size("tile")
    band_at = lax.axis_index(("sect", "sub"))
    band_count = lax.axis_size(("sect", "sub"))
    tile_first = tile_at == 0
    tile_final = tile_at == tile_count - 1
    band_first = band_at == 0
    band_final = band_at == band_count - 1
    air_field = air_state
    local_depth = air_state.shape[1]
    offset = band_at * local_depth
    profile_part = lax.dynamic_slice_in_dim(profile, offset, local_depth)
    column_part = lax.dynamic_slice_in_dim(column, offset, local_depth)
    level_set = fire_level
    fuel_now = fuel_left
    for coupling in range(STEPS):
        partial_value = jnp.sum(column_part[None, :, None, None] * air_field[2:4], axis=1)
        wind_coarse = lax.psum_scatter(
            partial_value, ("sect", "sub"), scatter_dimension=2, tiled=True
        )
        wind_fine = jnp.repeat(jnp.repeat(wind_coarse, REFINE, axis=1), REFINE, axis=2)
        fire_step = plan[coupling].astype(jnp.float32) * fire_delta
        level_set = jnp.where(ignition <= coupling, jnp.minimum(level_set, -1.0), level_set)
        energy = jnp.zeros_like(level_set)
        vapour = jnp.zeros_like(level_set)
        for sub_step in range(SUBSTEPS):
            padded = padded_2(level_set, (("tile", 0), (("sect", "sub"), 1)), 1)
            padded = mend_edges(padded, tile_first, tile_final, 0)
            padded = mend_edges(padded, band_first, band_final, 1)
            level_set, fuel_now, energy, vapour = fire_core(
                padded,
                fuel_now,
                energy,
                vapour,
                rate_cell,
                burnout,
                heat_cell,
                moist_cell,
                wind_fine[0],
                wind_fine[1],
                fire_step,
            )
        flux_coarse = coarsen(jnp.stack([energy, vapour]), REFINE)
        flux_whole = lax.all_gather(flux_coarse, ("sect", "sub"), axis=2, tiled=True)
        padded_air = padded_2(air_field, (("tile", 2), (("sect", "sub"), 1)), 1)
        padded_air = jnp.pad(padded_air, ((0, 0), (0, 0), (0, 0), (1, 1)))
        air_field = air_core(padded_air, flux_whole, profile_part)
    return (air_field, level_set, fuel_now)


def solution(mesh):
    placed = (
        P(None, ("sect", "sub"), ("group", "tile"), None),
        P(("group", "tile"), ("sect", "sub")),
        P(("group", "tile"), ("sect", "sub")),
        P(("group", "tile"), ("sect", "sub")),
        P(("group", "tile"), ("sect", "sub")),
        P(),
        P(),
        P(),
        P(),
        P(),
    )
    return jax.shard_map(
        local,
        mesh=mesh,
        in_specs=placed,
        out_specs=(
            P(None, ("sect", "sub"), ("group", "tile"), None),
            P(("group", "tile"), ("sect", "sub")),
            P(("group", "tile"), ("sect", "sub")),
        ),
        check_vma=False,
    )
```

profile of v0, /device:TPU:1, one launch (start us, length us, event | category | flops | bytes accessed | tf_op | source)
XLA Modules:
  0.0 516.2 jit_solution(6921379794625309916)
XLA Ops:
  8.3 4.2 collective-permute-start.4
  20.0 4.0 collective-permute-start.6
  30.6 8.9 %reduce-scatter.13.cloned.1.call-done = f32[64,16]{1,0:T(8,128)} async-done(((f32[256,16]{1,0:T(8,128)}), f32[64,16]{1,0:T(8,128)}) %reduce-scatter.13.cloned.1.call-update) | async-done | bytes 4112
  52.0 4.6 collective-permute-start.10
  58.6 3.4 collective-permute-done.11
  68.2 4.6 collective-permute-start
  83.4 4.3 collective-permute-start.16
  108.6 3.6 stack.85
  113.8 3.6 stack.84
  120.5 4.6 all_gather.12
  125.6 3.5 collective-permute-start.26
  148.4 17.2 %reduce-scatter.15.cloned.1.call-done = f32[64,16]{1,0:T(8,128)} async-done(((f32[256,16]{1,0:T(8,128)}), f32[64,16]{1,0:T(8,128)}) %reduce-scatter.15.cloned.1.call-update) | async-done | bytes 4112
  177.1 4.6 collective-permute-start.30
  183.7 3.4 collective-permute-done.31
  223.3 4.0 collective-permute-start.44
  229.6 4.3 stack.89
  236.5 4.3 stack.88
  243.6 7.1 %all_gather.13 = f32[2,8,256]{1,0,2:T(2,128)S(1)} all-gather(f32[2,8,64]{1,0,2:T(2,128)S(1)} %copy.237), channel_id=1, replica_groups=mesh['group'=2,'tile'=4,'sect'=2,'sub'=2] {'sect','sub'}, dimensions={2}, use_global_device_ids=true | all-gather | bytes 20480 | tf_op jit(solution)/shard_map/all_gather | solution.py:212
  272.7 17.8 %reduce-scatter.17.cloned.1.call-done = f32[64,16]{1,0:T(8,128)} async-done(((f32[256,16]{1,0:T(8,128)}), f32[64,16]{1,0:T(8,128)}) %reduce-scatter.17.cloned.1.call-update) | async-done | bytes 4112
  303.6 4.6 collective-permute-start.50
  327.5 3.4 collective-permute-done.55
  349.7 4.0 collective-permute-start.64
  355.3 4.3 stack.93
  362.2 4.3 stack.92
  369.3 7.1 %all_gather.14 = f32[2,8,256]{1,0,2:T(2,128)S(1)} all-gather(f32[2,8,64]{1,0,2:T(2,128)S(1)} %copy.252), channel_id=1, replica_groups=mesh['group'=2,'tile'=4,'sect'=2,'sub'=2] {'sect','sub'}, dimensions={2}, use_global_device_ids=true | all-gather | bytes 20480 | tf_op jit(solution)/shard_map/all_gather | solution.py:212
  398.3 17.8 %reduce-scatter.19.cloned.1.call-done = f32[64,16]{1,0:T(8,128)} async-done(((f32[256,16]{1,0:T(8,128)}), f32[64,16]{1,0:T(8,128)}) %reduce-scatter.19.cloned.1.call-update) | async-done | bytes 4112
  429.3 4.6 collective-permute-start.70
  435.9 3.4 collective-permute-done.71
  453.2 3.4 collective-permute-done.75
  476.3 4.3 stack.97
  483.3 4.3 stack.96
  490.4 6.5 %all_gather.15 = f32[2,8,256]{1,0,2:T(2,128)S(1)} all-gather(f32[2,8,64]{1,0,2:T(2,128)S(1)} %copy.267), channel_id=1, replica_groups=mesh['group'=2,'tile'=4,'sect'=2,'sub'=2] {'sect','sub'}, dimensions={2}, use_global_device_ids=true | all-gather | bytes 20480 | tf_op jit(solution)/shard_map/all_gather | solution.py:212
  (551 shorter events, 312.3 us)
Async XLA Ops:
  7.2 32.3 %reduce-scatter.13.cloned.1.call-start = ((), (), s32[]{:S(2)}) async-start(), calls=%async_computation.4 | async-start | bytes 163840
  8.3 11.6 %collective-permute-start.4 = (f32[1,640]{1,0:T(1,128)S(1)}, f32[1,640]{1,0:T(1,128)S(1)}, u32[]{:S(2)}, u32[]{:S(2)}) collective-permute-start(f32[1,640]{1,0:T(1,128)S(1)} %get-tuple-element.187), channel_id=1, source_target_pairs={{0,4},{4,8},{8,12},{1,5},{5,9},{9,13},{2,6},{6,10},{10,14},{3,7},{... | collective-permute-start | bytes 7688 | tf_op jit(solution)/shard_map/ppermute | solution.py:26
  12.5 7.4 %collective-permute-start.5 = (f32[1,640]{1,0:T(1,128)S(1)}, f32[1,640]{1,0:T(1,128)S(1)}, u32[]{:S(2)}, u32[]{:S(2)}) collective-permute-start(f32[1,640]{1,0:T(1,128)S(1)} %get-tuple-element.188), channel_id=1, source_target_pairs={{4,0},{8,4},{12,8},{5,1},{9,5},{13,9},{6,2},{10,6},{14,10},{7,3},{... | collective-permute-start | bytes 7688 | tf_op jit(solution)/shard_map/ppermute | solution.py:29
  17.7 148.0 %reduce-scatter.15.cloned.1.call-start = ((), (), s32[]{:S(2)}) async-start(), calls=%async_computation.5 | async-start | bytes 163840
  20.0 6.5 %collective-permute-start.6 = (f32[82,1]{1,0:T(8,128)S(1)}, f32[82,1]{1,0:T(8,128)S(1)}, u32[]{:S(2)}, u32[]{:S(2)}) collective-permute-start(f32[82,1]{1,0:T(8,128)S(1)} %get-tuple-element.155), channel_id=1, source_target_pairs={{0,1},{1,2},{2,3},{4,5},{5,6},{6,7},{8,9},{9,10},{10,11},{12,13},{... | collective-permute-start | bytes 992 | tf_op jit(solution)/shard_map/ppermute | solution.py:26
  52.0 6.6 %collective-permute-start.10 = (f32[82,1]{1,0:T(8,128)S(1)}, f32[82,1]{1,0:T(8,128)S(1)}, u32[]{:S(2)}, u32[]{:S(2)}) collective-permute-start(f32[82,1]{1,0:T(8,128)S(1)} %get-tuple-element.153), channel_id=1, source_target_pairs={{0,1},{1,2},{2,3},{4,5},{5,6},{6,7},{8,9},{9,10},{10,11},{12,13},{... | collective-permute-start | bytes 992 | tf_op jit(solution)/shard_map/ppermute | solution.py:26
  63.1 11.0 %collective-permute-start.12 = (f32[1,640]{1,0:T(1,128)S(1)}, f32[1,640]{1,0:T(1,128)S(1)}, u32[]{:S(2)}, u32[]{:S(2)}) collective-permute-start(f32[1,640]{1,0:T(1,128)S(1)} %get-tuple-element.183), channel_id=1, source_target_pairs={{0,4},{4,8},{8,12},{1,5},{5,9},{9,13},{2,6},{6,10},{10,14},{3,7},{... | collective-permute-start | bytes 7688 | tf_op jit(solution)/shard_map/ppermute | solution.py:26
  66.2 7.9 %collective-permute-start.13 = (f32[1,640]{1,0:T(1,128)S(1)}, f32[1,640]{1,0:T(1,128)S(1)}, u32[]{:S(2)}, u32[]{:S(2)}) collective-permute-start(f32[1,640]{1,0:T(1,128)S(1)} %get-tuple-element.184), channel_id=1, source_target_pairs={{4,0},{8,4},{12,8},{5,1},{9,5},{13,9},{6,2},{10,6},{14,10},{7,3},{... | collective-permute-start | bytes 7688 | tf_op jit(solution)/shard_map/ppermute | solution.py:29
  68.2 66.7 %collective-permute-start = (f32[4,20,1,256]{3,1,2,0:T(8,128)}, f32[4,20,1,256]{3,1,2,0:T(8,128)}, u32[]{:S(2)}, u32[]{:S(2)}) collective-permute-start(f32[4,20,1,256]{3,1,2,0:T(8,128)} %get-tuple-element.81), channel_id=1, source_target_pairs={{0,4},{4,8},{8,12},{1,5},{5,9},{9,13},{2,6},{6,10},{10,14},{3,7},{... | collective-permute-start | bytes 245768 | tf_op jit(solution)/shard_map/ppermute | solution.py:26
  72.8 63.3 %collective-permute-start.1 = (f32[4,20,1,256]{3,1,2,0:T(8,128)S(1)}, f32[4,20,1,256]{3,1,2,0:T(8,128)}, u32[]{:S(2)}, u32[]{:S(2)}) collective-permute-start(f32[4,20,1,256]{3,1,2,0:T(8,128)S(1)} %get-tuple-element.80), channel_id=1, source_target_pairs={{4,0},{8,4},{12,8},{5,1},{9,5},{13,9},{6,2},{10,6},{14,10},{7,3},{... | collective-permute-start | bytes 245768 | tf_op jit(solution)/shard_map/ppermute | solution.py:29
  74.2 6.2 %collective-permute-start.14 = (f32[82,1]{1,0:T(8,128)S(1)}, f32[82,1]{1,0:T(8,128)S(1)}, u32[]{:S(2)}, u32[]{:S(2)}) collective-permute-start(f32[82,1]{1,0:T(8,128)S(1)} %get-tuple-element.151), channel_id=1, source_target_pairs={{0,1},{1,2},{2,3},{4,5},{5,6},{6,7},{8,9},{9,10},{10,11},{12,13},{... | collective-permute-start | bytes 992 | tf_op jit(solution)/shard_map/ppermute | solution.py:26
  83.4 6.2 %collective-permute-start.16 = (f32[1,640]{1,0:T(1,128)S(1)}, f32[1,640]{1,0:T(1,128)S(1)}, u32[]{:S(2)}, u32[]{:S(2)}) collective-permute-start(f32[1,640]{1,0:T(1,128)S(1)} %get-tuple-element.181), channel_id=1, source_target_pairs={{0,4},{4,8},{8,12},{1,5},{5,9},{9,13},{2,6},{6,10},{10,14},{3,7},{... | collective-permute-start | bytes 7688 | tf_op jit(solution)/shard_map/ppermute | solution.py:26
  102.6 22.9 %collective-permute-start.24 = (f32[1,640]{1,0:T(1,128)}, f32[1,640]{1,0:T(1,128)S(1)}, u32[]{:S(2)}, u32[]{:S(2)}) collective-permute-start(f32[1,640]{1,0:T(1,128)} %get-tuple-element.179), channel_id=1, source_target_pairs={{0,4},{4,8},{8,12},{1,5},{5,9},{9,13},{2,6},{6,10},{10,14},{3,7},{... | collective-permute-start | bytes 7688 | tf_op jit(solution)/shard_map/ppermute | solution.py:26
  105.1 20.4 %collective-permute-start.25 = (f32[1,640]{1,0:T(1,128)}, f32[1,640]{1,0:T(1,128)S(1)}, u32[]{:S(2)}, u32[]{:S(2)}) collective-permute-start(f32[1,640]{1,0:T(1,128)} %get-tuple-element.180), channel_id=1, source_target_pairs={{4,0},{8,4},{12,8},{5,1},{9,5},{13,9},{6,2},{10,6},{14,10},{7,3},{... | collective-permute-start | bytes 7688 | tf_op jit(solution)/shard_map/ppermute | solution.py:29
  147.5 142.9 %reduce-scatter.17.cloned.1.call-start = ((), (), s32[]{:S(2)}) async-start(), calls=%async_computation.6 | async-start | bytes 163840
  177.1 6.6 %collective-permute-start.30 = (f32[82,1]{1,0:T(8,128)S(1)}, f32[82,1]{1,0:T(8,128)S(1)}, u32[]{:S(2)}, u32[]{:S(2)}) collective-permute-start(f32[82,1]{1,0:T(8,128)S(1)} %get-tuple-element.145), channel_id=1, source_target_pairs={{0,1},{1,2},{2,3},{4,5},{5,6},{6,7},{8,9},{9,10},{10,11},{12,13},{... | collective-permute-start | bytes 992 | tf_op jit(solution)/shard_map/ppermute | solution.py:26
  213.1 9.0 %collective-permute-start.38 = (f32[82,1]{1,0:T(8,128)S(1)}, f32[82,1]{1,0:T(8,128)S(1)}, u32[]{:S(2)}, u32[]{:S(2)}) collective-permute-start(f32[82,1]{1,0:T(8,128)S(1)} %get-tuple-element.141), channel_id=1, source_target_pairs={{0,1},{1,2},{2,3},{4,5},{5,6},{6,7},{8,9},{9,10},{10,11},{12,13},{... | collective-permute-start | bytes 992 | tf_op jit(solution)/shard_map/ppermute | solution.py:26
  219.1 41.8 %collective-permute-start.20 = (f32[4,20,1,256]{3,1,2,0:T(8,128)}, f32[4,20,1,256]{3,1,2,0:T(8,128)S(1)}, u32[]{:S(2)}, u32[]{:S(2)}) collective-permute-start(f32[4,20,1,256]{3,1,2,0:T(8,128)} %get-tuple-element.74), channel_id=1, source_target_pairs={{0,4},{4,8},{8,12},{1,5},{5,9},{9,13},{2,6},{6,10},{10,14},{3,7},{... | collective-permute-start | bytes 245768 | tf_op jit(solution)/shard_map/ppermute | solution.py:26
  220.7 40.2 %collective-permute-start.21 = (f32[4,20,1,256]{3,1,2,0:T(8,128)}, f32[4,20,1,256]{3,1,2,0:T(8,128)S(1)}, u32[]{:S(2)}, u32[]{:S(2)}) collective-permute-start(f32[4,20,1,256]{3,1,2,0:T(8,128)} %get-tuple-element.75), channel_id=1, source_target_pairs={{4,0},{8,4},{12,8},{5,1},{9,5},{13,9},{6,2},{10,6},{14,10},{7,3},{... | collective-permute-start | bytes 245768 | tf_op jit(solution)/shard_map/ppermute | solution.py:29
  223.3 27.7 %collective-permute-start.44 = (f32[1,640]{1,0:T(1,128)S(1)}, f32[1,640]{1,0:T(1,128)S(1)}, u32[]{:S(2)}, u32[]{:S(2)}) collective-permute-start(f32[1,640]{1,0:T(1,128)S(1)} %get-tuple-element.171), channel_id=1, source_target_pairs={{0,4},{4,8},{8,12},{1,5},{5,9},{9,13},{2,6},{6,10},{10,14},{3,7},{... | collective-permute-start | bytes 7688 | tf_op jit(solution)/shard_map/ppermute | solution.py:26
  227.3 23.7 %collective-permute-start.45 = (f32[1,640]{1,0:T(1,128)S(1)}, f32[1,640]{1,0:T(1,128)S(1)}, u32[]{:S(2)}, u32[]{:S(2)}) collective-permute-start(f32[1,640]{1,0:T(1,128)S(1)} %get-tuple-element.172), channel_id=1, source_target_pairs={{4,0},{8,4},{12,8},{5,1},{9,5},{13,9},{6,2},{10,6},{14,10},{7,3},{... | collective-permute-start | bytes 7688 | tf_op jit(solution)/shard_map/ppermute | solution.py:29
  272.4 143.7 %reduce-scatter.19.cloned.1.call-start = ((), (), s32[]{:S(2)}) async-start(), calls=%async_computation.7 | async-start | bytes 163840
  303.6 6.8 %collective-permute-start.50 = (f32[82,1]{1,0:T(8,128)S(1)}, f32[82,1]{1,0:T(8,128)S(1)}, u32[]{:S(2)}, u32[]{:S(2)}) collective-permute-start(f32[82,1]{1,0:T(8,128)S(1)} %get-tuple-element.137), channel_id=1, source_target_pairs={{0,1},{1,2},{2,3},{4,5},{5,6},{6,7},{8,9},{9,10},{10,11},{12,13},{... | collective-permute-start | bytes 992 | tf_op jit(solution)/shard_map/ppermute | solution.py:26
  339.6 8.9 %collective-permute-start.58 = (f32[82,1]{1,0:T(8,128)S(1)}, f32[82,1]{1,0:T(8,128)S(1)}, u32[]{:S(2)}, u32[]{:S(2)}) collective-permute-start(f32[82,1]{1,0:T(8,128)S(1)} %get-tuple-element.133), channel_id=1, source_target_pairs={{0,1},{1,2},{2,3},{4,5},{5,6},{6,7},{8,9},{9,10},{10,11},{12,13},{... | collective-permute-start | bytes 992 | tf_op jit(solution)/shard_map/ppermute | solution.py:26
  345.6 41.0 %collective-permute-start.40 = (f32[4,20,1,256]{3,1,2,0:T(8,128)}, f32[4,20,1,256]{3,1,2,0:T(8,128)S(1)}, u32[]{:S(2)}, u32[]{:S(2)}) collective-permute-start(f32[4,20,1,256]{3,1,2,0:T(8,128)} %get-tuple-element.67), channel_id=1, source_target_pairs={{0,4},{4,8},{8,12},{1,5},{5,9},{9,13},{2,6},{6,10},{10,14},{3,7},{... | collective-permute-start | bytes 245768 | tf_op jit(solution)/shard_map/ppermute | solution.py:26
  347.2 39.4 %collective-permute-start.41 = (f32[4,20,1,256]{3,1,2,0:T(8,128)}, f32[4,20,1,256]{3,1,2,0:T(8,128)S(1)}, u32[]{:S(2)}, u32[]{:S(2)}) collective-permute-start(f32[4,20,1,256]{3,1,2,0:T(8,128)} %get-tuple-element.68), channel_id=1, source_target_pairs={{4,0},{8,4},{12,8},{5,1},{9,5},{13,9},{6,2},{10,6},{14,10},{7,3},{... | collective-permute-start | bytes 245768 | tf_op jit(solution)/shard_map/ppermute | solution.py:29
  349.7 27.1 %collective-permute-start.64 = (f32[1,640]{1,0:T(1,128)S(1)}, f32[1,640]{1,0:T(1,128)S(1)}, u32[]{:S(2)}, u32[]{:S(2)}) collective-permute-start(f32[1,640]{1,0:T(1,128)S(1)} %get-tuple-element.163), channel_id=1, source_target_pairs={{0,4},{4,8},{8,12},{1,5},{5,9},{9,13},{2,6},{6,10},{10,14},{3,7},{... | collective-permute-start | bytes 7688 | tf_op jit(solution)/shard_map/ppermute | solution.py:26
  353.7 23.1 %collective-permute-start.65 = (f32[1,640]{1,0:T(1,128)S(1)}, f32[1,640]{1,0:T(1,128)S(1)}, u32[]{:S(2)}, u32[]{:S(2)}) collective-permute-start(f32[1,640]{1,0:T(1,128)S(1)} %get-tuple-element.164), channel_id=1, source_target_pairs={{4,0},{8,4},{12,8},{5,1},{9,5},{13,9},{6,2},{10,6},{14,10},{7,3},{... | collective-permute-start | bytes 7688 | tf_op jit(solution)/shard_map/ppermute | solution.py:29
  429.3 6.6 %collective-permute-start.70 = (f32[82,1]{1,0:T(8,128)S(1)}, f32[82,1]{1,0:T(8,128)S(1)}, u32[]{:S(2)}, u32[]{:S(2)}) collective-permute-start(f32[82,1]{1,0:T(8,128)S(1)} %get-tuple-element.129), channel_id=1, source_target_pairs={{0,1},{1,2},{2,3},{4,5},{5,6},{6,7},{8,9},{9,10},{10,11},{12,13},{... | collective-permute-start | bytes 992 | tf_op jit(solution)/shard_map/ppermute | solution.py:26
  465.3 8.8 %collective-permute-start.78 = (f32[82,1]{1,0:T(8,128)S(1)}, f32[82,1]{1,0:T(8,128)S(1)}, u32[]{:S(2)}, u32[]{:S(2)}) collective-permute-start(f32[82,1]{1,0:T(8,128)S(1)} %get-tuple-element.125), channel_id=1, source_target_pairs={{0,1},{1,2},{2,3},{4,5},{5,6},{6,7},{8,9},{9,10},{10,11},{12,13},{... | collective-permute-start | bytes 992 | tf_op jit(solution)/shard_map/ppermute | solution.py:26
  471.2 26.2 %collective-permute-start.60 = (f32[4,20,1,256]{3,1,2,0:T(8,128)}, f32[4,20,1,256]{3,1,2,0:T(8,128)S(1)}, u32[]{:S(2)}, u32[]{:S(2)}) collective-permute-start(f32[4,20,1,256]{3,1,2,0:T(8,128)} %get-tuple-element.60), channel_id=1, source_target_pairs={{0,4},{4,8},{8,12},{1,5},{5,9},{9,13},{2,6},{6,10},{10,14},{3,7},{... | collective-permute-start | bytes 245768 | tf_op jit(solution)/shard_map/ppermute | solution.py:26
  472.8 24.5 %collective-permute-start.61 = (f32[4,20,1,256]{3,1,2,0:T(8,128)S(1)}, f32[4,20,1,256]{3,1,2,0:T(8,128)S(1)}, u32[]{:S(2)}, u32[]{:S(2)}) collective-permute-start(f32[4,20,1,256]{3,1,2,0:T(8,128)S(1)} %get-tuple-element.61), channel_id=1, source_target_pairs={{4,0},{8,4},{12,8},{5,1},{9,5},{13,9},{6,2},{10,6},{14,10},{7,3},{... | collective-permute-start | bytes 245768 | tf_op jit(solution)/shard_map/ppermute | solution.py:29
  (91 other events, 627.6 us)
Sparse Core Ops, SparseCore 0:
  17.8 21.6 reduce-scatter.12
  147.7 17.9 reduce-scatter.14
  272.5 17.8 reduce-scatter.16
  398.2 17.8 reduce-scatter.18
where the time goes:
time: 525 us; the launch traced here: 516 us
  starting transfers between devices  197 us (38%)
  waiting for transfers between devices  146 us (28%)
  local copies, waits for them, and re-layouts  85.8 us (16%)
  other arithmetic  42.7 us (8%)
  blocking collectives  25.3 us (5%)
  between operations  19.8 us (4%)
    ppermute x40, starting transfers between devices, padded_2(): lax.ppermute(lax.slice_in_dim(block, block.shape[dim] - width, None, axis...  130 us
    ppermute x40, waiting for transfers between devices, padded_2(): lax.ppermute(lax.slice_in_dim(block, 0, width, axis=dim), axis, backward)  83.7 us
    ppermute x40, starting transfers between devices, padded_2(): lax.ppermute(lax.slice_in_dim(block, 0, width, axis=dim), axis, backward)  66.9 us
    unnamed x8, waiting for transfers between devices  61.7 us
    another operation x16, local copies, waits for them, and re-layouts, local(): flux_coarse = coarsen(jnp.stack([energy, vapour]), REFINE)  51.9 us
    all_gather x4, blocking collectives, local(): lax.all_gather(flux_coarse, ('sect', 'sub'), axis=2, tiled=True)  25.3 us
    broadcast_in_dim x24, local copies, waits for them, and re-layouts, local(): jnp.repeat(jnp.repeat(wind_coarse, REFINE, axis=1), REFINE, axis=2)  12 us
    unnamed x102, local copies, waits for them, and re-layouts  11.6 us
  transfers between devices with their start and end apart: 84, of which 32 were waited for; matrix products, arithmetic and copies ran while one was open for 16% of the time, Pallas kernels for 0%

commit v1 on v0

v1 whole, which is shorter than its diff:
```python
import functools

import jax
import jax.numpy as jnp
import numpy as np
from jax import lax
from jax.experimental import pallas as pl
from jax.experimental.pallas import tpu as pltpu
from jax.sharding import PartitionSpec as P

LEVELS = 80
REFINE = 10
STEPS = 4
SUBSTEPS = 4
NFUEL = 13

LANES = 128
HALO = STEPS
EDGE = HALO * REFINE
PAD = 8

air_delta = 0.1
diffusion = 0.2
heat_gain = 20.0
vapour_gain = 20.0
lift_gain = 0.3
wind_gain = 0.5
fire_delta = 0.15

BANDS = ("sect", "sub")
VMEM_LIMIT = 48 * 1024 * 1024


def iota(shape, dim):
    return lax.broadcasted_iota(jnp.int32, shape, dim)


def roll(value, shift, axis):
    return pltpu.roll(value, shift, axis)


def level_weights(layer_count):
    height = np.arange(layer_count).astype(np.float64)
    profile = np.exp(-2.0 * height / layer_count)
    profile = layer_count * profile / np.sum(profile)
    column = np.exp(-height / layer_count)
    column = column / np.sum(column)
    return profile.astype(np.float32), column.astype(np.float32)


def air_tiles(depth):
    return 2 * depth + -(-depth // 3)


def pack_kernel(bands, at_ref, air_ref, level_ref, fuel_ref, class_ref, ignite_ref, *outs):
    slots, up_ref, down_ref = outs[:bands], outs[bands], outs[bands + 1]
    depth = air_ref.shape[1]
    lane_tiles = air_ref.shape[3] // LANES
    rows, width = level_ref.shape
    lane = iota((8, LANES), 1)
    fields = [ref[...] for ref in (level_ref, fuel_ref)]
    fields += [ref[...].astype(jnp.float32) for ref in (class_ref, ignite_ref)]
    for a, field in enumerate(fields):
        for j in range(width // LANES):
            cols = field[:, j * LANES : (j + 1) * LANES]
            up_ref[a, j] = cols[:EDGE]
            down_ref[a, j] = cols[rows - EDGE :]
    base = air_tiles(depth)
    wide = iota((rows, LANES), 1)
    for pair in range(2):
        first, second = fields[2 * pair], fields[2 * pair + 1]
        at = pl.ds(base + pair * (rows // 8), rows // 8)
        to_next = jnp.where(wide < 64, roll(second[:, width - LANES :], 64, 1), first[:, width - LANES :])
        slots[1][at] = to_next.reshape(rows // 8, 8, LANES)
        to_prev = jnp.where(wide < 64, first[:, :LANES], roll(second[:, :LANES], 64, 1))
        slots[bands - 1][at] = to_prev.reshape(rows // 8, 8, LANES)
    band = at_ref[1]
    for k in range(bands):
        dest = lax.rem(band + k, bands)
        odd = lax.rem(dest, 2)
        own = pl.multiple_of((dest // 2) * LANES, LANES)
        high = (dest + 1) // 2
        right = pl.multiple_of(jnp.minimum(high, lane_tiles - 1) * LANES, LANES)
        left = pl.multiple_of(jnp.maximum(high - 1, 0) * LANES, LANES)
        turn = 64 * odd
        back = 64 - turn
        from_right = lane < 96 - turn
        for l in range(depth):
            for p in range(2):
                first = air_ref[2 * p, l, :, pl.ds(own, LANES)]
                second = air_ref[2 * p + 1, l, :, pl.ds(own, LANES)]
                slots[k][2 * l + p] = jnp.where(lane < 64, roll(first, turn, 1), roll(second, back, 1))
        for g in range(-(-depth // 3)):
            packed = jnp.zeros((8, LANES), jnp.float32)
            for l in range(3 * g, min(3 * g + 3, depth)):
                for f in range(4):
                    j = (l - 3 * g) * 4 + f
                    edge = jnp.where(
                        from_right, air_ref[f, l, :, pl.ds(right, LANES)], air_ref[f, l, :, pl.ds(left, LANES)]
                    )
                    edge = roll(edge, 4 * j + back, 1)
                    here = ((lane >= 4 * j) & (lane < 4 * j + 4)) | ((lane >= 60 + 4 * j) & (lane < 64 + 4 * j))
                    packed = jnp.where(here, edge, packed)
            slots[k][2 * depth + g] = packed


def corner_tiles(next_ref, prev_ref, base, rows):
    lane = iota((rows, LANES), 1)
    result = []
    for pair in range(2):
        at = pl.ds(base + pair * (rows // 8), rows // 8)
        left = prev_ref[at].reshape(rows, LANES)
        right = next_ref[at].reshape(rows, LANES)
        result.append(jnp.where(lane < 64, right, left))
        result.append(roll(jnp.where(lane < 64, left, right), 64, 1))
    return result


def relay_kernel(bands, rows, *refs):
    slots, up_ref, down_ref = refs[:bands], refs[bands], refs[bands + 1]
    tiles = slots[0].shape[0]
    sub = iota((8, LANES), 0)
    for half in range(bands // 2):
        one, two = slots[2 * half], slots[2 * half + 1]

        def body(i, carry, one=one, two=two, half=half):
            first, second = one[i], two[i]
            up_ref[half * tiles + i] = jnp.where(sub < 4, first, roll(second, 4, 0))
            down_ref[half * tiles + i] = jnp.where(sub < 4, roll(first, 4, 0), second)
            return carry

        lax.fori_loop(0, tiles, body, 0)
    corners = corner_tiles(slots[bands - 1], slots[1], tiles, rows)
    base = (bands // 2) * tiles
    count = EDGE // 8
    for a, corner in enumerate(corners):
        at = pl.ds(base + a * count, count)
        up_ref[at] = corner[:EDGE].reshape(count, 8, LANES)
        down_ref[at] = corner[rows - EDGE :].reshape(count, 8, LANES)


def main_kernel(
    bands,
    at_ref,
    plan_ref,
    tables_ref,
    weights_ref,
    level_in,
    fuel_in,
    class_in,
    ignite_in,
    *refs,
):
    slots = refs[:bands]
    fire_up, fire_down, edge_up, edge_down = refs[bands : bands + 4]
    level_out, fuel_out = refs[bands + 4 : bands + 6]
    outs = refs[bands + 6 : 2 * bands + 6]
    (lev_a, lev_b, fuel, ignite, rate, decay, heat, moist, burnt, wind_u, wind_v, energy, vapour, air_a, air_b) = refs[
        2 * bands + 6 :
    ]
    tile, band, tile_count = at_ref[0], at_ref[1], at_ref[2]
    rows, width = level_in.shape
    tiles = width // LANES
    depth = LEVELS // bands
    count = air_tiles(depth)
    own = PAD + EDGE
    span = rows + 2 * EDGE
    lane = iota((8, LANES), 1)

    corners = corner_tiles(slots[bands - 1], slots[1], count, rows)
    base = (bands // 2) * count
    for a, (source, scratch) in enumerate(
        ((level_in, lev_a), (fuel_in, fuel), (class_in, rate), (ignite_in, ignite))
    ):
        for j in range(tiles):
            scratch[j, PAD:own] = fire_up[a, j]
            scratch[j, own : own + rows] = source[:, j * LANES : (j + 1) * LANES].astype(jnp.float32)
            scratch[j, own + rows : own + rows + EDGE] = fire_down[a, j]
        at = pl.ds(base + a * (EDGE // 8), EDGE // 8)
        scratch[tiles, PAD:own] = edge_up[at].reshape(EDGE, LANES)
        scratch[tiles, own : own + rows] = corners[a]
        scratch[tiles, own + rows : own + rows + EDGE] = edge_down[at].reshape(EDGE, LANES)
    spare = jnp.zeros((tiles + 1, PAD, LANES), jnp.float32)
    for scratch in (lev_a, lev_b):
        scratch[:, :PAD] = spare
        scratch[:, PAD + span :] = spare
    for scratch in (energy, vapour):
        scratch[...] = jnp.zeros_like(scratch)

    vectors = []
    for n in range(4):
        vector = jnp.zeros((8, LANES), jnp.float32)
        for category in range(NFUEL):
            vector = jnp.where(lane == category, tables_ref[n, category], vector)
        vectors.append(vector)
    vectors[1] = -1.0 / jnp.where(lane < NFUEL, vectors[1], 1.0)

    def lookup(t, carry):
        at = pl.ds(pl.multiple_of(PAD + 8 * t, 8), 8)
        for j in range(tiles + 1):
            index = rate[j, at].astype(jnp.int32)
            for vector, scratch in zip(vectors, (rate, decay, heat, moist)):
                scratch[j, at] = jnp.take_along_axis(vector, index, axis=1, mode="promise_in_bounds")
        return carry

    lax.fori_loop(0, span // 8, lookup, 0)

    row16 = iota((16, LANES), 0)
    lane16 = iota((16, LANES), 1)
    first_tile, final_tile = tile == 0, tile == tile_count - 1
    first_band, final_band = band == 0, band == bands - 1
    low_row = jnp.where(final_tile, 8, 12)
    high_row = jnp.where(first_tile, 16, 12)
    low_lane = jnp.where(final_band, 64, 68)
    high_lane = jnp.where(first_band, 128, 124)
    inside = ((row16 < low_row) | (row16 >= high_row)) & ((lane16 < low_lane) | (lane16 >= high_lane))
    sub = iota((8, LANES), 0)
    for k in range(bands):
        source = lax.rem(band - k + bands, bands)
        half = k // 2

        def whole(i, k=k, half=half):
            below, above = edge_down[half * count + i], edge_up[half * count + i]
            if k % 2 == 0:
                halo = jnp.where(sub < 4, below, roll(above, 4, 0))
            else:
                halo = jnp.where(sub < 4, roll(below, 4, 0), above)
            return jnp.concatenate([slots[k][i], halo], axis=0)

        for g in range(-(-depth // 3)):
            edges = whole(2 * depth + g)
            for l in range(3 * g, min(3 * g + 3, depth)):
                level_at = source * depth + l + 1
                for p in range(2):
                    both = whole(2 * l + p)
                    for f in range(2):
                        j = (l - 3 * g) * 4 + 2 * p + f
                        inner = both if f == 0 else roll(both, 64, 1)
                        value = jnp.where(lane16 < 64, inner, roll(edges, 64 - 4 * j, 1))
                        air_a[2 * p + f, level_at] = jnp.where(inside, value, 0.0)
    nothing = jnp.zeros((16, LANES), jnp.float32)
    for scratch in (air_a, air_b):
        for f in range(4):
            scratch[f, 0] = nothing
            scratch[f, LEVELS + 1] = nothing

    cell, column = iota((LANES, LANES), 0), iota((LANES, LANES), 1)
    start = jnp.where(
        column < 64 + HALO,
        REFINE * column,
        jnp.where(column >= LANES - HALO, REFINE * column + (tiles + 1) * LANES - REFINE * LANES, -LANES * 1000),
    )
    across = []
    for j in range(tiles + 1):
        place = cell + j * LANES
        across.append(jnp.where((place >= start) & (place < start + REFINE), 1.0, 0.0).astype(jnp.float32))
    cell, column = iota((span, 16), 0), iota((span, 16), 1)
    start = jnp.where(column < 8 + HALO, EDGE + REFINE * column, REFINE * (column - 12))
    along = jnp.where((cell >= start) & (cell < start + REFINE), 1.0, 0.0).astype(jnp.float32)

    def dot(a, b, dims):
        return lax.dot_general(
            a, b, (dims, ((), ())), precision=lax.Precision.HIGHEST, preferred_element_type=jnp.float32
        )

    def first_wind(k, carry):
        weight = weights_ref[1, k]
        return (carry[0] + weight * air_a[2, k + 1], carry[1] + weight * air_a[3, k + 1])

    wind = lax.fori_loop(0, LEVELS, first_wind, (nothing, nothing))

    def mend_rows(scratch):
        @pl.when(first_tile)
        def _():
            for j in range(tiles + 1):
                scratch[j, own - 1 : own] = scratch[j, own : own + 1]

        @pl.when(final_tile)
        def _():
            for j in range(tiles + 1):
                scratch[j, own + rows : own + rows + 1] = scratch[j, own + rows - 1 : own + rows]

    mend_low = first_band & (lane == LANES - 1)
    mend_high = final_band & (lane == 0)

    def mend_lanes(values):
        halo = jnp.where(mend_low, roll(values[0], LANES - 1, 1), values[tiles])
        halo = jnp.where(mend_high, roll(values[tiles - 1], 1, 1), halo)
        return values[:tiles] + [halo]

    state, other = air_a, air_b
    for c in range(STEPS):
        reach = EDGE - REFINE * (c + 1)
        fire_step = plan_ref[c].astype(jnp.float32) * fire_delta
        wide = [dot(w * wind_gain, m, ((1,), (1,))) for w in wind for m in across]
        for j in range(tiles + 1):
            wind_u[j] = dot(along, wide[j], ((1,), (0,)))
            wind_v[j] = dot(along, wide[tiles + 1 + j], ((1,), (0,)))

        def strips(margin):
            return (EDGE - margin) // 8, -(-(EDGE + rows + margin) // 8)

        def kindle(t, carry, c=c):
            at = pl.ds(pl.multiple_of(PAD + 8 * t, 8), 8)
            values = []
            for j in range(tiles + 1):
                value = lev_a[j, at]
                values.append(jnp.where(ignite[j, at] <= c, jnp.minimum(value, -1.0), value))
            for j, value in enumerate(mend_lanes(values)):
                lev_a[j, at] = value
            return carry

        lax.fori_loop(*strips(reach + SUBSTEPS), kindle, 0)
        mend_rows(lev_a)
        before, after = lev_a, lev_b
        for s in range(SUBSTEPS):

            def advance(t, carry, s=s, before=before, after=after):
                row = pl.multiple_of(PAD + 8 * t, 8)
                at = pl.ds(row, 8)
                flat = pl.ds(pl.multiple_of(8 * t, 8), 8)
                centre = [before[j, at] for j in range(tiles + 1)]
                lower = [roll(value, 1, 1) for value in centre]
                upper = [roll(value, LANES - 1, 1) for value in centre]
                result = []
                for j in range(tiles + 1):
                    west = before[j, pl.ds(row - 1, 8)]
                    east = before[j, pl.ds(row + 1, 8)]
                    south = jnp.where(lane == 0, lower[j - 1], lower[j])
                    north = jnp.where(lane == LANES - 1, upper[(j + 1) % (tiles + 1)], upper[j])
                    here = centre[j]
                    back, ahead = here - west, east - here
                    below, above = here - south, north - here
                    a, b = jnp.maximum(back, 0.0), jnp.minimum(ahead, 0.0)
                    d, e = jnp.maximum(below, 0.0), jnp.minimum(above, 0.0)
                    square = (a * a + b * b) + (d * d + e * e)
                    steep = square * lax.rsqrt(jnp.maximum(square, 1.2e-38))
                    gx, gy = back + ahead, below + above
                    tail = (wind_u[j, flat] * gx + wind_v[j, flat] * gy) * lax.rsqrt((gx * gx + 4.0) + gy * gy)
                    speed = (fire_step * rate[j, at]) * (1.0 + jnp.maximum(tail, 0.0))
                    result.append(here - speed * steep)
                for j in range(tiles + 1):
                    burning = jnp.clip(0.5 - result[j], 0.0, 1.0)
                    if s > 0:
                        burning = burning + burnt[j, at]
                    if s < SUBSTEPS - 1:
                        burnt[j, at] = burning
                    else:
                        held = fuel[j, at]
                        remain = held * jnp.exp(burning * (fire_step * decay[j, at]))
                        spent = held - remain
                        fuel[j, at] = remain
                        energy[j, flat] = spent * heat[j, at]
                        vapour[j, flat] = spent * moist[j, at]
                for j, value in enumerate(mend_lanes(result)):
                    after[j, at] = value
                return carry

            lax.fori_loop(*strips(reach + SUBSTEPS - 1 - s), advance, 0)
            if s < SUBSTEPS - 1:
                mend_rows(after)
            before, after = after, before

        flux = []
        for scratch in (energy, vapour):
            total = dot(scratch[0], across[0], ((1,), (0,)))
            for j in range(1, tiles + 1):
                total = total + dot(scratch[j], across[j], ((1,), (0,)))
            flux.append(dot(along, total, ((0,), (0,))) * (1.0 / (REFINE * REFINE)))
        heat_in = flux[0] * (air_delta * heat_gain)
        vapour_in = flux[1] * (air_delta * vapour_gain)

        def air_step(k, state=state, heat_in=heat_in, vapour_in=vapour_in):
            here = [state[f, k + 1] for f in range(4)]
            u, v = here[2], here[3]
            spread = air_delta * diffusion
            to_west = spread + air_delta * jnp.maximum(u, 0.0)
            to_east = spread - air_delta * jnp.minimum(u, 0.0)
            to_south = spread + air_delta * jnp.maximum(v, 0.0)
            to_north = spread - air_delta * jnp.minimum(v, 0.0)
            keep = (1.0 - 2.0 * spread) - ((to_west + to_east) + (to_south + to_north))
            height = weights_ref[0, k]
            sides = []
            result = []
            for f in range(4):
                west, east = roll(here[f], 1, 0), roll(here[f], 15, 0)
                south, north = roll(here[f], 1, 1), roll(here[f], LANES - 1, 1)
                if f < 2:
                    sides.append((east - west, north - south))
                new = keep * here[f] + spread * (state[f, k] + state[f, k + 2])
                new = new + (to_west * west + to_east * east) + (to_south * south + to_north * north)
                if f == 0:
                    new = new + height * heat_in
                elif f == 1:
                    new = new + height * vapour_in
                else:
                    lift = sides[0][f - 2] + 0.6 * sides[1][f - 2]
                    new = new + (0.5 * lift_gain * air_delta) * lift
                result.append(new)
            return result

        if c < STEPS - 1:

            def layer(k, carry, other=other, air_step=air_step):
                result = [jnp.where(inside, new, 0.0) for new in air_step(k)]
                for f in range(4):
                    other[f, k + 1] = result[f]
                weight = weights_ref[1, k]
                return (carry[0] + weight * result[2], carry[1] + weight * result[3])

            wind = lax.fori_loop(0, LEVELS, layer, (nothing, nothing))
            state, other = other, state
        else:
            for k in range(bands):
                first = lax.rem(band + k, bands) * depth

                def final(l, carry, out=outs[k], first=first, air_step=air_step):
                    result = [new[:8] for new in air_step(first + l)]
                    for p in range(2):
                        out[2 * l + p] = jnp.where(lane < 64, result[2 * p], roll(result[2 * p + 1], 64, 1))
                    return carry

                lax.fori_loop(0, depth, final, 0)

    for j in range(tiles):
        level_out[:, j * LANES : (j + 1) * LANES] = lev_a[j, own : own + rows]
        fuel_out[:, j * LANES : (j + 1) * LANES] = fuel[j, own : own + rows]


def unpack_kernel(bands, at_ref, *refs):
    slots, out = refs[:bands], refs[bands]
    depth = out.shape[1]
    lane = iota((8, LANES), 1)
    for k in range(bands):
        source = lax.rem(at_ref[1] - k + bands, bands)
        odd = lax.rem(source, 2)
        cols = pl.ds(pl.multiple_of((source // 2) * LANES, LANES), LANES)
        mine = (lane >= 64 * odd) & (lane < 64 * odd + 64)

        def body(l, carry, slot=slots[k], odd=odd, cols=cols, mine=mine):
            for p in range(2):
                both = slot[2 * l + p]
                for f in range(2):
                    shift = 64 * odd if f == 0 else 64 - 64 * odd
                    old = out[2 * p + f, l, :, cols]
                    out[2 * p + f, l, :, cols] = jnp.where(mine, roll(both, shift, 1), old)
            return carry

        lax.fori_loop(0, depth, body, 0)


def shape(*dims):
    return jax.ShapeDtypeStruct(dims, jnp.float32)


def vmem():
    return pl.BlockSpec(memory_space=pltpu.VMEM)


def smem():
    return pl.BlockSpec(memory_space=pltpu.SMEM)


def local(
    air_state,
    fire_level,
    fuel_left,
    fuel_class,
    ignition,
    plan,
    spread_rate,
    burn_time,
    heat_content,
    moisture_content,
):
    tables = jnp.stack([spread_rate, burn_time, heat_content, moisture_content])
    weights = np.stack(level_weights(LEVELS))
    bands = lax.axis_size(BANDS)
    tile_count = lax.axis_size("tile")
    at = jnp.stack([lax.axis_index("tile"), lax.axis_index(BANDS), tile_count]).astype(jnp.int32)
    depth = air_state.shape[1]
    rows, width = fire_level.shape
    tiles = width // LANES
    count = air_tiles(depth)
    extra = 2 * (rows // 8)
    params = pltpu.CompilerParams(vmem_limit_bytes=VMEM_LIMIT)

    sizes = [count + (extra if k in (1, bands - 1) else 0) for k in range(bands)]
    packed = pl.pallas_call(
        functools.partial(pack_kernel, bands),
        out_shape=[shape(size, 8, LANES) for size in sizes] + [shape(4, tiles, EDGE, LANES)] * 2,
        in_specs=[smem()] + [vmem()] * 5,
        out_specs=[vmem()] * (bands + 2),
        compiler_params=params,
        name="pack",
    )(at, air_state, fire_level, fuel_left, fuel_class, ignition)
    slots, up, down = packed[:bands], packed[bands], packed[bands + 1]

    rise = [(i, i + 1) for i in range(tile_count - 1)]
    sink = [(j, i) for i, j in rise]

    def turn(values):
        moved = [values[0]]
        for k in range(1, bands):
            moved.append(lax.ppermute(values[k], BANDS, [(i, (i + k) % bands) for i in range(bands)]))
        return moved

    fire_up = lax.ppermute(down, "tile", rise)
    fire_down = lax.ppermute(up, "tile", sink)
    slots = turn(slots)
    edges = (bands // 2) * count + 4 * (EDGE // 8)
    up, down = pl.pallas_call(
        functools.partial(relay_kernel, bands, rows),
        out_shape=[shape(edges, 8, LANES)] * 2,
        in_specs=[vmem()] * bands,
        out_specs=[vmem()] * 2,
        compiler_params=params,
        name="relay",
    )(*slots)
    edge_up = lax.ppermute(down, "tile", rise)
    edge_down = lax.ppermute(up, "tile", sink)

    span = rows + 2 * EDGE
    fire = pltpu.VMEM((tiles + 1, span + 2 * PAD, LANES), jnp.float32)
    flat = pltpu.VMEM((tiles + 1, span, LANES), jnp.float32)
    atmosphere = pltpu.VMEM((4, LEVELS + 2, 16, LANES), jnp.float32)
    results = pl.pallas_call(
        functools.partial(main_kernel, bands),
        out_shape=[shape(rows, width)] * 2 + [shape(2 * depth, 8, LANES)] * bands,
        in_specs=[smem()] * 4 + [vmem()] * (4 + bands + 4),
        out_specs=[vmem()] * (2 + bands),
        scratch_shapes=[fire] * 9 + [flat] * 4 + [atmosphere] * 2,
        compiler_params=params,
        name="window",
    )(
        at,
        plan,
        tables,
        weights,
        fire_level,
        fuel_left,
        fuel_class,
        ignition,
        *slots,
        fire_up,
        fire_down,
        edge_up,
        edge_down,
    )
    level_out, fuel_out = results[:2]
    slabs = turn(results[2:])
    air_out = pl.pallas_call(
        functools.partial(unpack_kernel, bands),
        out_shape=shape(*air_state.shape),
        in_specs=[smem()] + [vmem()] * bands,
        out_specs=vmem(),
        compiler_params=params,
        name="unpack",
    )(at, *slabs)
    return (air_out, level_out, fuel_out)


def solution(mesh):
    placed = (
        P(None, ("sect", "sub"), ("group", "tile"), None),
        P(("group", "tile"), ("sect", "sub")),
        P(("group", "tile"), ("sect", "sub")),
        P(("group", "tile"), ("sect", "sub")),
        P(("group", "tile"), ("sect", "sub")),
        P(),
        P(),
        P(),
        P(),
        P(),
    )
    return jax.shard_map(
        local,
        mesh=mesh,
        in_specs=placed,
        out_specs=(
            P(None, ("sect", "sub"), ("group", "tile"), None),
            P(("group", "tile"), ("sect", "sub")),
            P(("group", "tile"), ("sect", "sub")),
        ),
        check_vma=False,
    )
```

time: 525 us -> 164 us (0.31); the launches traced: 516 us -> 163 us
  starting transfers between devices: 197 us -> 17.9 us
  waiting for transfers between devices: 146 us -> 30.1 us
  Pallas kernels: 0 us -> 109 us
  local copies, waits for them, and re-layouts: 85.8 us -> 5.5 us
  other arithmetic: 42.7 us -> 0.09 us
  blocking collectives: 25.3 us -> 0 us
  between operations: 19.8 us -> 0.8 us
    ppermute x80 -> x10, starting transfers between devices: 197 us -> 17.9 us  [the longest x6 8.75 us: turn(): lax.ppermute(values[k], BANDS, [(i, (i + k) % bands) for i in range(bands)])]
    pallas_call x0 -> x4, Pallas kernels: none -> 109 us  [the longest x1 99.5 us: local(): pl.pallas_call(functools.partial(main_kernel, bands), out_shape=[shape(ro...]
    unnamed x8 -> x0, waiting for transfers between devices: 61.7 us -> none
    ppermute x80 -> x10, waiting for transfers between devices: 83.8 us -> 30.1 us  [the longest x6 17.1 us: turn(): lax.ppermute(values[k], BANDS, [(i, (i + k) % bands) for i in range(bands)])]
    another operation x16 -> x0, local copies, waits for them, and re-layouts: 51.9 us -> none  [local(): flux_coarse = coarsen(jnp.stack([energy, vapour]), REFINE)]
    all_gather x4 -> x0, blocking collectives: 25.3 us -> none  [local(): lax.all_gather(flux_coarse, ('sect', 'sub'), axis=2, tiled=True)]
    broadcast_in_dim x48 -> x0, local copies, waits for them, and re-layouts: 12.8 us -> none  [the longest x24 12 us: local(): jnp.repeat(jnp.repeat(wind_coarse, REFINE, axis=1), REFINE, axis=2)]
    add x12 -> x0, other arithmetic: 10.8 us -> none  [the longest x4 6.29 us: air_core(): return at_centre + air_delta * (diffusion * diffused - advect + forcing)]
  transfers between devices with their start and end apart: 84 -> 10, of which waited for: 32 -> 6; matrix products, arithmetic and copies ran while one was open for 16% -> 0% of each run, Pallas kernels for 0% -> 0%
where the time goes in v1:
time: 164 us; the launch traced here: 163 us
  Pallas kernels  109 us (66%)
  waiting for transfers between devices  30.1 us (18%)
  starting transfers between devices  17.9 us (11%)
  local copies, waits for them, and re-layouts  5.5 us (3%)
    pallas_call x1, Pallas kernels, local(): pl.pallas_call(functools.partial(main_kernel, bands), out_shape=[shape(ro...  99.5 us
    ppermute x6, waiting for transfers between devices, turn(): lax.ppermute(values[k], BANDS, [(i, (i + k) % bands) for i in range(bands)])  17.1 us
    ppermute x1, waiting for transfers between devices, local(): fire_up = lax.ppermute(down, 'tile', rise)  9.19 us
    ppermute x6, starting transfers between devices, turn(): lax.ppermute(values[k], BANDS, [(i, (i + k) % bands) for i in range(bands)])  8.75 us
    pallas_call x1, Pallas kernels, local(): pl.pallas_call(functools.partial(unpack_kernel, bands), out_shape=shape(*...  7.08 us
    unnamed x30, local copies, waits for them, and re-layouts  5.5 us
    ppermute x1, starting transfers between devices, local(): fire_up = lax.ppermute(down, 'tile', rise)  4.01 us
    ppermute x1, waiting for transfers between devices, local(): fire_down = lax.ppermute(up, 'tile', sink)  3.86 us
  transfers between devices with their start and end apart: 10, of which 6 were waited for; matrix products, arithmetic and copies ran while one was open for 0% of the time, Pallas kernels for 0%

profile of v1, /device:TPU:1, one launch (start us, length us, event | category | flops | bytes accessed | tf_op | source)
XLA Modules:
  0.0 162.9 jit_solution(10678507831337955373)
XLA Ops:
  0.6 0.1 pad_add_fusion.at_ref
  0.7 0.9 copy-done
  1.6 0.9 copy-done.2
  2.6 0.9 copy-done.4
  3.5 0.9 copy-done.6
  4.4 1.1 copy-done.8
  5.5 1.3 pack.1
  6.9 2.7 %collective-permute-start = (f32[67,8,128]{2,1,0:T(8,128)S(1)}, f32[67,8,128]{2,1,0:T(8,128)S(1)}, u32[]{:S(2)}, u32[]{:S(2)}) collective-permute-start(f32[67,8,128]{2,1,0:T(8,128)S(1)} %get-tuple-element.18), channel_id=1, source_target_pairs={{0,1},{1,2},{2,3},{3,0},{4,5},{5,6},{6,7},{7,4},{8,9},{9,10},{10,1... | collective-permute-start | bytes 823304 | tf_op jit(solution)/shard_map/ppermute | solution.py:505
  9.5 0.2 collective-permute-start.1
  9.7 10.3 %collective-permute-done.1.refs_2_ = f32[47,8,128]{2,1,0:T(8,128)S(1)} collective-permute-done((f32[47,8,128]{2,1,0:T(8,128)S(1)}, f32[47,8,128]{2,1,0:T(8,128)S(1)}, u32[]{:S(2)}, u32[]{:S(2)}) %collective-permute-start.1) | collective-permute-done | bytes 192544 | tf_op jit(solution)/shard_map/ppermute | solution.py:505
  20.0 0.0 copy-start.3
  20.0 0.0 copy-start.5
  20.0 0.0 copy-start.7
  20.0 0.7 relay.1
  20.7 2.5 %collective-permute-start.5 = (f32[114,8,128]{2,1,0:T(8,128)S(1)}, f32[114,8,128]{2,1,0:T(8,128)S(1)}, u32[]{:S(2)}, u32[]{:S(2)}) collective-permute-start(f32[114,8,128]{2,1,0:T(8,128)S(1)} %get-tuple-element.23), channel_id=1, source_target_pairs={{0,4},{4,8},{8,12},{1,5},{5,9},{9,13},{2,6},{6,10},{10,14},{3,7},{... | collective-permute-start | bytes 1400840 | tf_op jit(solution)/shard_map/ppermute | solution.py:520
  23.2 1.3 collective-permute-start.6
  24.5 4.0 %collective-permute-start.3 = (f32[4,5,40,128]{3,2,1,0:T(8,128)S(1)}, f32[4,5,40,128]{3,2,1,0:T(8,128)S(1)}, u32[]{:S(2)}, u32[]{:S(2)}) collective-permute-start(f32[4,5,40,128]{3,2,1,0:T(8,128)S(1)} %get-tuple-element.21), channel_id=1, source_target_pairs={{0,4},{4,8},{8,12},{1,5},{5,9},{9,13},{2,6},{6,10},{10,14},{3,7},{... | collective-permute-start | bytes 1228808 | tf_op jit(solution)/shard_map/ppermute | solution.py:508
  28.6 1.3 collective-permute-start.4
  29.9 0.0 copy-start.11
  29.9 0.0 copy-start.12
  29.9 0.6 copy-done.11
  30.5 0.0 copy-done.12
  30.5 0.0 copy-done.13
  30.6 9.2 %collective-permute-done.3.refs_4_ = f32[4,5,40,128]{3,2,1,0:T(8,128)S(1)} collective-permute-done((f32[4,5,40,128]{3,2,1,0:T(8,128)S(1)}, f32[4,5,40,128]{3,2,1,0:T(8,128)S(1)}, u32[]{:S(2)}, u32[]{:S(2)}) %collective-permute-start.3) | collective-permute-done | bytes 409632 | tf_op jit(solution)/shard_map/ppermute | solution.py:508
  39.8 3.9 %collective-permute-done.4.refs_5_ = f32[4,5,40,128]{3,2,1,0:T(8,128)S(1)} collective-permute-done((f32[4,5,40,128]{3,2,1,0:T(8,128)S(1)}, f32[4,5,40,128]{3,2,1,0:T(8,128)S(1)}, u32[]{:S(2)}, u32[]{:S(2)}) %collective-permute-start.4) | collective-permute-done | bytes 409632 | tf_op jit(solution)/shard_map/ppermute | solution.py:509
  43.7 99.5 %window.1 = (f32[80,640]{1,0:T(8,128)}, f32[80,640]{1,0:T(8,128)}, f32[40,8,128]{2,1,0:T(8,128)S(1)}, f32[40,8,128]{2,1,0:T(8,128)S(1)}, f32[40,8,128]{2,1,0:T(8,128)S(1)}, /*index=5*/f32[40,8,128]{2,1,0:T(8,128)S(1)}) custom-call(s32[3]{0:T(128)S(1)} %pad_add_fusion.at_ref, s32[4]{0:T(128)S(1)} %copy-done.10, f32[4,13]{1,0:T(4,128)S(1)} %pad_maximum_fusion.tables_ref, ...), custom_call_target="tpu_custom_call" | custom-call | tf_op jit(solution)/shard_map/window/pallas_call | solution.py:527
  143.1 5.5 %collective-permute-start.7 = (f32[40,8,128]{2,1,0:T(8,128)S(1)}, f32[40,8,128]{2,1,0:T(8,128)S(1)}, u32[]{:S(2)}, u32[]{:S(2)}) collective-permute-start(f32[40,8,128]{2,1,0:T(8,128)S(1)} %get-tuple-element.26), channel_id=1, source_target_pairs={{0,1},{1,2},{2,3},{3,0},{4,5},{5,6},{6,7},{7,4},{8,9},{9,10},{10,1... | collective-permute-start | bytes 491528 | tf_op jit(solution)/shard_map/ppermute | solution.py:505
  148.6 0.4 collective-permute-start.9
  149.0 3.0 %collective-permute-done.7.refs_1_ = f32[40,8,128]{2,1,0:T(8,128)S(1)} collective-permute-done((f32[40,8,128]{2,1,0:T(8,128)S(1)}, f32[40,8,128]{2,1,0:T(8,128)S(1)}, u32[]{:S(2)}, u32[]{:S(2)}) %collective-permute-start.7) | collective-permute-done | bytes 163872 | tf_op jit(solution)/shard_map/ppermute | solution.py:505
  152.1 3.5 %collective-permute-done.8.refs_2_ = f32[40,8,128]{2,1,0:T(8,128)S(1)} collective-permute-done((f32[40,8,128]{2,1,0:T(8,128)S(1)}, f32[40,8,128]{2,1,0:T(8,128)S(1)}, u32[]{:S(2)}, u32[]{:S(2)}) %collective-permute-start.8) | collective-permute-done | bytes 163872 | tf_op jit(solution)/shard_map/ppermute | solution.py:505
  155.6 0.3 collective-permute-done.9.refs_3_
  155.9 7.1 %unpack.1 = f32[4,20,8,256]{3,2,1,0:T(8,128)} custom-call(s32[3]{0:T(128)S(1)} %pad_add_fusion.at_ref, f32[40,8,128]{2,1,0:T(8,128)S(1)} %get-tuple-element.25.refs_0_, f32[40,8,128]{2,1,0:T(8,128)S(1)} %collective-permute-done.7.refs_1_, f32[40,8,128]{2,1,0:T(8,128)S(1)} %collective-permute-done.8.refs_2_, f32[40,8,128]{2,1,0:T(8,128)S(1)} %collective-permute-done.9.refs_3_), custom_call_target="tpu_custom_call" | custom-call | tf_op jit(solution)/shard_map/unpack/pallas_call | solution.py:552
  (24 shorter events, 0.1 us)
Async XLA Ops:
  0.7 0.9 copy-start
  1.6 0.9 copy-start.2
  2.6 0.9 copy-start.4
  3.5 0.9 copy-start.6
  4.4 1.1 copy-start.8
  6.9 13.1 %collective-permute-start = (f32[67,8,128]{2,1,0:T(8,128)S(1)}, f32[67,8,128]{2,1,0:T(8,128)S(1)}, u32[]{:S(2)}, u32[]{:S(2)}) collective-permute-start(f32[67,8,128]{2,1,0:T(8,128)S(1)} %get-tuple-element.18), channel_id=1, source_target_pairs={{0,1},{1,2},{2,3},{3,0},{4,5},{5,6},{6,7},{7,4},{8,9},{9,10},{10,1... | collective-permute-start | bytes 823304 | tf_op jit(solution)/shard_map/ppermute | solution.py:505
  9.5 10.4 %collective-permute-start.2 = (f32[67,8,128]{2,1,0:T(8,128)S(1)}, f32[67,8,128]{2,1,0:T(8,128)S(1)}, u32[]{:S(2)}, u32[]{:S(2)}) collective-permute-start(f32[67,8,128]{2,1,0:T(8,128)S(1)} %get-tuple-element.20), channel_id=1, source_target_pairs={{0,3},{1,0},{2,1},{3,2},{4,7},{5,4},{6,5},{7,6},{8,11},{9,8},{10,9... | collective-permute-start | bytes 823304 | tf_op jit(solution)/shard_map/ppermute | solution.py:505
  9.5 10.4 %collective-permute-start.1 = (f32[47,8,128]{2,1,0:T(8,128)S(1)}, f32[47,8,128]{2,1,0:T(8,128)S(1)}, u32[]{:S(2)}, u32[]{:S(2)}) collective-permute-start(f32[47,8,128]{2,1,0:T(8,128)S(1)} %get-tuple-element.19), channel_id=1, source_target_pairs={{0,2},{1,3},{2,0},{3,1},{4,6},{5,7},{6,4},{7,5},{8,10},{9,11},{10,... | collective-permute-start | bytes 577544 | tf_op jit(solution)/shard_map/ppermute | solution.py:505
  19.9 9.9 %copy-start.14 = (f32[13]{0:T(128)S(1)}, f32[13]{0:T(128)}, u32[]{:S(2)}) copy-start(f32[13]{0:T(128)} %param.17) | copy-start | bytes 160
  20.0 23.7 %copy-start.1 = (f32[80,640]{1,0:T(8,128)S(1)}, f32[80,640]{1,0:T(8,128)}, u32[]{:S(2)}) copy-start(f32[80,640]{1,0:T(8,128)} %level_in.1) | copy-start | bytes 614404
  20.0 23.7 %copy-start.3 = (f32[80,640]{1,0:T(8,128)S(1)}, f32[80,640]{1,0:T(8,128)}, u32[]{:S(2)}) copy-start(f32[80,640]{1,0:T(8,128)} %fuel_in.1) | copy-start | bytes 614404
  20.0 23.7 %copy-start.5 = (s32[80,640]{1,0:T(8,128)S(1)}, s32[80,640]{1,0:T(8,128)}, u32[]{:S(2)}) copy-start(s32[80,640]{1,0:T(8,128)} %class_in.1) | copy-start | bytes 614404
  20.0 23.7 %copy-start.7 = (s32[80,640]{1,0:T(8,128)S(1)}, s32[80,640]{1,0:T(8,128)}, u32[]{:S(2)}) copy-start(s32[80,640]{1,0:T(8,128)} %ignite_in.1) | copy-start | bytes 614404
  20.7 22.9 %collective-permute-start.5 = (f32[114,8,128]{2,1,0:T(8,128)S(1)}, f32[114,8,128]{2,1,0:T(8,128)S(1)}, u32[]{:S(2)}, u32[]{:S(2)}) collective-permute-start(f32[114,8,128]{2,1,0:T(8,128)S(1)} %get-tuple-element.23), channel_id=1, source_target_pairs={{0,4},{4,8},{8,12},{1,5},{5,9},{9,13},{2,6},{6,10},{10,14},{3,7},{... | collective-permute-start | bytes 1400840 | tf_op jit(solution)/shard_map/ppermute | solution.py:520
  23.2 20.4 %collective-permute-start.6 = (f32[114,8,128]{2,1,0:T(8,128)S(1)}, f32[114,8,128]{2,1,0:T(8,128)S(1)}, u32[]{:S(2)}, u32[]{:S(2)}) collective-permute-start(f32[114,8,128]{2,1,0:T(8,128)S(1)} %get-tuple-element.24), channel_id=1, source_target_pairs={{4,0},{8,4},{12,8},{5,1},{9,5},{13,9},{6,2},{10,6},{14,10},{7,3},{... | collective-permute-start | bytes 1400840 | tf_op jit(solution)/shard_map/ppermute | solution.py:521
  24.5 15.2 %collective-permute-start.3 = (f32[4,5,40,128]{3,2,1,0:T(8,128)S(1)}, f32[4,5,40,128]{3,2,1,0:T(8,128)S(1)}, u32[]{:S(2)}, u32[]{:S(2)}) collective-permute-start(f32[4,5,40,128]{3,2,1,0:T(8,128)S(1)} %get-tuple-element.21), channel_id=1, source_target_pairs={{0,4},{4,8},{8,12},{1,5},{5,9},{9,13},{2,6},{6,10},{10,14},{3,7},{... | collective-permute-start | bytes 1228808 | tf_op jit(solution)/shard_map/ppermute | solution.py:508
  28.6 15.1 %collective-permute-start.4 = (f32[4,5,40,128]{3,2,1,0:T(8,128)S(1)}, f32[4,5,40,128]{3,2,1,0:T(8,128)S(1)}, u32[]{:S(2)}, u32[]{:S(2)}) collective-permute-start(f32[4,5,40,128]{3,2,1,0:T(8,128)S(1)} %get-tuple-element.22), channel_id=1, source_target_pairs={{4,0},{8,4},{12,8},{5,1},{9,5},{13,9},{6,2},{10,6},{14,10},{7,3},{... | collective-permute-start | bytes 1228808 | tf_op jit(solution)/shard_map/ppermute | solution.py:509
  29.9 0.7 copy-start.11
  29.9 0.7 copy-start.12
  29.9 0.7 copy-start.13
  30.5 13.1 %copy-start.9 = (f32[2,80]{1,0:T(2,128)S(1)}, f32[2,80]{1,0:T(2,128)}, u32[]{:S(2)}) copy-start(f32[2,80]{1,0:T(2,128)} %constant.17.clone.weights_ref) | copy-start | bytes 1924
  30.5 13.1 %copy-start.10 = (s32[4]{0:T(128)S(1)}, s32[4]{0:T(128)}, u32[]{:S(2)}) copy-start(s32[4]{0:T(128)} %plan_ref.1) | copy-start | bytes 52
  143.1 9.0 %collective-permute-start.7 = (f32[40,8,128]{2,1,0:T(8,128)S(1)}, f32[40,8,128]{2,1,0:T(8,128)S(1)}, u32[]{:S(2)}, u32[]{:S(2)}) collective-permute-start(f32[40,8,128]{2,1,0:T(8,128)S(1)} %get-tuple-element.26), channel_id=1, source_target_pairs={{0,1},{1,2},{2,3},{3,0},{4,5},{5,6},{6,7},{7,4},{8,9},{9,10},{10,1... | collective-permute-start | bytes 491528 | tf_op jit(solution)/shard_map/ppermute | solution.py:505
  148.6 7.0 %collective-permute-start.8 = (f32[40,8,128]{2,1,0:T(8,128)S(1)}, f32[40,8,128]{2,1,0:T(8,128)S(1)}, u32[]{:S(2)}, u32[]{:S(2)}) collective-permute-start(f32[40,8,128]{2,1,0:T(8,128)S(1)} %get-tuple-element.27), channel_id=1, source_target_pairs={{0,2},{1,3},{2,0},{3,1},{4,6},{5,7},{6,4},{7,5},{8,10},{9,11},{10,... | collective-permute-start | bytes 491528 | tf_op jit(solution)/shard_map/ppermute | solution.py:505
  148.6 7.2 %collective-permute-start.9 = (f32[40,8,128]{2,1,0:T(8,128)S(1)}, f32[40,8,128]{2,1,0:T(8,128)S(1)}, u32[]{:S(2)}, u32[]{:S(2)}) collective-permute-start(f32[40,8,128]{2,1,0:T(8,128)S(1)} %get-tuple-element.28), channel_id=1, source_target_pairs={{0,3},{1,0},{2,1},{3,2},{4,7},{5,4},{6,5},{7,6},{8,11},{9,8},{10,9... | collective-permute-start | bytes 491528 | tf_op jit(solution)/shard_map/ppermute | solution.py:505

commit v2 on v1

v2 whole, which is shorter than its diff:
```python
import functools
import math

import jax
import jax.numpy as jnp
from jax import lax
from jax.experimental import pallas as pl
from jax.experimental.pallas import tpu as pltpu
from jax.sharding import PartitionSpec as P

LEVELS = 80
REFINE = 10
STEPS = 4
SUBSTEPS = 4
NFUEL = 13

LANES = 128
HALO = STEPS
EDGE = HALO * REFINE
PAD = 8

air_delta = 0.1
diffusion = 0.2
heat_gain = 20.0
vapour_gain = 20.0
lift_gain = 0.3
wind_gain = 0.5
fire_delta = 0.15

BANDS = ("sect", "sub")
UNROLL_LOOKUP = 4
UNROLL_FIRE = 8
UNROLL_AIR = 8
UNROLL_FINAL = 10
RELAY_FLOPS = 5 * 10**9
SURVEY_FLOPS = 10**10
PACK_LIMIT = 62 * 1024 * 1024
VMEM_LIMIT = 40 * 1024 * 1024


def iota(shape, dim):
    return lax.broadcasted_iota(jnp.int32, shape, dim)


def roll(value, shift, axis):
    return pltpu.roll(value, shift, axis)


def unrolled(low, high, step, body, carry):
    def group(i, carry):
        for n in range(step):
            carry = body(low + i * step + n, carry)
        return carry

    whole = (high - low) // step
    carry = lax.fori_loop(0, whole, group, carry)
    for i in range(low + whole * step, high):
        carry = body(i, carry)
    return carry


def level_weight(k, rate, total):
    scale = total / sum(math.exp(-rate * j / LEVELS) for j in range(LEVELS))
    height = jnp.full((8, LANES), k, jnp.int32).astype(jnp.float32)
    return jnp.exp(height * (-rate / LEVELS)) * scale


def band_index():
    return lax.axis_index("sect") * lax.axis_size("sub") + lax.axis_index("sub")


def air_tiles(depth):
    return 2 * depth + -(-depth // 3)


def pack_kernel(bands, *refs):
    sources, outs, scratch, sems = refs[:5], refs[5 : bands + 7], refs[bands + 7 : bands + 12], refs[bands + 12]
    slots, up_ref, down_ref = outs[:bands], outs[bands], outs[bands + 1]
    copies = [pltpu.make_async_copy(a, b, sems.at[n]) for n, (a, b) in enumerate(zip(sources, scratch))]
    for copy in copies:
        copy.start()
    for copy in copies:
        copy.wait()
    air_ref, level_ref, fuel_ref, class_ref, ignite_ref = scratch
    depth = air_ref.shape[1]
    lane_tiles = air_ref.shape[3] // LANES
    rows, width = level_ref.shape
    lane = iota((8, LANES), 1)
    fields = [ref[...] for ref in (level_ref, fuel_ref)]
    fields += [ref[...].astype(jnp.float32) for ref in (class_ref, ignite_ref)]
    for a, field in enumerate(fields):
        for j in range(width // LANES):
            cols = field[:, j * LANES : (j + 1) * LANES]
            up_ref[a, j] = cols[:EDGE]
            down_ref[a, j] = cols[rows - EDGE :]
    base = air_tiles(depth)
    wide = iota((rows, LANES), 1)
    for pair in range(2):
        first, second = fields[2 * pair], fields[2 * pair + 1]
        at = pl.ds(base + pair * (rows // 8), rows // 8)
        to_next = jnp.where(wide < 64, roll(second[:, width - LANES :], 64, 1), first[:, width - LANES :])
        slots[1][at] = to_next.reshape(rows // 8, 8, LANES)
        to_prev = jnp.where(wide < 64, first[:, :LANES], roll(second[:, :LANES], 64, 1))
        slots[bands - 1][at] = to_prev.reshape(rows // 8, 8, LANES)
    band = band_index()
    for k in range(bands):
        dest = lax.rem(band + k, bands)
        odd = lax.rem(dest, 2)
        own = pl.multiple_of((dest // 2) * LANES, LANES)
        high = (dest + 1) // 2
        right = pl.multiple_of(jnp.minimum(high, lane_tiles - 1) * LANES, LANES)
        left = pl.multiple_of(jnp.maximum(high - 1, 0) * LANES, LANES)
        turn = 64 * odd
        back = 64 - turn
        from_right = lane < 96 - turn
        for l in range(depth):
            for p in range(2):
                first = air_ref[2 * p, l, :, pl.ds(own, LANES)]
                second = air_ref[2 * p + 1, l, :, pl.ds(own, LANES)]
                slots[k][2 * l + p] = jnp.where(lane < 64, roll(first, turn, 1), roll(second, back, 1))
        for g in range(-(-depth // 3)):
            packed = jnp.zeros((8, LANES), jnp.float32)
            for l in range(3 * g, min(3 * g + 3, depth)):
                for f in range(4):
                    j = (l - 3 * g) * 4 + f
                    edge = jnp.where(
                        from_right, air_ref[f, l, :, pl.ds(right, LANES)], air_ref[f, l, :, pl.ds(left, LANES)]
                    )
                    edge = roll(edge, 4 * j + back, 1)
                    here = ((lane >= 4 * j) & (lane < 4 * j + 4)) | ((lane >= 60 + 4 * j) & (lane < 64 + 4 * j))
                    packed = jnp.where(here, edge, packed)
            slots[k][2 * depth + g] = packed


def corner_tiles(next_ref, prev_ref, base, rows):
    lane = iota((rows, LANES), 1)
    result = []
    for pair in range(2):
        at = pl.ds(base + pair * (rows // 8), rows // 8)
        left = prev_ref[at].reshape(rows, LANES)
        right = next_ref[at].reshape(rows, LANES)
        result.append(jnp.where(lane < 64, right, left))
        result.append(roll(jnp.where(lane < 64, left, right), 64, 1))
    return result


def relay_kernel(bands, rows, *refs):
    slots, up_ref, down_ref = refs[:bands], refs[bands], refs[bands + 1]
    tiles = slots[0].shape[0]
    sub = iota((8, LANES), 0)
    for half in range(bands // 2):
        one, two = slots[2 * half], slots[2 * half + 1]

        def body(i, carry, one=one, two=two, half=half):
            first, second = one[i], two[i]
            up_ref[half * tiles + i] = jnp.where(sub < 4, first, roll(second, 4, 0))
            down_ref[half * tiles + i] = jnp.where(sub < 4, roll(first, 4, 0), second)
            return carry

        unrolled(0, tiles, 8, body, 0)
    corners = corner_tiles(slots[bands - 1], slots[1], tiles, rows)
    base = (bands // 2) * tiles
    count = EDGE // 8
    for a, corner in enumerate(corners):
        at = pl.ds(base + a * count, count)
        up_ref[at] = corner[:EDGE].reshape(count, 8, LANES)
        down_ref[at] = corner[rows - EDGE :].reshape(count, 8, LANES)


def table_vectors(tables_ref):
    lane = iota((8, LANES), 1)
    vectors = []
    for n in range(4):
        vector = jnp.zeros((8, LANES), jnp.float32)
        for category in range(NFUEL):
            vector = jnp.where(lane == category, tables_ref[n, category], vector)
        vectors.append(vector)
    vectors[1] = -1.0 / jnp.where(lane < NFUEL, vectors[1], 1.0)
    return vectors


def pick(vector, index):
    return jnp.take_along_axis(vector, index, axis=1, mode="promise_in_bounds")


def survey_kernel(tables_ref, class_ref, up_ref, down_ref, *outs):
    vectors = table_vectors(tables_ref)
    rows, width = class_ref.shape
    tiles = width // LANES

    def fill(first, count, read):
        def body(t, carry):
            for j in range(tiles):
                index = read(j, pl.ds(pl.multiple_of(8 * t, 8), 8)).astype(jnp.int32)
                for vector, out in zip(vectors, outs):
                    out[j, pl.ds(pl.multiple_of(first + 8 * t, 8), 8)] = pick(vector, index)
            return carry

        unrolled(0, count // 8, 5, body, 0)

    fill(0, EDGE, lambda j, at: up_ref[2, j, at])
    fill(EDGE, rows, lambda j, at: class_ref[at, j * LANES : (j + 1) * LANES])
    fill(EDGE + rows, EDGE, lambda j, at: down_ref[2, j, at])


def main_kernel(bands, plan_ref, tables_ref, level_in, fuel_in, ignite_in, *refs):
    slots = refs[:bands]
    fire_up, fire_down, edge_up, edge_down = refs[bands : bands + 4]
    values_in = refs[bands + 4 : bands + 8]
    level_out, fuel_out = refs[bands + 8 : bands + 10]
    outs = refs[bands + 10 : 2 * bands + 10]
    scratch = list(refs[2 * bands + 10 :])
    lev_a, lev_b, fuel, ignite = scratch[:4]
    pace, burnt, wind_u, wind_v, energy, vapour, air_a, air_b = scratch[4:12]
    values_side = scratch[12:]
    tile, band, tile_count = lax.axis_index("tile"), band_index(), lax.axis_size("tile")
    rows, width = level_in.shape
    tiles = width // LANES
    depth = LEVELS // bands
    count = air_tiles(depth)
    own = PAD + EDGE
    span = rows + 2 * EDGE
    lane = iota((8, LANES), 1)
    first_tile, final_tile = tile == 0, tile == tile_count - 1
    first_band, final_band = band == 0, band == bands - 1

    def strip(t, base=PAD):
        return pl.ds(pl.multiple_of(base + 8 * t, 8), 8)

    corners = corner_tiles(slots[bands - 1], slots[1], count, rows)
    base = (bands // 2) * count
    sides = []
    for a, (source, held) in enumerate(((level_in, lev_a), (fuel_in, fuel), (None, None), (ignite_in, ignite))):
        at = pl.ds(base + a * (EDGE // 8), EDGE // 8)
        upper, lower = edge_up[at].reshape(EDGE, LANES), edge_down[at].reshape(EDGE, LANES)
        if held is None:
            side = jnp.concatenate([upper, corners[a], lower], axis=0).astype(jnp.int32)
            vectors = table_vectors(tables_ref)
            for n in range(span // 8):
                for vector, out in zip(vectors, values_side):
                    out[8 * n : 8 * n + 8] = pick(vector, side[8 * n : 8 * n + 8])
            continue
        for j in range(tiles):
            held[j, PAD:own] = fire_up[a, j]
            held[j, own : own + rows] = source[:, j * LANES : (j + 1) * LANES].astype(jnp.float32)
            held[j, own + rows : own + rows + EDGE] = fire_down[a, j]
        held[tiles, PAD:own] = upper
        held[tiles, own : own + rows] = corners[a]
        held[tiles, own + rows : own + rows + EDGE] = lower

    def value_at(n, j, t):
        return values_in[n][j, strip(t, 0)] if j < tiles else values_side[n][strip(t, 0)]

    spare = jnp.zeros((tiles + 1, PAD, LANES), jnp.float32)
    for held in (lev_a, lev_b):
        held[:, :PAD] = spare
        held[:, PAD + span :] = spare

    def kindled(values, t, c):
        return [
            jnp.where(ignite[j, strip(t)] <= c, jnp.minimum(value, -1.0), value) for j, value in enumerate(values)
        ]

    mend_low = first_band & (lane == LANES - 1)
    mend_high = final_band & (lane == 0)

    def mend_lanes(values):
        halo = jnp.where(mend_low, roll(values[0], LANES - 1, 1), values[tiles])
        halo = jnp.where(mend_high, roll(values[tiles - 1], 1, 1), halo)
        return values[:tiles] + [halo]

    def mend_rows(held):
        @pl.when(first_tile)
        def _():
            for j in range(tiles + 1):
                held[j, own - 1 : own] = held[j, own : own + 1]

        @pl.when(final_tile)
        def _():
            for j in range(tiles + 1):
                held[j, own + rows : own + rows + 1] = held[j, own + rows - 1 : own + rows]

    def kindle(t, carry):
        values = mend_lanes(kindled([lev_a[j, strip(t)] for j in range(tiles + 1)], t, 0))
        for j, value in enumerate(values):
            lev_a[j, strip(t)] = value
        return carry

    unrolled(0, span // 8, UNROLL_LOOKUP, kindle, 0)
    mend_rows(lev_a)

    sub = iota((8, LANES), 0)
    low_row = jnp.where(final_tile, 0, 4)
    high_row = jnp.where(first_tile, 8, 4)
    low_lane = jnp.where(final_band, 64, 68)
    high_lane = jnp.where(first_band, 128, 124)
    inside_own = (lane < low_lane) | (lane >= high_lane)
    inside = (inside_own, inside_own & ((sub < low_row) | (sub >= high_row)))

    def layer_at(k, part, shift=0):
        return pl.ds(pl.multiple_of((k + 1) * 24 + 8 * part, 8) + shift, 8)

    def put(held, f, k, part, value):
        held[f, layer_at(k, part)] = value
        if part == 2:
            held[f, layer_at(k, 0)] = value

    for k in range(bands):
        source = lax.rem(band - k + bands, bands)
        half = k // 2

        def whole(i, k=k, half=half):
            below, above = edge_down[half * count + i], edge_up[half * count + i]
            if k % 2 == 0:
                halo = jnp.where(sub < 4, below, roll(above, 4, 0))
            else:
                halo = jnp.where(sub < 4, roll(below, 4, 0), above)
            return slots[k][i], halo

        for g in range(-(-depth // 3)):
            edges = whole(2 * depth + g)
            for l in range(3 * g, min(3 * g + 3, depth)):
                for p in range(2):
                    both = whole(2 * l + p)
                    for f in range(2):
                        j = (l - 3 * g) * 4 + 2 * p + f
                        for part in range(2):
                            inner = both[part] if f == 0 else roll(both[part], 64, 1)
                            value = jnp.where(lane < 64, inner, roll(edges[part], 64 - 4 * j, 1))
                            value = jnp.where(inside[part], value, 0.0)
                            put(air_a, 2 * p + f, source * depth + l, part + 1, value)
    nothing = jnp.zeros((8, LANES), jnp.float32)
    for held in (air_a, air_b):
        for f in range(4):
            for part in range(3):
                held[f, layer_at(-1, part)] = nothing
                held[f, layer_at(LEVELS, part)] = nothing

    cell, column = iota((LANES, LANES), 0), iota((LANES, LANES), 1)
    start = jnp.where(
        column < 64 + HALO,
        REFINE * column,
        jnp.where(column >= LANES - HALO, REFINE * column + (tiles + 1) * LANES - REFINE * LANES, -LANES * 1000),
    )
    across = []
    for j in range(tiles + 1):
        place = cell + j * LANES
        across.append(jnp.where((place >= start) & (place < start + REFINE), 1.0, 0.0).astype(jnp.bfloat16))
    outward = [jnp.concatenate([matrix] * 2, axis=1) for matrix in across]
    across = [jnp.concatenate([matrix] * 2, axis=0) for matrix in across]
    cell, column = iota((span, 16), 0), iota((span, 16), 1)
    start = jnp.where(column < 8 + HALO, EDGE + REFINE * column, REFINE * (column - 12))
    along = jnp.where((cell >= start) & (cell < start + REFINE), 1.0, 0.0).astype(jnp.float32)

    def parts(value, axis):
        high = value.astype(jnp.bfloat16)
        low = (value - high.astype(jnp.float32)).astype(jnp.bfloat16)
        return jnp.concatenate([high, low], axis=axis)

    def dot(a, b, dims):
        return lax.dot_general(a, b, (dims, ((), ())), preferred_element_type=jnp.float32)

    def blow(total, k, result):
        weight = level_weight(k, 1.0, 1.0)
        return [a + weight * b for a, b in zip(total, result)]

    def first_wind(k, carry):
        return blow(carry, k, [air_a[f, layer_at(k, part)] for f in (2, 3) for part in (1, 2)])

    calm = [nothing] * 4
    wind = unrolled(0, LEVELS, UNROLL_AIR, first_wind, calm)

    spread = air_delta * diffusion
    mixing = [jnp.where(mask, spread, 0.0) for mask in inside]
    lifting = [jnp.where(mask, 0.5 * lift_gain * air_delta, 0.0) for mask in inside]
    lifting = [(value, 0.6 * value) for value in lifting]
    state, other = air_a, air_b
    for c in range(STEPS):
        reach = EDGE - REFINE * (c + 1)
        fire_step = plan_ref[c].astype(jnp.float32) * fire_delta

        def strips(margin):
            return (EDGE - margin) // 8, -(-(EDGE + rows + margin) // 8)

        low, high = (8 * t for t in strips(reach + SUBSTEPS - 1))
        spread_rows = jnp.concatenate([along[low:high].astype(jnp.bfloat16)] * 2, axis=1)
        coarse = parts(jnp.concatenate(wind, axis=0) * wind_gain, 1)
        for j in range(tiles + 1):
            wide = parts(dot(coarse, outward[j], ((1,), (1,))).reshape(2, 16, LANES), 1)
            wind_u[j, low:high] = dot(spread_rows, wide[0], ((1,), (0,)))
            wind_v[j, low:high] = dot(spread_rows, wide[1], ((1,), (0,)))

        before, after = lev_a, lev_b
        for s in range(SUBSTEPS):

            def advance(t, carry, c=c, s=s, fire_step=fire_step, before=before, after=after):
                row = pl.multiple_of(PAD + 8 * t, 8)
                at, flat = strip(t), strip(t, 0)
                centre = [before[j, at] for j in range(tiles + 1)]
                lower = [roll(value, 1, 1) for value in centre]
                upper = [roll(value, LANES - 1, 1) for value in centre]
                result = []
                for j in range(tiles + 1):
                    west = before[j, pl.ds(row - 1, 8)]
                    east = before[j, pl.ds(row + 1, 8)]
                    south = jnp.where(lane == 0, lower[j - 1], lower[j])
                    north = jnp.where(lane == LANES - 1, upper[(j + 1) % (tiles + 1)], upper[j])
                    here = centre[j]
                    back, ahead = here - west, east - here
                    below, above = here - south, north - here
                    a, b = jnp.maximum(back, 0.0), jnp.minimum(ahead, 0.0)
                    d, e = jnp.maximum(below, 0.0), jnp.minimum(above, 0.0)
                    square = (a * a + b * b) + (d * d + e * e)
                    steep = square * lax.rsqrt(jnp.maximum(square, 1.2e-38))
                    gx, gy = back + ahead, below + above
                    tail = (wind_u[j, flat] * gx + wind_v[j, flat] * gy) * lax.rsqrt((gx * gx + 4.0) + gy * gy)
                    if s == 0:
                        speed = fire_step * value_at(0, j, t)
                        pace[j, flat] = speed
                    else:
                        speed = pace[j, flat]
                    result.append(here - (speed * (1.0 + jnp.maximum(tail, 0.0))) * steep)
                for j in range(tiles + 1):
                    unburnt = jnp.clip(result[j], -0.5, 0.5)
                    if s > 0:
                        unburnt = unburnt + burnt[j, flat]
                    if s < SUBSTEPS - 1:
                        burnt[j, flat] = unburnt
                    else:
                        held = fuel[j, at]
                        remain = held * jnp.exp((0.5 * SUBSTEPS - unburnt) * (fire_step * value_at(1, j, t)))
                        spent = held - remain
                        fuel[j, at] = remain
                        energy[j, flat] = spent * value_at(2, j, t)
                        vapour[j, flat] = spent * value_at(3, j, t)
                if s == SUBSTEPS - 1 and c < STEPS - 1:
                    result = kindled(result, t, c + 1)
                for j, value in enumerate(mend_lanes(result)):
                    after[j, at] = value
                return carry

            unrolled(*strips(reach + SUBSTEPS - 1 - s), UNROLL_FIRE, advance, 0)
            mend_rows(after)
            before, after = after, before

        low, high = (8 * t for t in strips(reach))
        gather_rows = along[low:high].astype(jnp.bfloat16)
        forcing = []
        for held, gain in ((energy, heat_gain), (vapour, vapour_gain)):
            total = dot(parts(held[0, low:high], 1), across[0], ((1,), (0,)))
            for j in range(1, tiles + 1):
                total = total + dot(parts(held[j, low:high], 1), across[j], ((1,), (0,)))
            both = dot(gather_rows, parts(total, 1), ((0,), (0,)))
            flux = (both[:, :LANES] + both[:, LANES:]) * (air_delta * gain / (REFINE * REFINE))
            forcing.append([jnp.where(inside[part], flux[8 * part : 8 * part + 8], 0.0) for part in range(2)])

        def air_step(k, part, state=state, forcing=forcing):
            at = layer_at(k, part + 1)
            here = [state[f, at] for f in range(4)]
            west = [state[f, layer_at(k, part + 1, -1)] for f in range(4)]
            east = [state[f, layer_at(k, 1 if part == 0 else 0, 1)] for f in range(4)]
            south = [roll(value, 1, 1) for value in here]
            north = [roll(value, LANES - 1, 1) for value in here]
            u, v = air_delta * here[2], air_delta * here[3]
            mix = mixing[part]
            to_west, to_east = mix + jnp.maximum(u, 0.0), mix - jnp.minimum(u, 0.0)
            to_south, to_north = mix + jnp.maximum(v, 0.0), mix - jnp.minimum(v, 0.0)
            keep = (1.0 - 6.0 * spread) - (jnp.abs(u) + jnp.abs(v))
            height = level_weight(k, 2.0, float(LEVELS))
            result = []
            for f in range(4):
                new = keep * here[f] + mix * (state[f, layer_at(k - 1, part + 1)] + state[f, layer_at(k + 1, part + 1)])
                new = new + (to_west * west[f] + to_east * east[f]) + (to_south * south[f] + to_north * north[f])
                if f < 2:
                    new = new + height * forcing[f][part]
                else:
                    low, high = (west, east) if f == 2 else (south, north)
                    new = new + (lifting[part][0] * (high[0] - low[0]) + lifting[part][1] * (high[1] - low[1]))
                result.append(new)
            return result

        if c < STEPS - 1:

            def layer(k, carry, other=other, air_step=air_step):
                result = [air_step(k, part) for part in range(2)]
                for part in range(2):
                    for f in range(4):
                        put(other, f, k, part + 1, result[part][f])
                return blow(carry, k, [result[part][f] for f in (2, 3) for part in range(2)])

            wind = unrolled(0, LEVELS, UNROLL_AIR, layer, calm)
            state, other = other, state
        else:
            for k in range(bands):
                first = lax.rem(band + k, bands) * depth

                def final(l, carry, out=outs[k], first=first, air_step=air_step):
                    result = air_step(first + l, 0)
                    for p in range(2):
                        out[2 * l + p] = jnp.where(lane < 64, result[2 * p], roll(result[2 * p + 1], 64, 1))
                    return carry

                unrolled(0, depth, UNROLL_FINAL, final, 0)

    for j in range(tiles):
        level_out[:, j * LANES : (j + 1) * LANES] = lev_a[j, own : own + rows]
        fuel_out[:, j * LANES : (j + 1) * LANES] = fuel[j, own : own + rows]


def unpack_kernel(bands, *refs):
    slots, out = refs[:bands], refs[bands]
    depth = out.shape[1]
    lane = iota((8, LANES), 1)
    for k in range(bands):
        source = lax.rem(band_index() - k + bands, bands)
        odd = lax.rem(source, 2)
        cols = pl.ds(pl.multiple_of((source // 2) * LANES, LANES), LANES)
        mine = (lane >= 64 * odd) & (lane < 64 * odd + 64)

        def body(l, carry, slot=slots[k], odd=odd, cols=cols, mine=mine):
            for p in range(2):
                both = slot[2 * l + p]
                for f in range(2):
                    shift = 64 * odd if f == 0 else 64 - 64 * odd
                    old = out[2 * p + f, l, :, cols]
                    out[2 * p + f, l, :, cols] = jnp.where(mine, roll(both, shift, 1), old)
            return carry

        unrolled(0, depth, 10, body, 0)


def shape(*dims):
    return jax.ShapeDtypeStruct(dims, jnp.float32)


def vmem():
    return pl.BlockSpec(memory_space=pltpu.VMEM)


def smem():
    return pl.BlockSpec(memory_space=pltpu.SMEM)


def local(
    air_state,
    fire_level,
    fuel_left,
    fuel_class,
    ignition,
    plan,
    spread_rate,
    burn_time,
    heat_content,
    moisture_content,
):
    tables = jnp.stack([spread_rate, burn_time, heat_content, moisture_content])
    bands = lax.axis_size(BANDS)
    tile_count = lax.axis_size("tile")
    depth = air_state.shape[1]
    rows, width = fire_level.shape
    tiles = width // LANES
    count = air_tiles(depth)
    extra = 2 * (rows // 8)
    params = pltpu.CompilerParams(vmem_limit_bytes=VMEM_LIMIT)

    sizes = [count + (extra if k in (1, bands - 1) else 0) for k in range(bands)]
    packed = pl.pallas_call(
        functools.partial(pack_kernel, bands),
        out_shape=[shape(size, 8, LANES) for size in sizes] + [shape(4, tiles, EDGE, LANES)] * 2,
        in_specs=[pl.BlockSpec(memory_space=pltpu.HBM)] * 5,
        out_specs=[vmem()] * (bands + 2),
        scratch_shapes=[
            pltpu.VMEM(x.shape, x.dtype) for x in (air_state, fire_level, fuel_left, fuel_class, ignition)
        ]
        + [pltpu.SemaphoreType.DMA((5,))],
        compiler_params=pltpu.CompilerParams(vmem_limit_bytes=PACK_LIMIT),
        name="pack",
    )(air_state, fire_level, fuel_left, fuel_class, ignition)
    slots, up, down = packed[:bands], packed[bands], packed[bands + 1]

    rise = [(i, i + 1) for i in range(tile_count - 1)]
    sink = [(j, i) for i, j in rise]

    def turn(values):
        moved = [values[0]]
        for k in range(1, bands):
            moved.append(lax.ppermute(values[k], BANDS, [(i, (i + k) % bands) for i in range(bands)]))
        return moved

    fire_up = lax.ppermute(down, "tile", rise)
    fire_down = lax.ppermute(up, "tile", sink)
    slots = turn(slots)
    edges = (bands // 2) * count + 4 * (EDGE // 8)
    up, down = pl.pallas_call(
        functools.partial(relay_kernel, bands, rows),
        out_shape=[shape(edges, 8, LANES)] * 2,
        in_specs=[vmem()] * bands,
        out_specs=[vmem()] * 2,
        compiler_params=params,
        cost_estimate=pl.CostEstimate(flops=RELAY_FLOPS, bytes_accessed=0, transcendentals=0),
        name="relay",
    )(*slots)
    edge_up = lax.ppermute(down, "tile", rise)
    edge_down = lax.ppermute(up, "tile", sink)

    span = rows + 2 * EDGE
    values = pl.pallas_call(
        survey_kernel,
        out_shape=[shape(tiles, span, LANES)] * 4,
        in_specs=[smem()] + [vmem()] * 3,
        out_specs=[vmem()] * 4,
        compiler_params=params,
        cost_estimate=pl.CostEstimate(flops=SURVEY_FLOPS, bytes_accessed=0, transcendentals=0),
        name="survey",
    )(tables, fuel_class, fire_up, fire_down)
    fire = pltpu.VMEM((tiles + 1, span + 2 * PAD, LANES), jnp.float32)
    flat = pltpu.VMEM((tiles + 1, span, LANES), jnp.float32)
    side = pltpu.VMEM((span, LANES), jnp.float32)
    atmosphere = pltpu.VMEM((4, (LEVELS + 2) * 24, LANES), jnp.float32)
    results = pl.pallas_call(
        functools.partial(main_kernel, bands),
        out_shape=[shape(rows, width)] * 2 + [shape(2 * depth, 8, LANES)] * bands,
        in_specs=[smem()] * 2 + [vmem()] * (3 + bands + 8),
        out_specs=[vmem()] * (2 + bands),
        scratch_shapes=[fire] * 4 + [flat] * 6 + [atmosphere] * 2 + [side] * 4,
        compiler_params=params,
        name="window",
    )(
        plan,
        tables,
        fire_level,
        fuel_left,
        ignition,
        *slots,
        fire_up,
        fire_down,
        edge_up,
        edge_down,
        *values,
    )
    level_out, fuel_out = results[:2]
    slabs = turn(results[2:])
    air_out = pl.pallas_call(
        functools.partial(unpack_kernel, bands),
        out_shape=shape(*air_state.shape),
        in_specs=[vmem()] * bands,
        out_specs=vmem(),
        compiler_params=params,
        name="unpack",
    )(*slabs)
    return (air_out, level_out, fuel_out)


def solution(mesh):
    placed = (
        P(None, ("sect", "sub"), ("group", "tile"), None),
        P(("group", "tile"), ("sect", "sub")),
        P(("group", "tile"), ("sect", "sub")),
        P(("group", "tile"), ("sect", "sub")),
        P(("group", "tile"), ("sect", "sub")),
        P(),
        P(),
        P(),
        P(),
        P(),
    )
    return jax.shard_map(
        local,
        mesh=mesh,
        in_specs=placed,
        out_specs=(
            P(None, ("sect", "sub"), ("group", "tile"), None),
            P(("group", "tile"), ("sect", "sub")),
            P(("group", "tile"), ("sect", "sub")),
        ),
        check_vma=False,
    )
```

time: 164 us -> 76.3 us (0.47)
  Pallas kernels: 109 us -> 34.3 us
  waiting for transfers between devices: 30.1 us -> 21 us
  local copies, waits for them, and re-layouts: 5.5 us -> 2.26 us
    pallas_call x1, Pallas kernels: 99.5 us -> 27.7 us  [local(): pl.pallas_call(functools.partial(main_kernel, bands), out_shape=[shape(ro...]
    ppermute x1, waiting for transfers between devices: 9.19 us -> 0.01 us  [local(): fire_up = lax.ppermute(down, 'tile', rise)]
    pallas_call x1, Pallas kernels: 7.08 us -> 1.72 us  [local(): pl.pallas_call(functools.partial(unpack_kernel, bands), out_shape=shape(*...]
    ppermute x6, waiting for transfers between devices: 17.1 us -> 12.2 us  [turn(): lax.ppermute(values[k], BANDS, [(i, (i + k) % bands) for i in range(bands)])]
    ppermute x1, waiting for transfers between devices: 0.01 us -> 4.85 us  [local(): edge_up = lax.ppermute(down, 'tile', rise)]
    ppermute x1, waiting for transfers between devices: 0.01 us -> 4.03 us  [local(): edge_down = lax.ppermute(up, 'tile', sink)]
    ppermute x1, waiting for transfers between devices: 3.86 us -> 0.01 us  [local(): fire_down = lax.ppermute(up, 'tile', sink)]
    unnamed x30 -> x20, local copies, waits for them, and re-layouts: 5.5 us -> 2.26 us
  transfers between devices with their start and end apart: 10 -> 10, of which waited for: 6 -> 6; matrix products, arithmetic and copies ran while one was open for 0% -> 0% of each run, Pallas kernels for 0% -> 2%
where the time goes in v2:
time: 76.3 us; the launch traced here: 75.5 us
  Pallas kernels  34.3 us (45%)
  waiting for transfers between devices  21 us (28%)
  starting transfers between devices  17.1 us (22%)
  local copies, waits for them, and re-layouts  2.26 us (3%)
  between operations  0.78 us (1%)
    pallas_call x1, Pallas kernels, local(): pl.pallas_call(functools.partial(main_kernel, bands), out_shape=[shape(ro...  27.7 us
    ppermute x6, waiting for transfers between devices, turn(): lax.ppermute(values[k], BANDS, [(i, (i + k) % bands) for i in range(bands)])  12.2 us
    ppermute x6, starting transfers between devices, turn(): lax.ppermute(values[k], BANDS, [(i, (i + k) % bands) for i in range(bands)])  8.52 us
    ppermute x1, waiting for transfers between devices, local(): edge_up = lax.ppermute(down, 'tile', rise)  4.85 us
    ppermute x1, waiting for transfers between devices, local(): edge_down = lax.ppermute(up, 'tile', sink)  4.03 us
    ppermute x1, starting transfers between devices, local(): fire_up = lax.ppermute(down, 'tile', rise)  3.32 us
    pallas_call x1, Pallas kernels, local(): pl.pallas_call(functools.partial(pack_kernel, bands), out_shape=[shape(si...  3.26 us
    ppermute x1, starting transfers between devices, local(): edge_up = lax.ppermute(down, 'tile', rise)  2.51 us
  transfers between devices with their start and end apart: 10, of which 6 were waited for; matrix products, arithmetic and copies ran while one was open for 0% of the time, Pallas kernels for 2%

profile of v2, /device:TPU:1, one launch (start us, length us, event | category | flops | bytes accessed | tf_op | source)
XLA Modules:
  0.0 75.5 jit_solution(10834357136347323338)
XLA Ops:
  0.6 3.3 %pack.1 = (f32[47,8,128]{2,1,0:T(8,128)}, f32[67,8,128]{2,1,0:T(8,128)}, f32[47,8,128]{2,1,0:T(8,128)}, f32[67,8,128]{2,1,0:T(8,128)}, f32[4,5,40,128]{3,2,1,0:T(8,128)}, /*index=5*/f32[4,5,40,128]{3,2,1,0:T(8,128)}) custom-call(f32[4,20,8,256]{3,2,1,0:T(8,128)} %refs_0_.1, f32[80,640]{1,0:T(8,128)} %level_in.1, f32[80,640]{1,0:T(8,128)} %fuel_in.1, ...), custom_call_target="tpu_custom_call" | custom-call | tf_op jit(solution)/shard_map/pack/pallas_call | solution.py:567
  3.9 0.0 copy-start.9
  3.9 2.7 %collective-permute-start = (f32[67,8,128]{2,1,0:T(8,128)}, f32[67,8,128]{2,1,0:T(8,128)S(1)}, u32[]{:S(2)}, u32[]{:S(2)}) collective-permute-start(f32[67,8,128]{2,1,0:T(8,128)} %get-tuple-element.22), channel_id=1, source_target_pairs={{0,1},{1,2},{2,3},{3,0},{4,5},{5,6},{6,7},{7,4},{8,9},{9,10},{10,1... | collective-permute-start | bytes 823304 | tf_op jit(solution)/shard_map/ppermute | solution.py:587
  6.6 0.0 collective-permute-start.2
  6.6 0.2 collective-permute-start.1
  6.7 3.3 %collective-permute-start.3 = (f32[4,5,40,128]{3,2,1,0:T(8,128)}, f32[4,5,40,128]{3,2,1,0:T(8,128)S(1)}, u32[]{:S(2)}, u32[]{:S(2)}) collective-permute-start(f32[4,5,40,128]{3,2,1,0:T(8,128)} %get-tuple-element.25), channel_id=1, source_target_pairs={{0,4},{4,8},{8,12},{1,5},{5,9},{9,13},{2,6},{6,10},{10,14},{3,7},{... | collective-permute-start | bytes 1228808 | tf_op jit(solution)/shard_map/ppermute | solution.py:590
  10.1 1.3 %collective-permute-start.4 = (f32[4,5,40,128]{3,2,1,0:T(8,128)}, f32[4,5,40,128]{3,2,1,0:T(8,128)S(1)}, u32[]{:S(2)}, u32[]{:S(2)}) collective-permute-start(f32[4,5,40,128]{3,2,1,0:T(8,128)} %get-tuple-element.26), channel_id=1, source_target_pairs={{4,0},{8,4},{12,8},{5,1},{9,5},{13,9},{6,2},{10,6},{14,10},{7,3},{... | collective-permute-start | bytes 1228808 | tf_op jit(solution)/shard_map/ppermute | solution.py:591
  11.4 0.0 copy-start.6
  11.4 0.0 copy-start.7
  11.4 0.0 copy-start.8
  11.4 0.6 copy-done.6
  12.0 0.0 copy-done.7
  12.0 0.0 copy-done.8
  12.1 5.2 %collective-permute-done.1.refs_2_ = f32[47,8,128]{2,1,0:T(8,128)S(1)} collective-permute-done((f32[47,8,128]{2,1,0:T(8,128)}, f32[47,8,128]{2,1,0:T(8,128)S(1)}, u32[]{:S(2)}, u32[]{:S(2)}) %collective-permute-start.1) | collective-permute-done | bytes 192544 | tf_op jit(solution)/shard_map/ppermute | solution.py:587
  17.3 0.9 %copy-done.4 = f32[47,8,128]{2,1,0:T(8,128)S(1)} copy-done((f32[47,8,128]{2,1,0:T(8,128)S(1)}, f32[47,8,128]{2,1,0:T(8,128)}, u32[]{:S(2)}) %copy-start.4) | copy-done | bytes 192536
  18.2 0.2 relay.1
  18.4 2.5 %collective-permute-start.5 = (f32[114,8,128]{2,1,0:T(8,128)S(1)}, f32[114,8,128]{2,1,0:T(8,128)S(1)}, u32[]{:S(2)}, u32[]{:S(2)}) collective-permute-start(f32[114,8,128]{2,1,0:T(8,128)S(1)} %get-tuple-element.27), channel_id=1, source_target_pairs={{0,4},{4,8},{8,12},{1,5},{5,9},{9,13},{2,6},{6,10},{10,14},{3,7},{... | collective-permute-start | bytes 1400840 | tf_op jit(solution)/shard_map/ppermute | solution.py:603
  20.9 0.0 copy-start
  20.9 0.0 copy-start.1
  21.0 0.0 copy-start.2
  21.0 1.4 %collective-permute-start.6 = (f32[114,8,128]{2,1,0:T(8,128)S(1)}, f32[114,8,128]{2,1,0:T(8,128)S(1)}, u32[]{:S(2)}, u32[]{:S(2)}) collective-permute-start(f32[114,8,128]{2,1,0:T(8,128)S(1)} %get-tuple-element.28), channel_id=1, source_target_pairs={{4,0},{8,4},{12,8},{5,1},{9,5},{13,9},{6,2},{10,6},{14,10},{7,3},{... | collective-permute-start | bytes 1400840 | tf_op jit(solution)/shard_map/ppermute | solution.py:604
  22.4 1.5 %survey.1 = (f32[5,160,128]{2,1,0:T(8,128)S(1)}, f32[5,160,128]{2,1,0:T(8,128)S(1)}, f32[5,160,128]{2,1,0:T(8,128)S(1)}, f32[5,160,128]{2,1,0:T(8,128)S(1)}) custom-call(f32[4,13]{1,0:T(4,128)S(1)} %pad_maximum_fusion.tables_ref, s32[80,640]{1,0:T(8,128)S(1)} %copy-done.3, f32[4,5,40,128]{3,2,1,0:T(8,128)S(1)} %collective-permute-done.3.up_ref.refs_4_, ...), custom_call_target="tpu_custom_call" | custom-call | flops 10000000000 | tf_op jit(solution)/shard_map/survey/pallas_call | solution.py:607
  23.9 4.8 %collective-permute-done.5.refs_6_ = f32[114,8,128]{2,1,0:T(8,128)S(1)} collective-permute-done((f32[114,8,128]{2,1,0:T(8,128)S(1)}, f32[114,8,128]{2,1,0:T(8,128)S(1)}, u32[]{:S(2)}, u32[]{:S(2)}) %collective-permute-start.5) | collective-permute-done | bytes 466976 | tf_op jit(solution)/shard_map/ppermute | solution.py:603
  28.8 4.0 %collective-permute-done.6.refs_7_ = f32[114,8,128]{2,1,0:T(8,128)S(1)} collective-permute-done((f32[114,8,128]{2,1,0:T(8,128)S(1)}, f32[114,8,128]{2,1,0:T(8,128)S(1)}, u32[]{:S(2)}, u32[]{:S(2)}) %collective-permute-start.6) | collective-permute-done | bytes 466976 | tf_op jit(solution)/shard_map/ppermute | solution.py:604
  32.8 0.6 copy-done.5
  33.5 27.7 %window.1 = (f32[80,640]{1,0:T(8,128)}, f32[80,640]{1,0:T(8,128)}, f32[40,8,128]{2,1,0:T(8,128)S(1)}, f32[40,8,128]{2,1,0:T(8,128)S(1)}, f32[40,8,128]{2,1,0:T(8,128)S(1)}, /*index=5*/f32[40,8,128]{2,1,0:T(8,128)S(1)}) custom-call(s32[4]{0:T(128)S(1)} %copy-done.5, f32[4,13]{1,0:T(4,128)S(1)} %pad_maximum_fusion.tables_ref, f32[80,640]{1,0:T(8,128)S(1)} %copy-done, ...), custom_call_target="tpu_custom_call" | custom-call | tf_op jit(solution)/shard_map/window/pallas_call | solution.py:620
  61.2 5.3 %collective-permute-start.7 = (f32[40,8,128]{2,1,0:T(8,128)S(1)}, f32[40,8,128]{2,1,0:T(8,128)S(1)}, u32[]{:S(2)}, u32[]{:S(2)}) collective-permute-start(f32[40,8,128]{2,1,0:T(8,128)S(1)} %get-tuple-element.34), channel_id=1, source_target_pairs={{0,1},{1,2},{2,3},{3,0},{4,5},{5,6},{6,7},{7,4},{8,9},{9,10},{10,1... | collective-permute-start | bytes 491528 | tf_op jit(solution)/shard_map/ppermute | solution.py:587
  66.4 0.4 collective-permute-start.9
  66.8 3.0 %collective-permute-done.7.refs_1_ = f32[40,8,128]{2,1,0:T(8,128)S(1)} collective-permute-done((f32[40,8,128]{2,1,0:T(8,128)S(1)}, f32[40,8,128]{2,1,0:T(8,128)S(1)}, u32[]{:S(2)}, u32[]{:S(2)}) %collective-permute-start.7) | collective-permute-done | bytes 163872 | tf_op jit(solution)/shard_map/ppermute | solution.py:587
  69.9 3.5 %collective-permute-done.8.refs_2_ = f32[40,8,128]{2,1,0:T(8,128)S(1)} collective-permute-done((f32[40,8,128]{2,1,0:T(8,128)S(1)}, f32[40,8,128]{2,1,0:T(8,128)S(1)}, u32[]{:S(2)}, u32[]{:S(2)}) %collective-permute-start.8) | collective-permute-done | bytes 163872 | tf_op jit(solution)/shard_map/ppermute | solution.py:587
  73.4 0.4 collective-permute-done.9.refs_3_
  73.8 1.7 %unpack.1 = f32[4,20,8,256]{3,2,1,0:T(8,128)} custom-call(f32[40,8,128]{2,1,0:T(8,128)S(1)} %get-tuple-element.33.refs_0_, f32[40,8,128]{2,1,0:T(8,128)S(1)} %collective-permute-done.7.refs_1_, f32[40,8,128]{2,1,0:T(8,128)S(1)} %collective-permute-done.8.refs_2_, f32[40,8,128]{2,1,0:T(8,128)S(1)} %collective-permute-done.9.refs_3_), custom_call_target="tpu_custom_call" | custom-call | tf_op jit(solution)/shard_map/unpack/pallas_call | solution.py:643
  (14 shorter events, 0.0 us)
Async XLA Ops:
  3.9 7.5 %copy-start.9 = (f32[13]{0:T(128)S(1)}, f32[13]{0:T(128)}, u32[]{:S(2)}) copy-start(f32[13]{0:T(128)} %param.16) | copy-start | bytes 160
  3.9 13.4 %collective-permute-start = (f32[67,8,128]{2,1,0:T(8,128)}, f32[67,8,128]{2,1,0:T(8,128)S(1)}, u32[]{:S(2)}, u32[]{:S(2)}) collective-permute-start(f32[67,8,128]{2,1,0:T(8,128)} %get-tuple-element.22), channel_id=1, source_target_pairs={{0,1},{1,2},{2,3},{3,0},{4,5},{5,6},{6,7},{7,4},{8,9},{9,10},{10,1... | collective-permute-start | bytes 823304 | tf_op jit(solution)/shard_map/ppermute | solution.py:587
  6.6 10.8 %collective-permute-start.2 = (f32[67,8,128]{2,1,0:T(8,128)}, f32[67,8,128]{2,1,0:T(8,128)S(1)}, u32[]{:S(2)}, u32[]{:S(2)}) collective-permute-start(f32[67,8,128]{2,1,0:T(8,128)} %get-tuple-element.24), channel_id=1, source_target_pairs={{0,3},{1,0},{2,1},{3,2},{4,7},{5,4},{6,5},{7,6},{8,11},{9,8},{10,9... | collective-permute-start | bytes 823304 | tf_op jit(solution)/shard_map/ppermute | solution.py:587
  6.6 10.7 %collective-permute-start.1 = (f32[47,8,128]{2,1,0:T(8,128)}, f32[47,8,128]{2,1,0:T(8,128)S(1)}, u32[]{:S(2)}, u32[]{:S(2)}) collective-permute-start(f32[47,8,128]{2,1,0:T(8,128)} %get-tuple-element.23), channel_id=1, source_target_pairs={{0,2},{1,3},{2,0},{3,1},{4,6},{5,7},{6,4},{7,5},{8,10},{9,11},{10,... | collective-permute-start | bytes 577544 | tf_op jit(solution)/shard_map/ppermute | solution.py:587
  6.7 15.7 %collective-permute-start.3 = (f32[4,5,40,128]{3,2,1,0:T(8,128)}, f32[4,5,40,128]{3,2,1,0:T(8,128)S(1)}, u32[]{:S(2)}, u32[]{:S(2)}) collective-permute-start(f32[4,5,40,128]{3,2,1,0:T(8,128)} %get-tuple-element.25), channel_id=1, source_target_pairs={{0,4},{4,8},{8,12},{1,5},{5,9},{9,13},{2,6},{6,10},{10,14},{3,7},{... | collective-permute-start | bytes 1228808 | tf_op jit(solution)/shard_map/ppermute | solution.py:590
  10.1 12.4 %collective-permute-start.4 = (f32[4,5,40,128]{3,2,1,0:T(8,128)}, f32[4,5,40,128]{3,2,1,0:T(8,128)S(1)}, u32[]{:S(2)}, u32[]{:S(2)}) collective-permute-start(f32[4,5,40,128]{3,2,1,0:T(8,128)} %get-tuple-element.26), channel_id=1, source_target_pairs={{4,0},{8,4},{12,8},{5,1},{9,5},{13,9},{6,2},{10,6},{14,10},{7,3},{... | collective-permute-start | bytes 1228808 | tf_op jit(solution)/shard_map/ppermute | solution.py:591
  11.4 0.7 copy-start.6
  11.4 0.7 copy-start.7
  11.4 0.7 copy-start.8
  17.3 0.9 %copy-start.4 = (f32[47,8,128]{2,1,0:T(8,128)S(1)}, f32[47,8,128]{2,1,0:T(8,128)}, u32[]{:S(2)}) copy-start(f32[47,8,128]{2,1,0:T(8,128)} %get-tuple-element.21.refs_0_) | copy-start | bytes 577540
  18.2 4.2 %copy-start.3 = (s32[80,640]{1,0:T(8,128)S(1)}, s32[80,640]{1,0:T(8,128)}, u32[]{:S(2)}) copy-start(s32[80,640]{1,0:T(8,128)} %class_ref.1) | copy-start | bytes 614404
  18.4 10.4 %collective-permute-start.5 = (f32[114,8,128]{2,1,0:T(8,128)S(1)}, f32[114,8,128]{2,1,0:T(8,128)S(1)}, u32[]{:S(2)}, u32[]{:S(2)}) collective-permute-start(f32[114,8,128]{2,1,0:T(8,128)S(1)} %get-tuple-element.27), channel_id=1, source_target_pairs={{0,4},{4,8},{8,12},{1,5},{5,9},{9,13},{2,6},{6,10},{10,14},{3,7},{... | collective-permute-start | bytes 1400840 | tf_op jit(solution)/shard_map/ppermute | solution.py:603
  20.9 11.9 %copy-start = (f32[80,640]{1,0:T(8,128)S(1)}, f32[80,640]{1,0:T(8,128)}, u32[]{:S(2)}) copy-start(f32[80,640]{1,0:T(8,128)} %level_in.1) | copy-start | bytes 614404
  20.9 11.9 %copy-start.1 = (f32[80,640]{1,0:T(8,128)S(1)}, f32[80,640]{1,0:T(8,128)}, u32[]{:S(2)}) copy-start(f32[80,640]{1,0:T(8,128)} %fuel_in.1) | copy-start | bytes 614404
  21.0 11.9 %copy-start.2 = (s32[80,640]{1,0:T(8,128)S(1)}, s32[80,640]{1,0:T(8,128)}, u32[]{:S(2)}) copy-start(s32[80,640]{1,0:T(8,128)} %ignite_in.1) | copy-start | bytes 614404
  21.0 11.8 %collective-permute-start.6 = (f32[114,8,128]{2,1,0:T(8,128)S(1)}, f32[114,8,128]{2,1,0:T(8,128)S(1)}, u32[]{:S(2)}, u32[]{:S(2)}) collective-permute-start(f32[114,8,128]{2,1,0:T(8,128)S(1)} %get-tuple-element.28), channel_id=1, source_target_pairs={{4,0},{8,4},{12,8},{5,1},{9,5},{13,9},{6,2},{10,6},{14,10},{7,3},{... | collective-permute-start | bytes 1400840 | tf_op jit(solution)/shard_map/ppermute | solution.py:604
  32.8 0.7 copy-start.5
  61.2 8.7 %collective-permute-start.7 = (f32[40,8,128]{2,1,0:T(8,128)S(1)}, f32[40,8,128]{2,1,0:T(8,128)S(1)}, u32[]{:S(2)}, u32[]{:S(2)}) collective-permute-start(f32[40,8,128]{2,1,0:T(8,128)S(1)} %get-tuple-element.34), channel_id=1, source_target_pairs={{0,1},{1,2},{2,3},{3,0},{4,5},{5,6},{6,7},{7,4},{8,9},{9,10},{10,1... | collective-permute-start | bytes 491528 | tf_op jit(solution)/shard_map/ppermute | solution.py:587
  66.4 7.0 %collective-permute-start.8 = (f32[40,8,128]{2,1,0:T(8,128)S(1)}, f32[40,8,128]{2,1,0:T(8,128)S(1)}, u32[]{:S(2)}, u32[]{:S(2)}) collective-permute-start(f32[40,8,128]{2,1,0:T(8,128)S(1)} %get-tuple-element.35), channel_id=1, source_target_pairs={{0,2},{1,3},{2,0},{3,1},{4,6},{5,7},{6,4},{7,5},{8,10},{9,11},{10,... | collective-permute-start | bytes 491528 | tf_op jit(solution)/shard_map/ppermute | solution.py:587
  66.4 7.3 %collective-permute-start.9 = (f32[40,8,128]{2,1,0:T(8,128)S(1)}, f32[40,8,128]{2,1,0:T(8,128)S(1)}, u32[]{:S(2)}, u32[]{:S(2)}) collective-permute-start(f32[40,8,128]{2,1,0:T(8,128)S(1)} %get-tuple-element.36), channel_id=1, source_target_pairs={{0,3},{1,0},{2,1},{3,2},{4,7},{5,4},{6,5},{7,6},{8,11},{9,8},{10,9... | collective-permute-start | bytes 491528 | tf_op jit(solution)/shard_map/ppermute | solution.py:587

commit v3 on v2

--- a/solution.py
+++ b/solution.py
@@ -29,9 +29,10 @@
 
 BANDS = ("sect", "sub")
 UNROLL_LOOKUP = 4
-UNROLL_FIRE = 8
-UNROLL_AIR = 8
+UNROLL_FIRE = 10
+UNROLL_AIR = 16
 UNROLL_FINAL = 10
+KEEP_FLOPS = 10**9
 RELAY_FLOPS = 5 * 10**9
 SURVEY_FLOPS = 10**10
 PACK_LIMIT = 62 * 1024 * 1024
@@ -52,6 +53,8 @@
             carry = body(low + i * step + n, carry)
         return carry
 
+    groups = -(-(high - low) // step)
+    step = -(-(high - low) // groups)
     whole = (high - low) // step
     carry = lax.fori_loop(0, whole, group, carry)
     for i in range(low + whole * step, high):
@@ -59,10 +62,9 @@
     return carry
 
 
-def level_weight(k, rate, total):
+def level_weights(rate, total):
     scale = total / sum(math.exp(-rate * j / LEVELS) for j in range(LEVELS))
-    height = jnp.full((8, LANES), k, jnp.int32).astype(jnp.float32)
-    return jnp.exp(height * (-rate / LEVELS)) * scale
+    return jnp.exp(iota((LEVELS, LANES), 0).astype(jnp.float32) * (-rate / LEVELS)) * scale
 
 
 def band_index():
@@ -73,9 +75,41 @@
     return 2 * depth + -(-depth // 3)
 
 
+def pack_slot(bands, k, air_ref, slot):
+    depth = air_ref.shape[1]
+    lane_tiles = air_ref.shape[3] // LANES
+    lane = iota((8, LANES), 1)
+    dest = lax.rem(band_index() + k, bands)
+    odd = lax.rem(dest, 2)
+    own = pl.multiple_of((dest // 2) * LANES, LANES)
+    high = (dest + 1) // 2
+    right = pl.multiple_of(jnp.minimum(high, lane_tiles - 1) * LANES, LANES)
+    left = pl.multiple_of(jnp.maximum(high - 1, 0) * LANES, LANES)
+    turn = 64 * odd
+    back = 64 - turn
+    from_right = lane < 96 - turn
+    for l in range(depth):
+        for p in range(2):
+            first = air_ref[2 * p, l, :, pl.ds(own, LANES)]
+            second = air_ref[2 * p + 1, l, :, pl.ds(own, LANES)]
+            slot[2 * l + p] = jnp.where(lane < 64, roll(first, turn, 1), roll(second, back, 1))
+    for g in range(-(-depth // 3)):
+        packed = jnp.zeros((8, LANES), jnp.float32)
+        for l in range(3 * g, min(3 * g + 3, depth)):
+            for f in range(4):
+                j = (l - 3 * g) * 4 + f
+                edge = jnp.where(
+                    from_right, air_ref[f, l, :, pl.ds(right, LANES)], air_ref[f, l, :, pl.ds(left, LANES)]
+                )
+                edge = roll(edge, 4 * j + back, 1)
+                here = ((lane >= 4 * j) & (lane < 4 * j + 4)) | ((lane >= 60 + 4 * j) & (lane < 64 + 4 * j))
+                packed = jnp.where(here, edge, packed)
+        slot[2 * depth + g] = packed
+
+
 def pack_kernel(bands, *refs):
-    sources, outs, scratch, sems = refs[:5], refs[5 : bands + 7], refs[bands + 7 : bands + 12], refs[bands + 12]
-    slots, up_ref, down_ref = outs[:bands], outs[bands], outs[bands + 1]
+    sources, outs, scratch, sems = refs[:5], refs[5 : bands + 6], refs[bands + 6 : bands + 11], refs[bands + 11]
+    slots, up_ref, down_ref = outs[: bands - 1], outs[bands - 1], outs[bands]
     copies = [pltpu.make_async_copy(a, b, sems.at[n]) for n, (a, b) in enumerate(zip(sources, scratch))]
     for copy in copies:
         copy.start()
@@ -83,9 +117,7 @@
         copy.wait()
     air_ref, level_ref, fuel_ref, class_ref, ignite_ref = scratch
     depth = air_ref.shape[1]
-    lane_tiles = air_ref.shape[3] // LANES
     rows, width = level_ref.shape
-    lane = iota((8, LANES), 1)
     fields = [ref[...] for ref in (level_ref, fuel_ref)]
     fields += [ref[...].astype(jnp.float32) for ref in (class_ref, ignite_ref)]
     for a, field in enumerate(fields):
@@ -99,37 +131,15 @@
         first, second = fields[2 * pair], fields[2 * pair + 1]
         at = pl.ds(base + pair * (rows // 8), rows // 8)
         to_next = jnp.where(wide < 64, roll(second[:, width - LANES :], 64, 1), first[:, width - LANES :])
-        slots[1][at] = to_next.reshape(rows // 8, 8, LANES)
+        slots[0][at] = to_next.reshape(rows // 8, 8, LANES)
         to_prev = jnp.where(wide < 64, first[:, :LANES], roll(second[:, :LANES], 64, 1))
-        slots[bands - 1][at] = to_prev.reshape(rows // 8, 8, LANES)
-    band = band_index()
-    for k in range(bands):
-        dest = lax.rem(band + k, bands)
-        odd = lax.rem(dest, 2)
-        own = pl.multiple_of((dest // 2) * LANES, LANES)
-        high = (dest + 1) // 2
-        right = pl.multiple_of(jnp.minimum(high, lane_tiles - 1) * LANES, LANES)
-        left = pl.multiple_of(jnp.maximum(high - 1, 0) * LANES, LANES)
-        turn = 64 * odd
-        back = 64 - turn
-        from_right = lane < 96 - turn
-        for l in range(depth):
-            for p in range(2):
-                first = air_ref[2 * p, l, :, pl.ds(own, LANES)]
-                second = air_ref[2 * p + 1, l, :, pl.ds(own, LANES)]
-                slots[k][2 * l + p] = jnp.where(lane < 64, roll(first, turn, 1), roll(second, back, 1))
-        for g in range(-(-depth // 3)):
-            packed = jnp.zeros((8, LANES), jnp.float32)
-            for l in range(3 * g, min(3 * g + 3, depth)):
-                for f in range(4):
-                    j = (l - 3 * g) * 4 + f
-                    edge = jnp.where(
-                        from_right, air_ref[f, l, :, pl.ds(right, LANES)], air_ref[f, l, :, pl.ds(left, LANES)]
-                    )
-                    edge = roll(edge, 4 * j + back, 1)
-                    here = ((lane >= 4 * j) & (lane < 4 * j + 4)) | ((lane >= 60 + 4 * j) & (lane < 64 + 4 * j))
-                    packed = jnp.where(here, edge, packed)
-            slots[k][2 * depth + g] = packed
+        slots[bands - 2][at] = to_prev.reshape(rows // 8, 8, LANES)
+    for k in range(1, bands):
+        pack_slot(bands, k, air_ref, slots[k - 1])
+
+
+def keep_kernel(bands, air_ref, slot):
+    pack_slot(bands, 0, air_ref, slot)
 
 
 def corner_tiles(next_ref, prev_ref, base, rows):
@@ -203,7 +213,7 @@
     fill(EDGE + rows, EDGE, lambda j, at: down_ref[2, j, at])
 
 
-def main_kernel(bands, plan_ref, tables_ref, level_in, fuel_in, ignite_in, *refs):
+def main_kernel(bands, tables_ref, level_in, fuel_in, ignite_in, *refs):
     slots = refs[:bands]
     fire_up, fire_down, edge_up, edge_down = refs[bands : bands + 4]
     values_in = refs[bands + 4 : bands + 8]
@@ -212,7 +222,8 @@
     scratch = list(refs[2 * bands + 10 :])
     lev_a, lev_b, fuel, ignite = scratch[:4]
     pace, burnt, wind_u, wind_v, energy, vapour, air_a, air_b = scratch[4:12]
-    values_side = scratch[12:]
+    values_side = scratch[12:16]
+    weights = scratch[16]
     tile, band, tile_count = lax.axis_index("tile"), band_index(), lax.axis_size("tile")
     rows, width = level_in.shape
     tiles = width // LANES
@@ -336,32 +347,40 @@
                 held[f, layer_at(-1, part)] = nothing
                 held[f, layer_at(LEVELS, part)] = nothing
 
-    cell, column = iota((LANES, LANES), 0), iota((LANES, LANES), 1)
-    start = jnp.where(
-        column < 64 + HALO,
-        REFINE * column,
-        jnp.where(column >= LANES - HALO, REFINE * column + (tiles + 1) * LANES - REFINE * LANES, -LANES * 1000),
-    )
-    across = []
-    for j in range(tiles + 1):
-        place = cell + j * LANES
-        across.append(jnp.where((place >= start) & (place < start + REFINE), 1.0, 0.0).astype(jnp.bfloat16))
-    outward = [jnp.concatenate([matrix] * 2, axis=1) for matrix in across]
-    across = [jnp.concatenate([matrix] * 2, axis=0) for matrix in across]
-    cell, column = iota((span, 16), 0), iota((span, 16), 1)
-    start = jnp.where(column < 8 + HALO, EDGE + REFINE * column, REFINE * (column - 12))
-    along = jnp.where((cell >= start) & (cell < start + REFINE), 1.0, 0.0).astype(jnp.float32)
+    weights[0] = level_weights(2.0, float(LEVELS))
+    weights[1] = level_weights(1.0, 1.0)
+    for held in (energy, vapour):
+        for j in range(tiles + 1):
+            held[j, :8] = nothing
+            held[j, span - 8 :] = nothing
+
+    def covers(shape, cell_dim):
+        cell, column = iota(shape, cell_dim), iota(shape, 1 - cell_dim)
+        start = jnp.where(
+            column < 64 + HALO,
+            REFINE * column,
+            jnp.where(column >= LANES - HALO, REFINE * column + (tiles + 1 - REFINE) * LANES, -LANES * 1000),
+        )
+        return jnp.where((cell >= start) & (cell < start + REFINE), 1.0, 0.0).astype(jnp.bfloat16)
+
+    cells = (tiles + 1) * LANES
+    to_cells = jnp.concatenate([covers((LANES, cells), 1)] * 2, axis=0)
+    to_columns = jnp.concatenate([covers((cells, LANES), 0)] * 2, axis=0)
 
     def parts(value, axis):
         high = value.astype(jnp.bfloat16)
         low = (value - high.astype(jnp.float32)).astype(jnp.bfloat16)
         return jnp.concatenate([high, low], axis=axis)
 
-    def dot(a, b, dims):
-        return lax.dot_general(a, b, (dims, ((), ())), preferred_element_type=jnp.float32)
+    def dot(a, b):
+        return jnp.dot(a, b, preferred_element_type=jnp.float32)
+
+    def swap(a, b):
+        a, b = roll(a, 4, 0), roll(b, 4, 0)
+        return jnp.where(sub < 4, a, b), jnp.where(sub < 4, b, a)
 
     def blow(total, k, result):
-        weight = level_weight(k, 1.0, 1.0)
+        weight = weights[1, pl.ds(k, 1)]
         return [a + weight * b for a, b in zip(total, result)]
 
     def first_wind(k, carry):
@@ -377,18 +396,19 @@
     state, other = air_a, air_b
     for c in range(STEPS):
         reach = EDGE - REFINE * (c + 1)
-        fire_step = plan_ref[c].astype(jnp.float32) * fire_delta
+        fire_step = tables_ref[4, c]
 
         def strips(margin):
             return (EDGE - margin) // 8, -(-(EDGE + rows + margin) // 8)
 
-        low, high = (8 * t for t in strips(reach + SUBSTEPS - 1))
-        spread_rows = jnp.concatenate([along[low:high].astype(jnp.bfloat16)] * 2, axis=1)
-        coarse = parts(jnp.concatenate(wind, axis=0) * wind_gain, 1)
-        for j in range(tiles + 1):
-            wide = parts(dot(coarse, outward[j], ((1,), (1,))).reshape(2, 16, LANES), 1)
-            wind_u[j, low:high] = dot(spread_rows, wide[0], ((1,), (0,)))
-            wind_v[j, low:high] = dot(spread_rows, wide[1], ((1,), (0,)))
+        coarse = [half for n in range(2) for half in swap(wind[2 * n + 1], wind[2 * n])]
+        wide = dot(parts(jnp.concatenate(coarse, axis=0) * wind_gain, 1), to_cells)
+        for n, held in enumerate((wind_u, wind_v)):
+            for j in range(tiles + 1):
+                for half in range(2):
+                    value = wide[16 * n + 8 * half : 16 * n + 8 * half + 8, j * LANES : (j + 1) * LANES]
+                    for row in range(REFINE):
+                        held[j, pl.ds(half * (span // 2) + row, 8, stride=REFINE)] = value
 
         before, after = lev_a, lev_b
         for s in range(SUBSTEPS):
@@ -443,18 +463,25 @@
             mend_rows(after)
             before, after = after, before
 
-        low, high = (8 * t for t in strips(reach))
-        gather_rows = along[low:high].astype(jnp.bfloat16)
+        totals = []
+        for held in (energy, vapour):
+            for half in range(2):
+                total = []
+                for j in range(tiles + 1):
+                    value = [held[j, pl.ds(half * (span // 2) + row, 8, stride=REFINE)] for row in range(REFINE)]
+                    while len(value) > 1:
+                        value = [sum(value[n : n + 2]) for n in range(0, len(value), 2)]
+                    total.append(value[0])
+                totals.append(jnp.concatenate(total, axis=1))
+        flux = dot(parts(jnp.concatenate(totals, axis=0), 1), to_columns)
         forcing = []
-        for held, gain in ((energy, heat_gain), (vapour, vapour_gain)):
-            total = dot(parts(held[0, low:high], 1), across[0], ((1,), (0,)))
-            for j in range(1, tiles + 1):
-                total = total + dot(parts(held[j, low:high], 1), across[j], ((1,), (0,)))
-            both = dot(gather_rows, parts(total, 1), ((0,), (0,)))
-            flux = (both[:, :LANES] + both[:, LANES:]) * (air_delta * gain / (REFINE * REFINE))
-            forcing.append([jnp.where(inside[part], flux[8 * part : 8 * part + 8], 0.0) for part in range(2)])
-
-        def air_step(k, part, state=state, forcing=forcing):
+        for n, gain in enumerate((heat_gain, vapour_gain)):
+            first, second = (flux[16 * n + 8 * half : 16 * n + 8 * half + 8] for half in range(2))
+            halo, inner = swap(second, first)
+            scale = air_delta * gain / (REFINE * REFINE)
+            forcing.append([jnp.where(mask, value * scale, 0.0) for mask, value in zip(inside, (inner, halo))])
+
+        def air_step(k, part, height, state=state, forcing=forcing):
             at = layer_at(k, part + 1)
             here = [state[f, at] for f in range(4)]
             west = [state[f, layer_at(k, part + 1, -1)] for f in range(4)]
@@ -466,7 +493,6 @@
             to_west, to_east = mix + jnp.maximum(u, 0.0), mix - jnp.minimum(u, 0.0)
             to_south, to_north = mix + jnp.maximum(v, 0.0), mix - jnp.minimum(v, 0.0)
             keep = (1.0 - 6.0 * spread) - (jnp.abs(u) + jnp.abs(v))
-            height = level_weight(k, 2.0, float(LEVELS))
             result = []
             for f in range(4):
                 new = keep * here[f] + mix * (state[f, layer_at(k - 1, part + 1)] + state[f, layer_at(k + 1, part + 1)])
@@ -482,7 +508,8 @@
         if c < STEPS - 1:
 
             def layer(k, carry, other=other, air_step=air_step):
-                result = [air_step(k, part) for part in range(2)]
+                height = weights[0, pl.ds(k, 1)]
+                result = [air_step(k, part, height) for part in range(2)]
                 for part in range(2):
                     for f in range(4):
                         put(other, f, k, part + 1, result[part][f])
@@ -495,7 +522,7 @@
                 first = lax.rem(band + k, bands) * depth
 
                 def final(l, carry, out=outs[k], first=first, air_step=air_step):
-                    result = air_step(first + l, 0)
+                    result = air_step(first + l, 0, weights[0, pl.ds(first + l, 1)])
                     for p in range(2):
                         out[2 * l + p] = jnp.where(lane < 64, result[2 * p], roll(result[2 * p + 1], 64, 1))
                     return carry
@@ -553,7 +580,8 @@
     heat_content,
     moisture_content,
 ):
-    tables = jnp.stack([spread_rate, burn_time, heat_content, moisture_content])
+    steps = jnp.pad(plan.astype(jnp.float32) * fire_delta, (0, NFUEL - STEPS))
+    tables = jnp.stack([spread_rate, burn_time, heat_content, moisture_content, steps])
     bands = lax.axis_size(BANDS)
     tile_count = lax.axis_size("tile")
     depth = air_state.shape[1]
@@ -566,9 +594,9 @@
     sizes = [count + (extra if k in (1, bands - 1) else 0) for k in range(bands)]
     packed = pl.pallas_call(
         functools.partial(pack_kernel, bands),
-        out_shape=[shape(size, 8, LANES) for size in sizes] + [shape(4, tiles, EDGE, LANES)] * 2,
+        out_shape=[shape(size, 8, LANES) for size in sizes[1:]] + [shape(4, tiles, EDGE, LANES)] * 2,
         in_specs=[pl.BlockSpec(memory_space=pltpu.HBM)] * 5,
-        out_specs=[vmem()] * (bands + 2),
+        out_specs=[vmem()] * (bands + 1),
         scratch_shapes=[
             pltpu.VMEM(x.shape, x.dtype) for x in (air_state, fire_level, fuel_left, fuel_class, ignition)
         ]
@@ -576,7 +604,16 @@
         compiler_params=pltpu.CompilerParams(vmem_limit_bytes=PACK_LIMIT),
         name="pack",
     )(air_state, fire_level, fuel_left, fuel_class, ignition)
-    slots, up, down = packed[:bands], packed[bands], packed[bands + 1]
+    slots, up, down = packed[: bands - 1], packed[bands - 1], packed[bands]
+    kept = pl.pallas_call(
+        functools.partial(keep_kernel, bands),
+        out_shape=shape(count, 8, LANES),
+        in_specs=[vmem()],
+        out_specs=vmem(),
+        compiler_params=params,
+        cost_estimate=pl.CostEstimate(flops=KEEP_FLOPS, bytes_accessed=0, transcendentals=0),
+        name="keep",
+    )(air_state)
 
     rise = [(i, i + 1) for i in range(tile_count - 1)]
     sink = [(j, i) for i, j in rise]
@@ -589,7 +626,7 @@
 
     fire_up = lax.ppermute(down, "tile", rise)
     fire_down = lax.ppermute(up, "tile", sink)
-    slots = turn(slots)
+    slots = turn([kept, *slots])
     edges = (bands // 2) * count + 4 * (EDGE // 8)
     up, down = pl.pallas_call(
         functools.partial(relay_kernel, bands, rows),
@@ -620,13 +657,12 @@
     results = pl.pallas_call(
         functools.partial(main_kernel, bands),
         out_shape=[shape(rows, width)] * 2 + [shape(2 * depth, 8, LANES)] * bands,
-        in_specs=[smem()] * 2 + [vmem()] * (3 + bands + 8),
+        in_specs=[smem()] + [vmem()] * (3 + bands + 8),
         out_specs=[vmem()] * (2 + bands),
-        scratch_shapes=[fire] * 4 + [flat] * 6 + [atmosphere] * 2 + [side] * 4,
+        scratch_shapes=[fire] * 4 + [flat] * 6 + [atmosphere] * 2 + [side] * 4 + [pltpu.VMEM((2, LEVELS, LANES), jnp.float32)],
         compiler_params=params,
         name="window",
     )(
-        plan,
         tables,
         fire_level,
         fuel_left,

time: 76.3 us -> 70.2 us (0.920)
  Pallas kernels: 34.3 us -> 29.6 us
  waiting for transfers between devices: 21 us -> 23.6 us
  starting transfers between devices: 17.1 us -> 15.3 us
  local copies, waits for them, and re-layouts: 2.26 us -> 0.72 us
    pallas_call x1, Pallas kernels: 27.7 us -> 22.8 us  [local(): pl.pallas_call(functools.partial(main_kernel, bands), out_shape=[shape(ro...]
    ppermute x6, starting transfers between devices: 8.52 us -> 5.28 us  [turn(): lax.ppermute(values[k], BANDS, [(i, (i + k) % bands) for i in range(bands)])]
    ppermute x1, waiting for transfers between devices: 4.85 us -> 7.42 us  [local(): edge_up = lax.ppermute(down, 'tile', rise)]
    unnamed x20, local copies, waits for them, and re-layouts: 2.26 us -> 0.69 us
    ppermute x1, starting transfers between devices: 2.51 us -> 3.77 us  [local(): edge_up = lax.ppermute(down, 'tile', rise)]
  transfers between devices with their start and end apart: 10 -> 10, of which waited for: 6 -> 7; matrix products, arithmetic and copies ran while one was open for 0% -> 0% of each run, Pallas kernels for 2% -> 3%
where the time goes in v3:
time: 70.2 us; the launch traced here: 70 us
  Pallas kernels  29.6 us (42%)
  waiting for transfers between devices  23.6 us (34%)
  starting transfers between devices  15.3 us (22%)
  between operations  0.82 us (1%)
  local copies, waits for them, and re-layouts  0.72 us (1%)
    pallas_call x1, Pallas kernels, local(): pl.pallas_call(functools.partial(main_kernel, bands), out_shape=[shape(ro...  22.8 us
    ppermute x6, waiting for transfers between devices, turn(): lax.ppermute(values[k], BANDS, [(i, (i + k) % bands) for i in range(bands)])  12.1 us
    ppermute x1, waiting for transfers between devices, local(): edge_up = lax.ppermute(down, 'tile', rise)  7.42 us
    ppermute x6, starting transfers between devices, turn(): lax.ppermute(values[k], BANDS, [(i, (i + k) % bands) for i in range(bands)])  5.28 us
    ppermute x1, waiting for transfers between devices, local(): edge_down = lax.ppermute(up, 'tile', sink)  4.06 us
    ppermute x1, starting transfers between devices, local(): edge_up = lax.ppermute(down, 'tile', rise)  3.77 us
    ppermute x1, starting transfers between devices, local(): fire_up = lax.ppermute(down, 'tile', rise)  3.48 us
    pallas_call x1, Pallas kernels, local(): pl.pallas_call(functools.partial(pack_kernel, bands), out_shape=[shape(si...  3.1 us
  transfers between devices with their start and end apart: 10, of which 7 were waited for; matrix products, arithmetic and copies ran while one was open for 0% of the time, Pallas kernels for 3%

profile of v3, /device:TPU:1, one launch (start us, length us, event | category | flops | bytes accessed | tf_op | source)
XLA Modules:
  0.0 70.0 jit_solution(12597784807328178427)
XLA Ops:
  0.6 3.1 %pack.1 = (f32[67,8,128]{2,1,0:T(8,128)}, f32[47,8,128]{2,1,0:T(8,128)}, f32[67,8,128]{2,1,0:T(8,128)}, f32[4,5,40,128]{3,2,1,0:T(8,128)}, f32[4,5,40,128]{3,2,1,0:T(8,128)}) custom-call(f32[4,20,8,256]{3,2,1,0:T(8,128)} %refs_0_.1, f32[80,640]{1,0:T(8,128)} %level_in.1, f32[80,640]{1,0:T(8,128)} %fuel_in.1, s32[80,640]{1,0:T(8,128)} %class_ref.1, ...), custom_call_target="tpu_custom_call" | custom-call | tf_op jit(solution)/shard_map/pack/pallas_call | solution.py:595
  3.7 2.1 %collective-permute-start.1 = (f32[47,8,128]{2,1,0:T(8,128)}, f32[47,8,128]{2,1,0:T(8,128)S(1)}, u32[]{:S(2)}, u32[]{:S(2)}) collective-permute-start(f32[47,8,128]{2,1,0:T(8,128)} %get-tuple-element.21), channel_id=1, source_target_pairs={{0,2},{1,3},{2,0},{3,1},{4,6},{5,7},{6,4},{7,5},{8,10},{9,11},{10,... | collective-permute-start | bytes 577544 | tf_op jit(solution)/shard_map/ppermute | solution.py:624
  5.9 0.6 collective-permute-start
  6.5 0.3 collective-permute-start.2
  6.8 3.5 %collective-permute-start.3 = (f32[4,5,40,128]{3,2,1,0:T(8,128)}, f32[4,5,40,128]{3,2,1,0:T(8,128)S(1)}, u32[]{:S(2)}, u32[]{:S(2)}) collective-permute-start(f32[4,5,40,128]{3,2,1,0:T(8,128)} %get-tuple-element.23), channel_id=1, source_target_pairs={{0,4},{4,8},{8,12},{1,5},{5,9},{9,13},{2,6},{6,10},{10,14},{3,7},{... | collective-permute-start | bytes 1228808 | tf_op jit(solution)/shard_map/ppermute | solution.py:627
  10.3 1.3 %collective-permute-start.4 = (f32[4,5,40,128]{3,2,1,0:T(8,128)}, f32[4,5,40,128]{3,2,1,0:T(8,128)S(1)}, u32[]{:S(2)}, u32[]{:S(2)}) collective-permute-start(f32[4,5,40,128]{3,2,1,0:T(8,128)} %get-tuple-element.24), channel_id=1, source_target_pairs={{4,0},{8,4},{12,8},{5,1},{9,5},{13,9},{6,2},{10,6},{14,10},{7,3},{... | collective-permute-start | bytes 1228808 | tf_op jit(solution)/shard_map/ppermute | solution.py:628
  11.6 0.0 copy-start.5
  11.7 0.0 copy-start.6
  11.7 0.0 copy-start.7
  11.7 0.6 copy-done.5
  12.3 0.0 copy-done.6
  12.3 0.0 copy-done.7
  12.4 0.3 keep.1.refs_0_
  12.6 0.0 copy-start.4
  12.6 2.9 %collective-permute-done.refs_1_ = f32[67,8,128]{2,1,0:T(8,128)S(1)} collective-permute-done((f32[67,8,128]{2,1,0:T(8,128)}, f32[67,8,128]{2,1,0:T(8,128)S(1)}, u32[]{:S(2)}, u32[]{:S(2)}) %collective-permute-start) | collective-permute-done | bytes 274464 | tf_op jit(solution)/shard_map/ppermute | solution.py:624
  15.5 1.5 %collective-permute-done.2.refs_3_ = f32[67,8,128]{2,1,0:T(8,128)S(1)} collective-permute-done((f32[67,8,128]{2,1,0:T(8,128)}, f32[67,8,128]{2,1,0:T(8,128)S(1)}, u32[]{:S(2)}, u32[]{:S(2)}) %collective-permute-start.2) | collective-permute-done | bytes 274464 | tf_op jit(solution)/shard_map/ppermute | solution.py:624
  17.0 0.2 relay.1
  17.2 3.8 %collective-permute-start.5 = (f32[114,8,128]{2,1,0:T(8,128)S(1)}, f32[114,8,128]{2,1,0:T(8,128)S(1)}, u32[]{:S(2)}, u32[]{:S(2)}) collective-permute-start(f32[114,8,128]{2,1,0:T(8,128)S(1)} %get-tuple-element.25), channel_id=1, source_target_pairs={{0,4},{4,8},{8,12},{1,5},{5,9},{9,13},{2,6},{6,10},{10,14},{3,7},{... | collective-permute-start | bytes 1400840 | tf_op jit(solution)/shard_map/ppermute | solution.py:640
  21.0 0.0 copy-start
  21.0 0.0 copy-start.1
  21.0 1.4 %collective-permute-start.6 = (f32[114,8,128]{2,1,0:T(8,128)S(1)}, f32[114,8,128]{2,1,0:T(8,128)S(1)}, u32[]{:S(2)}, u32[]{:S(2)}) collective-permute-start(f32[114,8,128]{2,1,0:T(8,128)S(1)} %get-tuple-element.26), channel_id=1, source_target_pairs={{4,0},{8,4},{12,8},{5,1},{9,5},{13,9},{6,2},{10,6},{14,10},{7,3},{... | collective-permute-start | bytes 1400840 | tf_op jit(solution)/shard_map/ppermute | solution.py:641
  22.5 1.5 %survey.1 = (f32[5,160,128]{2,1,0:T(8,128)S(1)}, f32[5,160,128]{2,1,0:T(8,128)S(1)}, f32[5,160,128]{2,1,0:T(8,128)S(1)}, f32[5,160,128]{2,1,0:T(8,128)S(1)}) custom-call(f32[5,13]{1,0:T(8,128)S(1)} %stack.23.tables_ref, s32[80,640]{1,0:T(8,128)S(1)} %copy-done.4, f32[4,5,40,128]{3,2,1,0:T(8,128)S(1)} %collective-permute-done.3.up_ref.refs_4_, ...), custom_call_target="tpu_custom_call" | custom-call | flops 10000000000 | tf_op jit(solution)/shard_map/survey/pallas_call | solution.py:644
  24.0 7.4 %collective-permute-done.5.refs_6_ = f32[114,8,128]{2,1,0:T(8,128)S(1)} collective-permute-done((f32[114,8,128]{2,1,0:T(8,128)S(1)}, f32[114,8,128]{2,1,0:T(8,128)S(1)}, u32[]{:S(2)}, u32[]{:S(2)}) %collective-permute-start.5) | collective-permute-done | bytes 466976 | tf_op jit(solution)/shard_map/ppermute | solution.py:640
  31.5 4.1 %collective-permute-done.6.refs_7_ = f32[114,8,128]{2,1,0:T(8,128)S(1)} collective-permute-done((f32[114,8,128]{2,1,0:T(8,128)S(1)}, f32[114,8,128]{2,1,0:T(8,128)S(1)}, u32[]{:S(2)}, u32[]{:S(2)}) %collective-permute-start.6) | collective-permute-done | bytes 466976 | tf_op jit(solution)/shard_map/ppermute | solution.py:641
  35.5 22.8 %window.1 = (f32[80,640]{1,0:T(8,128)}, f32[80,640]{1,0:T(8,128)}, f32[40,8,128]{2,1,0:T(8,128)S(1)}, f32[40,8,128]{2,1,0:T(8,128)S(1)}, f32[40,8,128]{2,1,0:T(8,128)S(1)}, /*index=5*/f32[40,8,128]{2,1,0:T(8,128)S(1)}) custom-call(f32[5,13]{1,0:T(8,128)S(1)} %stack.23.tables_ref, f32[80,640]{1,0:T(8,128)S(1)} %copy-done, f32[80,640]{1,0:T(8,128)S(1)} %copy-done.1, ...), custom_call_target="tpu_custom_call" | custom-call | tf_op jit(solution)/shard_map/window/pallas_call | solution.py:657
  58.3 1.7 %collective-permute-start.7 = (f32[40,8,128]{2,1,0:T(8,128)S(1)}, f32[40,8,128]{2,1,0:T(8,128)S(1)}, u32[]{:S(2)}, u32[]{:S(2)}) collective-permute-start(f32[40,8,128]{2,1,0:T(8,128)S(1)} %get-tuple-element.32), channel_id=1, source_target_pairs={{0,1},{1,2},{2,3},{3,0},{4,5},{5,6},{6,7},{7,4},{8,9},{9,10},{10,1... | collective-permute-start | bytes 491528 | tf_op jit(solution)/shard_map/ppermute | solution.py:624
  60.0 0.3 collective-permute-start.8
  60.3 0.2 collective-permute-start.9
  60.5 2.9 %collective-permute-done.7.refs_1_ = f32[40,8,128]{2,1,0:T(8,128)S(1)} collective-permute-done((f32[40,8,128]{2,1,0:T(8,128)S(1)}, f32[40,8,128]{2,1,0:T(8,128)S(1)}, u32[]{:S(2)}, u32[]{:S(2)}) %collective-permute-start.7) | collective-permute-done | bytes 163872 | tf_op jit(solution)/shard_map/ppermute | solution.py:624
  63.4 4.3 %collective-permute-done.8.refs_2_ = f32[40,8,128]{2,1,0:T(8,128)S(1)} collective-permute-done((f32[40,8,128]{2,1,0:T(8,128)S(1)}, f32[40,8,128]{2,1,0:T(8,128)S(1)}, u32[]{:S(2)}, u32[]{:S(2)}) %collective-permute-start.8) | collective-permute-done | bytes 163872 | tf_op jit(solution)/shard_map/ppermute | solution.py:624
  67.7 0.6 collective-permute-done.9.refs_3_
  68.3 1.7 %unpack.1 = f32[4,20,8,256]{3,2,1,0:T(8,128)} custom-call(f32[40,8,128]{2,1,0:T(8,128)S(1)} %get-tuple-element.31.refs_0_, f32[40,8,128]{2,1,0:T(8,128)S(1)} %collective-permute-done.7.refs_1_, f32[40,8,128]{2,1,0:T(8,128)S(1)} %collective-permute-done.8.refs_2_, f32[40,8,128]{2,1,0:T(8,128)S(1)} %collective-permute-done.9.refs_3_), custom_call_target="tpu_custom_call" | custom-call | tf_op jit(solution)/shard_map/unpack/pallas_call | solution.py:679
  (17 shorter events, 0.1 us)
Async XLA Ops:
  0.6 11.7 %copy-start.3 = (f32[4,20,8,256]{3,2,1,0:T(8,128)S(1)}, f32[4,20,8,256]{3,2,1,0:T(8,128)}, u32[]{:S(2)}) copy-start(f32[4,20,8,256]{3,2,1,0:T(8,128)} %refs_0_.1) | copy-start | bytes 1966084
  3.7 8.9 %collective-permute-start.1 = (f32[47,8,128]{2,1,0:T(8,128)}, f32[47,8,128]{2,1,0:T(8,128)S(1)}, u32[]{:S(2)}, u32[]{:S(2)}) collective-permute-start(f32[47,8,128]{2,1,0:T(8,128)} %get-tuple-element.21), channel_id=1, source_target_pairs={{0,2},{1,3},{2,0},{3,1},{4,6},{5,7},{6,4},{7,5},{8,10},{9,11},{10,... | collective-permute-start | bytes 577544 | tf_op jit(solution)/shard_map/ppermute | solution.py:624
  5.9 9.7 %collective-permute-start = (f32[67,8,128]{2,1,0:T(8,128)}, f32[67,8,128]{2,1,0:T(8,128)S(1)}, u32[]{:S(2)}, u32[]{:S(2)}) collective-permute-start(f32[67,8,128]{2,1,0:T(8,128)} %get-tuple-element.20), channel_id=1, source_target_pairs={{0,1},{1,2},{2,3},{3,0},{4,5},{5,6},{6,7},{7,4},{8,9},{9,10},{10,1... | collective-permute-start | bytes 823304 | tf_op jit(solution)/shard_map/ppermute | solution.py:624
  6.5 5.2 %copy-start.8 = (f32[13]{0:T(128)S(1)}, f32[13]{0:T(128)}, u32[]{:S(2)}) copy-start(f32[13]{0:T(128)} %param.19) | copy-start | bytes 160
  6.5 10.5 %collective-permute-start.2 = (f32[67,8,128]{2,1,0:T(8,128)}, f32[67,8,128]{2,1,0:T(8,128)S(1)}, u32[]{:S(2)}, u32[]{:S(2)}) collective-permute-start(f32[67,8,128]{2,1,0:T(8,128)} %get-tuple-element.22), channel_id=1, source_target_pairs={{0,3},{1,0},{2,1},{3,2},{4,7},{5,4},{6,5},{7,6},{8,11},{9,8},{10,9... | collective-permute-start | bytes 823304 | tf_op jit(solution)/shard_map/ppermute | solution.py:624
  6.8 4.8 %copy-start.9 = (s32[4]{0:T(128)S(1)}, s32[4]{0:T(128)}, u32[]{:S(2)}) copy-start(s32[4]{0:T(128)} %param.15) | copy-start | bytes 52
  6.8 15.6 %collective-permute-start.3 = (f32[4,5,40,128]{3,2,1,0:T(8,128)}, f32[4,5,40,128]{3,2,1,0:T(8,128)S(1)}, u32[]{:S(2)}, u32[]{:S(2)}) collective-permute-start(f32[4,5,40,128]{3,2,1,0:T(8,128)} %get-tuple-element.23), channel_id=1, source_target_pairs={{0,4},{4,8},{8,12},{1,5},{5,9},{9,13},{2,6},{6,10},{10,14},{3,7},{... | collective-permute-start | bytes 1228808 | tf_op jit(solution)/shard_map/ppermute | solution.py:627
  10.3 12.2 %collective-permute-start.4 = (f32[4,5,40,128]{3,2,1,0:T(8,128)}, f32[4,5,40,128]{3,2,1,0:T(8,128)S(1)}, u32[]{:S(2)}, u32[]{:S(2)}) collective-permute-start(f32[4,5,40,128]{3,2,1,0:T(8,128)} %get-tuple-element.24), channel_id=1, source_target_pairs={{4,0},{8,4},{12,8},{5,1},{9,5},{13,9},{6,2},{10,6},{14,10},{7,3},{... | collective-permute-start | bytes 1228808 | tf_op jit(solution)/shard_map/ppermute | solution.py:628
  11.6 0.7 copy-start.5
  11.7 0.7 copy-start.6
  11.7 0.7 copy-start.7
  12.6 9.9 %copy-start.4 = (s32[80,640]{1,0:T(8,128)S(1)}, s32[80,640]{1,0:T(8,128)}, u32[]{:S(2)}) copy-start(s32[80,640]{1,0:T(8,128)} %class_ref.1) | copy-start | bytes 614404
  17.2 14.2 %collective-permute-start.5 = (f32[114,8,128]{2,1,0:T(8,128)S(1)}, f32[114,8,128]{2,1,0:T(8,128)S(1)}, u32[]{:S(2)}, u32[]{:S(2)}) collective-permute-start(f32[114,8,128]{2,1,0:T(8,128)S(1)} %get-tuple-element.25), channel_id=1, source_target_pairs={{0,4},{4,8},{8,12},{1,5},{5,9},{9,13},{2,6},{6,10},{10,14},{3,7},{... | collective-permute-start | bytes 1400840 | tf_op jit(solution)/shard_map/ppermute | solution.py:640
  21.0 14.5 %copy-start = (f32[80,640]{1,0:T(8,128)S(1)}, f32[80,640]{1,0:T(8,128)}, u32[]{:S(2)}) copy-start(f32[80,640]{1,0:T(8,128)} %level_in.1) | copy-start | bytes 614404
  21.0 14.5 %copy-start.1 = (f32[80,640]{1,0:T(8,128)S(1)}, f32[80,640]{1,0:T(8,128)}, u32[]{:S(2)}) copy-start(f32[80,640]{1,0:T(8,128)} %fuel_in.1) | copy-start | bytes 614404
  21.0 14.5 %copy-start.2 = (s32[80,640]{1,0:T(8,128)S(1)}, s32[80,640]{1,0:T(8,128)}, u32[]{:S(2)}) copy-start(s32[80,640]{1,0:T(8,128)} %ignite_in.1) | copy-start | bytes 614404
  21.0 14.5 %collective-permute-start.6 = (f32[114,8,128]{2,1,0:T(8,128)S(1)}, f32[114,8,128]{2,1,0:T(8,128)S(1)}, u32[]{:S(2)}, u32[]{:S(2)}) collective-permute-start(f32[114,8,128]{2,1,0:T(8,128)S(1)} %get-tuple-element.26), channel_id=1, source_target_pairs={{4,0},{8,4},{12,8},{5,1},{9,5},{13,9},{6,2},{10,6},{14,10},{7,3},{... | collective-permute-start | bytes 1400840 | tf_op jit(solution)/shard_map/ppermute | solution.py:641
  58.3 5.1 %collective-permute-start.7 = (f32[40,8,128]{2,1,0:T(8,128)S(1)}, f32[40,8,128]{2,1,0:T(8,128)S(1)}, u32[]{:S(2)}, u32[]{:S(2)}) collective-permute-start(f32[40,8,128]{2,1,0:T(8,128)S(1)} %get-tuple-element.32), channel_id=1, source_target_pairs={{0,1},{1,2},{2,3},{3,0},{4,5},{5,6},{6,7},{7,4},{8,9},{9,10},{10,1... | collective-permute-start | bytes 491528 | tf_op jit(solution)/shard_map/ppermute | solution.py:624
  60.0 7.7 %collective-permute-start.8 = (f32[40,8,128]{2,1,0:T(8,128)S(1)}, f32[40,8,128]{2,1,0:T(8,128)S(1)}, u32[]{:S(2)}, u32[]{:S(2)}) collective-permute-start(f32[40,8,128]{2,1,0:T(8,128)S(1)} %get-tuple-element.33), channel_id=1, source_target_pairs={{0,2},{1,3},{2,0},{3,1},{4,6},{5,7},{6,4},{7,5},{8,10},{9,11},{10,... | collective-permute-start | bytes 491528 | tf_op jit(solution)/shard_map/ppermute | solution.py:624
  60.3 8.0 %collective-permute-start.9 = (f32[40,8,128]{2,1,0:T(8,128)S(1)}, f32[40,8,128]{2,1,0:T(8,128)S(1)}, u32[]{:S(2)}, u32[]{:S(2)}) collective-permute-start(f32[40,8,128]{2,1,0:T(8,128)S(1)} %get-tuple-element.34), channel_id=1, source_target_pairs={{0,3},{1,0},{2,1},{3,2},{4,7},{5,4},{6,5},{7,6},{8,11},{9,8},{10,9... | collective-permute-start | bytes 491528 | tf_op jit(solution)/shard_map/ppermute | solution.py:624

commit v4 on v3

--- a/solution.py
+++ b/solution.py
@@ -17,6 +17,9 @@
 LANES = 128
 HALO = STEPS
 EDGE = HALO * REFINE
+BULK = 32
+HALO_ROWS = 4 * BULK + 8
+SENT_ROWS = HALO_ROWS + 8
 PAD = 8
 
 air_delta = 0.1
@@ -34,9 +37,10 @@
 UNROLL_FINAL = 10
 KEEP_FLOPS = 10**9
 RELAY_FLOPS = 5 * 10**9
-SURVEY_FLOPS = 10**10
+SURVEY_FLOPS = 10**9
+FIRST_FLOPS = 3 * 10**9
 PACK_LIMIT = 62 * 1024 * 1024
-VMEM_LIMIT = 40 * 1024 * 1024
+VMEM_LIMIT = 32 * 1024 * 1024
 
 
 def iota(shape, dim):
@@ -73,6 +77,29 @@
 
 def air_tiles(depth):
     return 2 * depth + -(-depth // 3)
+
+
+def halo_pack(fields, above):
+    rows = fields[0].shape[0]
+    sub = iota((8, LANES), 0)
+    if above:
+        bulk = [field[rows - BULK :] for field in fields]
+        odd = [fields[a][rows - BULK - 8 : rows - BULK] for a in (0, 2, 3)]
+        strip = jnp.where(sub >= 6, odd[0], jnp.where(sub >= 4, roll(odd[1], 6, 0), roll(odd[2], 4, 0)))
+    else:
+        bulk = [field[:BULK] for field in fields]
+        odd = [fields[a][BULK : BULK + 8] for a in (0, 2, 3)]
+        strip = jnp.where(sub < 2, odd[0], jnp.where(sub < 4, roll(odd[1], 2, 0), roll(odd[2], 4, 0)))
+    return jnp.concatenate(bulk + [strip], axis=0)
+
+
+def halo_unpack(packed, a, above):
+    bulk = packed[a * BULK : (a + 1) * BULK]
+    turn = {0: 0, 1: 0, 2: 2, 3: 4}[a]
+    strip = packed[4 * BULK : HALO_ROWS]
+    if turn:
+        strip = roll(strip, turn if above else 8 - turn, 0)
+    return jnp.concatenate([strip, bulk] if above else [bulk, strip], axis=0)
 
 
 def pack_slot(bands, k, air_ref, slot):
@@ -108,24 +135,49 @@
 
 
 def pack_kernel(bands, *refs):
-    sources, outs, scratch, sems = refs[:5], refs[5 : bands + 6], refs[bands + 6 : bands + 11], refs[bands + 11]
-    slots, up_ref, down_ref = outs[: bands - 1], outs[bands - 1], outs[bands]
+    sources, targets = refs[:5], refs[5 : bands + 6]
+    scratch, outs, sems = refs[bands + 6 : bands + 11], refs[bands + 11 : 2 * bands + 12], refs[2 * bands + 12]
+    slots = outs[: bands - 1]
     copies = [pltpu.make_async_copy(a, b, sems.at[n]) for n, (a, b) in enumerate(zip(sources, scratch))]
     for copy in copies:
         copy.start()
-    for copy in copies:
+    air_ref, level_ref, fuel_ref, class_ref, ignite_ref = scratch
+    base = air_tiles(air_ref.shape[1])
+    rows, width = level_ref.shape
+    sent = []
+
+    def send(n, first=None, count=None):
+        source, target = outs[n], targets[n]
+        if count is not None:
+            source, target = source.at[pl.ds(first, count)], target.at[pl.ds(first, count)]
+        sent.append(pltpu.make_async_copy(source, target, sems.at[5 + len(sent)]))
+        sent[-1].start()
+
+    copies[0].wait()
+    for k in range(1, bands):
+        pack_slot(bands, k, air_ref, slots[k - 1])
+        send(k - 1, 0, base)
+    weights = refs[2 * bands + 13]
+    weights[...] = level_weights(1.0, 1.0)
+    depth = air_ref.shape[1]
+    sub = iota((8, LANES), 0)
+    for j in range(width // LANES):
+        share = [jnp.zeros((8, LANES), jnp.float32)] * 2
+        if j < air_ref.shape[3] // LANES:
+            for l in range(depth):
+                weight = weights[pl.ds(band_index() * depth + l, 1)]
+                for f in range(2):
+                    share[f] = share[f] + weight * air_ref[2 + f, l, :, j * LANES : (j + 1) * LANES]
+        outs[bands - 1][j, HALO_ROWS:] = jnp.where(sub < 4, share[0], roll(share[1], 4, 0))
+        outs[bands][j, HALO_ROWS:] = jnp.where(sub < 4, roll(share[0], 4, 0), share[1])
+    for copy in copies[1:]:
         copy.wait()
-    air_ref, level_ref, fuel_ref, class_ref, ignite_ref = scratch
-    depth = air_ref.shape[1]
-    rows, width = level_ref.shape
     fields = [ref[...] for ref in (level_ref, fuel_ref)]
     fields += [ref[...].astype(jnp.float32) for ref in (class_ref, ignite_ref)]
-    for a, field in enumerate(fields):
+    for n, above in ((bands - 1, False), (bands, True)):
         for j in range(width // LANES):
-            cols = field[:, j * LANES : (j + 1) * LANES]
-            up_ref[a, j] = cols[:EDGE]
-            down_ref[a, j] = cols[rows - EDGE :]
-    base = air_tiles(depth)
+            outs[n][j, :HALO_ROWS] = halo_pack([field[:, j * LANES : (j + 1) * LANES] for field in fields], above)
+        send(n)
     wide = iota((rows, LANES), 1)
     for pair in range(2):
         first, second = fields[2 * pair], fields[2 * pair + 1]
@@ -134,8 +186,10 @@
         slots[0][at] = to_next.reshape(rows // 8, 8, LANES)
         to_prev = jnp.where(wide < 64, first[:, :LANES], roll(second[:, :LANES], 64, 1))
         slots[bands - 2][at] = to_prev.reshape(rows // 8, 8, LANES)
-    for k in range(1, bands):
-        pack_slot(bands, k, air_ref, slots[k - 1])
+    send(0, base, 2 * (rows // 8))
+    send(bands - 2, base, 2 * (rows // 8))
+    for copy in sent:
+        copy.wait()
 
 
 def keep_kernel(bands, air_ref, slot):
@@ -155,8 +209,10 @@
 
 
 def relay_kernel(bands, rows, *refs):
-    slots, up_ref, down_ref = refs[:bands], refs[bands], refs[bands + 1]
+    slots, (up_ref, down_ref, wind_ref, weights) = refs[:bands], refs[bands:]
     tiles = slots[0].shape[0]
+    depth = LEVELS // bands
+    lane = iota((8, LANES), 1)
     sub = iota((8, LANES), 0)
     for half in range(bands // 2):
         one, two = slots[2 * half], slots[2 * half + 1]
@@ -168,13 +224,48 @@
             return carry
 
         unrolled(0, tiles, 8, body, 0)
-    corners = corner_tiles(slots[bands - 1], slots[1], tiles, rows)
-    base = (bands // 2) * tiles
-    count = EDGE // 8
-    for a, corner in enumerate(corners):
-        at = pl.ds(base + a * count, count)
-        up_ref[at] = corner[:EDGE].reshape(count, 8, LANES)
-        down_ref[at] = corner[rows - EDGE :].reshape(count, 8, LANES)
+
+    weights[...] = level_weights(1.0, 1.0)
+    inner = [jnp.zeros((8, LANES), jnp.float32)] * 2
+    edges = jnp.zeros((8, LANES), jnp.float32)
+    for k in range(bands):
+        first = lax.rem(band_index() - k + bands, bands) * depth
+        for l in range(depth):
+            inner[l % 2] = inner[l % 2] + weights[pl.ds(first + l, 1)] * slots[k][2 * l + 1]
+        for g in range(-(-depth // 3)):
+            parts = [weights[pl.ds(first + min(3 * g + n, depth - 1), 1)] for n in range(3)]
+            weight = jnp.where(
+                (lane < 16) | ((lane >= 60) & (lane < 76)),
+                parts[0],
+                jnp.where((lane < 32) | ((lane >= 76) & (lane < 92)), parts[1], parts[2]),
+            )
+            edges = edges + weight * slots[k][2 * depth + g]
+    inner = inner[0] + inner[1]
+    for f in range(2):
+        halo = sum(roll(edges, 64 - 4 * (4 * n + 2 + f), 1) for n in range(3))
+        wind_ref[f] = jnp.where(lane < 64, inner if f == 0 else roll(inner, 64, 1), halo)
+
+
+def corner_kernel(bands, lane_tiles, up_ref, down_ref, *outs):
+    tiles = up_ref.shape[0]
+    lane = iota((8, LANES), 1)
+    wide = iota((HALO_ROWS, LANES), 1)
+    for k in range(bands):
+        dest = lax.rem(band_index() + k, bands)
+        odd = lax.rem(dest, 2)
+        high = (dest + 1) // 2
+        right = jnp.minimum(high, lane_tiles - 1)
+        left = jnp.maximum(high - 1, 0)
+        turn = 64 * odd
+        for n, ref in enumerate((up_ref, down_ref)):
+            inner, after, before = (ref[j, HALO_ROWS:] for j in (dest // 2, right, left))
+            edge = jnp.where(lane < 96 - turn, after, before)
+            outs[k][n] = jnp.where(lane < 64, roll(inner, turn, 1), roll(edge, turn, 1))
+    at = pl.ds(2, HALO_ROWS // 8)
+    up, down = up_ref[tiles - 1, :HALO_ROWS], down_ref[tiles - 1, :HALO_ROWS]
+    outs[1][at] = jnp.where(wide < 64, roll(down, 64, 1), up).reshape(HALO_ROWS // 8, 8, LANES)
+    up, down = up_ref[0, :HALO_ROWS], down_ref[0, :HALO_ROWS]
+    outs[bands - 1][at] = jnp.where(wide < 64, up, roll(down, 64, 1)).reshape(HALO_ROWS // 8, 8, LANES)
 
 
 def table_vectors(tables_ref):
@@ -198,161 +289,87 @@
     rows, width = class_ref.shape
     tiles = width // LANES
 
-    def fill(first, count, read):
-        def body(t, carry):
-            for j in range(tiles):
-                index = read(j, pl.ds(pl.multiple_of(8 * t, 8), 8)).astype(jnp.int32)
-                for vector, out in zip(vectors, outs):
-                    out[j, pl.ds(pl.multiple_of(first + 8 * t, 8), 8)] = pick(vector, index)
-            return carry
-
-        unrolled(0, count // 8, 5, body, 0)
-
-    fill(0, EDGE, lambda j, at: up_ref[2, j, at])
-    fill(EDGE, rows, lambda j, at: class_ref[at, j * LANES : (j + 1) * LANES])
-    fill(EDGE + rows, EDGE, lambda j, at: down_ref[2, j, at])
-
-
-def main_kernel(bands, tables_ref, level_in, fuel_in, ignite_in, *refs):
-    slots = refs[:bands]
-    fire_up, fire_down, edge_up, edge_down = refs[bands : bands + 4]
-    values_in = refs[bands + 4 : bands + 8]
-    level_out, fuel_out = refs[bands + 8 : bands + 10]
-    outs = refs[bands + 10 : 2 * bands + 10]
-    scratch = list(refs[2 * bands + 10 :])
-    lev_a, lev_b, fuel, ignite = scratch[:4]
-    pace, burnt, wind_u, wind_v, energy, vapour, air_a, air_b = scratch[4:12]
-    values_side = scratch[12:16]
-    weights = scratch[16]
+    def put(j, at, classes):
+        index = classes.astype(jnp.int32)
+        for vector, out in zip(vectors, outs):
+            out[j, at] = pick(vector, index)
+
+    for j in range(tiles):
+        for first, ref, above in ((0, up_ref, True), (EDGE + rows, down_ref, False)):
+            classes = halo_unpack(ref[j], 2, above)
+            for n in range(0, EDGE, 8):
+                put(j, slice(first + n, first + n + 8), classes[n : n + 8])
+
+    def body(t, carry):
+        for j in range(tiles):
+            at = pl.ds(pl.multiple_of(EDGE + 8 * t, 8), 8)
+            put(j, at, class_ref[pl.ds(pl.multiple_of(8 * t, 8), 8), j * LANES : (j + 1) * LANES])
+        return carry
+
+    unrolled(0, rows // 8, 5, body, 0)
+
+
+def slab_masks(bands):
     tile, band, tile_count = lax.axis_index("tile"), band_index(), lax.axis_size("tile")
-    rows, width = level_in.shape
-    tiles = width // LANES
-    depth = LEVELS // bands
-    count = air_tiles(depth)
-    own = PAD + EDGE
-    span = rows + 2 * EDGE
-    lane = iota((8, LANES), 1)
     first_tile, final_tile = tile == 0, tile == tile_count - 1
     first_band, final_band = band == 0, band == bands - 1
-
-    def strip(t, base=PAD):
-        return pl.ds(pl.multiple_of(base + 8 * t, 8), 8)
-
-    corners = corner_tiles(slots[bands - 1], slots[1], count, rows)
-    base = (bands // 2) * count
-    sides = []
-    for a, (source, held) in enumerate(((level_in, lev_a), (fuel_in, fuel), (None, None), (ignite_in, ignite))):
-        at = pl.ds(base + a * (EDGE // 8), EDGE // 8)
-        upper, lower = edge_up[at].reshape(EDGE, LANES), edge_down[at].reshape(EDGE, LANES)
-        if held is None:
-            side = jnp.concatenate([upper, corners[a], lower], axis=0).astype(jnp.int32)
-            vectors = table_vectors(tables_ref)
-            for n in range(span // 8):
-                for vector, out in zip(vectors, values_side):
-                    out[8 * n : 8 * n + 8] = pick(vector, side[8 * n : 8 * n + 8])
-            continue
-        for j in range(tiles):
-            held[j, PAD:own] = fire_up[a, j]
-            held[j, own : own + rows] = source[:, j * LANES : (j + 1) * LANES].astype(jnp.float32)
-            held[j, own + rows : own + rows + EDGE] = fire_down[a, j]
-        held[tiles, PAD:own] = upper
-        held[tiles, own : own + rows] = corners[a]
-        held[tiles, own + rows : own + rows + EDGE] = lower
-
-    def value_at(n, j, t):
-        return values_in[n][j, strip(t, 0)] if j < tiles else values_side[n][strip(t, 0)]
-
-    spare = jnp.zeros((tiles + 1, PAD, LANES), jnp.float32)
-    for held in (lev_a, lev_b):
-        held[:, :PAD] = spare
-        held[:, PAD + span :] = spare
-
-    def kindled(values, t, c):
-        return [
-            jnp.where(ignite[j, strip(t)] <= c, jnp.minimum(value, -1.0), value) for j, value in enumerate(values)
-        ]
-
-    mend_low = first_band & (lane == LANES - 1)
-    mend_high = final_band & (lane == 0)
-
-    def mend_lanes(values):
-        halo = jnp.where(mend_low, roll(values[0], LANES - 1, 1), values[tiles])
-        halo = jnp.where(mend_high, roll(values[tiles - 1], 1, 1), halo)
-        return values[:tiles] + [halo]
-
-    def mend_rows(held):
-        @pl.when(first_tile)
-        def _():
-            for j in range(tiles + 1):
-                held[j, own - 1 : own] = held[j, own : own + 1]
-
-        @pl.when(final_tile)
-        def _():
-            for j in range(tiles + 1):
-                held[j, own + rows : own + rows + 1] = held[j, own + rows - 1 : own + rows]
-
-    def kindle(t, carry):
-        values = mend_lanes(kindled([lev_a[j, strip(t)] for j in range(tiles + 1)], t, 0))
-        for j, value in enumerate(values):
-            lev_a[j, strip(t)] = value
-        return carry
-
-    unrolled(0, span // 8, UNROLL_LOOKUP, kindle, 0)
-    mend_rows(lev_a)
-
-    sub = iota((8, LANES), 0)
+    lane, sub = iota((8, LANES), 1), iota((8, LANES), 0)
     low_row = jnp.where(final_tile, 0, 4)
     high_row = jnp.where(first_tile, 8, 4)
     low_lane = jnp.where(final_band, 64, 68)
     high_lane = jnp.where(first_band, 128, 124)
     inside_own = (lane < low_lane) | (lane >= high_lane)
     inside = (inside_own, inside_own & ((sub < low_row) | (sub >= high_row)))
-
-    def layer_at(k, part, shift=0):
-        return pl.ds(pl.multiple_of((k + 1) * 24 + 8 * part, 8) + shift, 8)
-
-    def put(held, f, k, part, value):
-        held[f, layer_at(k, part)] = value
-        if part == 2:
-            held[f, layer_at(k, 0)] = value
-
-    for k in range(bands):
-        source = lax.rem(band - k + bands, bands)
-        half = k // 2
-
-        def whole(i, k=k, half=half):
-            below, above = edge_down[half * count + i], edge_up[half * count + i]
-            if k % 2 == 0:
-                halo = jnp.where(sub < 4, below, roll(above, 4, 0))
-            else:
-                halo = jnp.where(sub < 4, roll(below, 4, 0), above)
-            return slots[k][i], halo
-
-        for g in range(-(-depth // 3)):
-            edges = whole(2 * depth + g)
-            for l in range(3 * g, min(3 * g + 3, depth)):
-                for p in range(2):
-                    both = whole(2 * l + p)
-                    for f in range(2):
-                        j = (l - 3 * g) * 4 + 2 * p + f
-                        for part in range(2):
-                            inner = both[part] if f == 0 else roll(both[part], 64, 1)
-                            value = jnp.where(lane < 64, inner, roll(edges[part], 64 - 4 * j, 1))
-                            value = jnp.where(inside[part], value, 0.0)
-                            put(air_a, 2 * p + f, source * depth + l, part + 1, value)
-    nothing = jnp.zeros((8, LANES), jnp.float32)
-    for held in (air_a, air_b):
-        for f in range(4):
-            for part in range(3):
-                held[f, layer_at(-1, part)] = nothing
-                held[f, layer_at(LEVELS, part)] = nothing
-
-    weights[0] = level_weights(2.0, float(LEVELS))
-    weights[1] = level_weights(1.0, 1.0)
+    return first_tile, final_tile, first_band, final_band, inside
+
+
+def swap(a, b):
+    sub = iota((8, LANES), 0)
+    a, b = roll(a, 4, 0), roll(b, 4, 0)
+    return jnp.where(sub < 4, a, b), jnp.where(sub < 4, b, a)
+
+
+def strip(t, base=PAD):
+    return pl.ds(pl.multiple_of(base + 8 * t, 8), 8)
+
+
+def fire_steps(bands, tables_ref, tiles, rows, ignite, values_in, values_side, scratch):
+    pace, burnt, wind_u, wind_v, energy, vapour = scratch
+    first_tile, final_tile, first_band, final_band, inside = slab_masks(bands)
+    own = PAD + EDGE
+    span = rows + 2 * EDGE
+    lane = iota((8, LANES), 1)
     for held in (energy, vapour):
         for j in range(tiles + 1):
-            held[j, :8] = nothing
-            held[j, span - 8 :] = nothing
+            held[j, :16] = jnp.zeros((16, LANES), jnp.float32)
+            held[j, span - 16 :] = jnp.zeros((16, LANES), jnp.float32)
+
+    def value_at(n, j, t):
+        return values_in[n][j, strip(t, 0)] if j < tiles else values_side[n][strip(t, 0)]
+
+    def kindled(values, t, c):
+        return [
+            jnp.where(ignite[j, strip(t)] <= c, jnp.minimum(value, -1.0), value) for j, value in enumerate(values)
+        ]
+
+    mend_low = first_band & (lane == LANES - 1)
+    mend_high = final_band & (lane == 0)
+
+    def mend_lanes(values):
+        halo = jnp.where(mend_low, roll(values[0], LANES - 1, 1), values[tiles])
+        halo = jnp.where(mend_high, roll(values[tiles - 1], 1, 1), halo)
+        return values[:tiles] + [halo]
+
+    def mend_rows(held):
+        @pl.when(first_tile)
+        def _():
+            for j in range(tiles + 1):
+                held[j, own - 1 : own] = held[j, own : own + 1]
+
+        @pl.when(final_tile)
+        def _():
+            for j in range(tiles + 1):
+                held[j, own + rows : own + rows + 1] = held[j, own + rows - 1 : own + rows]
 
     def covers(shape, cell_dim):
         cell, column = iota(shape, cell_dim), iota(shape, 1 - cell_dim)
@@ -375,26 +392,7 @@
     def dot(a, b):
         return jnp.dot(a, b, preferred_element_type=jnp.float32)
 
-    def swap(a, b):
-        a, b = roll(a, 4, 0), roll(b, 4, 0)
-        return jnp.where(sub < 4, a, b), jnp.where(sub < 4, b, a)
-
-    def blow(total, k, result):
-        weight = weights[1, pl.ds(k, 1)]
-        return [a + weight * b for a, b in zip(total, result)]
-
-    def first_wind(k, carry):
-        return blow(carry, k, [air_a[f, layer_at(k, part)] for f in (2, 3) for part in (1, 2)])
-
-    calm = [nothing] * 4
-    wind = unrolled(0, LEVELS, UNROLL_AIR, first_wind, calm)
-
-    spread = air_delta * diffusion
-    mixing = [jnp.where(mask, spread, 0.0) for mask in inside]
-    lifting = [jnp.where(mask, 0.5 * lift_gain * air_delta, 0.0) for mask in inside]
-    lifting = [(value, 0.6 * value) for value in lifting]
-    state, other = air_a, air_b
-    for c in range(STEPS):
+    def couple(c, wind, chain, fuel_from, fuel_to):
         reach = EDGE - REFINE * (c + 1)
         fire_step = tables_ref[4, c]
 
@@ -410,8 +408,8 @@
                     for row in range(REFINE):
                         held[j, pl.ds(half * (span // 2) + row, 8, stride=REFINE)] = value
 
-        before, after = lev_a, lev_b
         for s in range(SUBSTEPS):
+            before, after = chain[s], chain[s + 1]
 
             def advance(t, carry, c=c, s=s, fire_step=fire_step, before=before, after=after):
                 row = pl.multiple_of(PAD + 8 * t, 8)
@@ -447,10 +445,10 @@
                     if s < SUBSTEPS - 1:
                         burnt[j, flat] = unburnt
                     else:
-                        held = fuel[j, at]
+                        held = fuel_from[j, at]
                         remain = held * jnp.exp((0.5 * SUBSTEPS - unburnt) * (fire_step * value_at(1, j, t)))
                         spent = held - remain
-                        fuel[j, at] = remain
+                        fuel_to[j, at] = remain
                         energy[j, flat] = spent * value_at(2, j, t)
                         vapour[j, flat] = spent * value_at(3, j, t)
                 if s == SUBSTEPS - 1 and c < STEPS - 1:
@@ -461,7 +459,6 @@
 
             unrolled(*strips(reach + SUBSTEPS - 1 - s), UNROLL_FIRE, advance, 0)
             mend_rows(after)
-            before, after = after, before
 
         totals = []
         for held in (energy, vapour):
@@ -480,6 +477,158 @@
             halo, inner = swap(second, first)
             scale = air_delta * gain / (REFINE * REFINE)
             forcing.append([jnp.where(mask, value * scale, 0.0) for mask, value in zip(inside, (inner, halo))])
+        return forcing
+
+    return couple, kindled, mend_lanes, mend_rows
+
+
+def first_kernel(bands, tables_ref, level_in, fuel_in, ignite_in, next_ref, prev_ref, wind_own, *refs):
+    fire_up, fire_down = refs[:2]
+    sides, refs = refs[2 : bands + 2], refs[bands + 2 :]
+    values_in = refs[:4]
+    level_out, fuel, ignite, flux_out = refs[4:8]
+    values_side = refs[8:12]
+    lev_a, lev_b = refs[12:14]
+    scratch = refs[14:]
+    rows, width = level_in.shape
+    tiles = width // LANES
+    own = PAD + EDGE
+    span = rows + 2 * EDGE
+    sub = iota((8, LANES), 0)
+
+    corners = corner_tiles(next_ref, prev_ref, air_tiles(LEVELS // bands), rows)
+    at = pl.ds(2, HALO_ROWS // 8)
+    left, right = (ref[at].reshape(HALO_ROWS, LANES) for ref in (sides[1], sides[bands - 1]))
+    wide = iota((HALO_ROWS, LANES), 1)
+    upper_side = jnp.where(wide < 64, right, left)
+    lower_side = roll(jnp.where(wide < 64, left, right), 64, 1)
+    for a, (source, held) in enumerate(((level_in, lev_a), (fuel_in, fuel), (None, None), (ignite_in, ignite))):
+        upper, lower = halo_unpack(upper_side, a, True), halo_unpack(lower_side, a, False)
+        if held is None:
+            side = jnp.concatenate([upper, corners[a], lower], axis=0).astype(jnp.int32)
+            vectors = table_vectors(tables_ref)
+            for n in range(span // 8):
+                for vector, out in zip(vectors, values_side):
+                    out[8 * n : 8 * n + 8] = pick(vector, side[8 * n : 8 * n + 8])
+            continue
+        for j in range(tiles):
+            held[j, PAD:own] = halo_unpack(fire_up[j], a, True)
+            held[j, own : own + rows] = source[:, j * LANES : (j + 1) * LANES].astype(jnp.float32)
+            held[j, own + rows : own + rows + EDGE] = halo_unpack(fire_down[j], a, False)
+        held[tiles, PAD:own] = upper
+        held[tiles, own : own + rows] = corners[a]
+        held[tiles, own + rows : own + rows + EDGE] = lower
+    spare = jnp.zeros((tiles + 1, PAD, LANES), jnp.float32)
+    for held in (lev_a, lev_b):
+        held[:, :PAD] = spare
+        held[:, PAD + span :] = spare
+
+    couple, kindled, mend_lanes, mend_rows = fire_steps(
+        bands, tables_ref, tiles, rows, ignite, values_in, values_side, scratch
+    )
+
+    def kindle(t, carry):
+        values = mend_lanes(kindled([lev_a[j, strip(t)] for j in range(tiles + 1)], t, 0))
+        for j, value in enumerate(values):
+            lev_a[j, strip(t)] = value
+        return carry
+
+    unrolled(0, span // 8, UNROLL_LOOKUP, kindle, 0)
+    mend_rows(lev_a)
+
+
+    inside = slab_masks(bands)[4]
+    above, below = (sum(ref[n] for ref in sides) for n in range(2))
+    halo_u = jnp.where(sub < 4, below, roll(above, 4, 0))
+    halo_v = jnp.where(sub < 4, roll(below, 4, 0), above)
+    wind = []
+    for value, halo in ((wind_own[0], halo_u), (wind_own[1], halo_v)):
+        wind += [jnp.where(inside[0], value, 0.0), jnp.where(inside[1], halo, 0.0)]
+    forcing = couple(0, wind, (lev_a, lev_b, lev_a, lev_b, level_out), fuel, fuel)
+    for n in range(2):
+        for part in range(2):
+            flux_out[2 * n + part] = forcing[n][part]
+
+
+def main_kernel(bands, tables_ref, level_in, fuel_in, ignite, flux_in, *refs):
+    slots = refs[:bands]
+    edge_up, edge_down = refs[bands : bands + 2]
+    values_in = refs[bands + 2 : bands + 6]
+    values_side = refs[bands + 6 : bands + 10]
+    level_out, fuel_out = refs[bands + 10 : bands + 12]
+    outs = refs[bands + 12 : 2 * bands + 12]
+    scratch = refs[2 * bands + 12 :]
+    lev_a, lev_b, fuel = scratch[:3]
+    air_a, air_b, weights = scratch[9:12]
+    rows, width = level_out.shape
+    tiles = width // LANES
+    depth = LEVELS // bands
+    count = air_tiles(depth)
+    own = PAD + EDGE
+    lane = iota((8, LANES), 1)
+    band = band_index()
+    couple = fire_steps(bands, tables_ref, tiles, rows, ignite, values_in, values_side, scratch[3:9])[0]
+
+    sub = iota((8, LANES), 0)
+    inside = slab_masks(bands)[4]
+
+    def layer_at(k, part, shift=0):
+        return pl.ds(pl.multiple_of((k + 1) * 24 + 8 * part, 8) + shift, 8)
+
+    def put(held, f, k, part, value):
+        held[f, layer_at(k, part)] = value
+        if part == 2:
+            held[f, layer_at(k, 0)] = value
+
+    for k in range(bands):
+        source = lax.rem(band - k + bands, bands)
+        half = k // 2
+
+        def whole(i, k=k, half=half):
+            below, above = edge_down[half * count + i], edge_up[half * count + i]
+            if k % 2 == 0:
+                halo = jnp.where(sub < 4, below, roll(above, 4, 0))
+            else:
+                halo = jnp.where(sub < 4, roll(below, 4, 0), above)
+            return slots[k][i], halo
+
+        for g in range(-(-depth // 3)):
+            edges = whole(2 * depth + g)
+            for l in range(3 * g, min(3 * g + 3, depth)):
+                for p in range(2):
+                    both = whole(2 * l + p)
+                    for f in range(2):
+                        j = (l - 3 * g) * 4 + 2 * p + f
+                        for part in range(2):
+                            inner = both[part] if f == 0 else roll(both[part], 64, 1)
+                            value = jnp.where(lane < 64, inner, roll(edges[part], 64 - 4 * j, 1))
+                            value = jnp.where(inside[part], value, 0.0)
+                            put(air_a, 2 * p + f, source * depth + l, part + 1, value)
+    nothing = jnp.zeros((8, LANES), jnp.float32)
+    for held in (air_a, air_b):
+        for f in range(4):
+            for part in range(3):
+                held[f, layer_at(-1, part)] = nothing
+                held[f, layer_at(LEVELS, part)] = nothing
+
+    weights[0] = level_weights(2.0, float(LEVELS))
+    weights[1] = level_weights(1.0, 1.0)
+    def blow(total, k, result):
+        weight = weights[1, pl.ds(k, 1)]
+        return [a + weight * b for a, b in zip(total, result)]
+
+    calm = [nothing] * 4
+    spread = air_delta * diffusion
+    mixing = [jnp.where(mask, spread, 0.0) for mask in inside]
+    lifting = [jnp.where(mask, 0.5 * lift_gain * air_delta, 0.0) for mask in inside]
+    lifting = [(value, 0.6 * value) for value in lifting]
+    state, other = air_a, air_b
+    for c in range(STEPS):
+        if c == 0:
+            forcing = [[flux_in[2 * n + part] for part in range(2)] for n in range(2)]
+        else:
+            chain = (level_in if c == 1 else lev_a, lev_b, lev_a, lev_b, lev_a)
+            forcing = couple(c, wind, chain, fuel_in if c == 1 else fuel, fuel)
 
         def air_step(k, part, height, state=state, forcing=forcing):
             at = layer_at(k, part + 1)
@@ -594,13 +743,15 @@
     sizes = [count + (extra if k in (1, bands - 1) else 0) for k in range(bands)]
     packed = pl.pallas_call(
         functools.partial(pack_kernel, bands),
-        out_shape=[shape(size, 8, LANES) for size in sizes[1:]] + [shape(4, tiles, EDGE, LANES)] * 2,
+        out_shape=[shape(size, 8, LANES) for size in sizes[1:]] + [shape(tiles, SENT_ROWS, LANES)] * 2,
         in_specs=[pl.BlockSpec(memory_space=pltpu.HBM)] * 5,
-        out_specs=[vmem()] * (bands + 1),
+        out_specs=[pl.BlockSpec(memory_space=pltpu.HBM)] * (bands + 1),
         scratch_shapes=[
             pltpu.VMEM(x.shape, x.dtype) for x in (air_state, fire_level, fuel_left, fuel_class, ignition)
         ]
-        + [pltpu.SemaphoreType.DMA((5,))],
+        + [pltpu.VMEM((size, 8, LANES), jnp.float32) for size in sizes[1:]]
+        + [pltpu.VMEM((tiles, SENT_ROWS, LANES), jnp.float32)] * 2
+        + [pltpu.SemaphoreType.DMA((bands + 8,)), pltpu.VMEM((LEVELS, LANES), jnp.float32)],
         compiler_params=pltpu.CompilerParams(vmem_limit_bytes=PACK_LIMIT),
         name="pack",
     )(air_state, fire_level, fuel_left, fuel_class, ignition)
@@ -627,18 +778,30 @@
     fire_up = lax.ppermute(down, "tile", rise)
     fire_down = lax.ppermute(up, "tile", sink)
     slots = turn([kept, *slots])
-    edges = (bands // 2) * count + 4 * (EDGE // 8)
-    up, down = pl.pallas_call(
+    edges = (bands // 2) * count
+    up, down, wind = pl.pallas_call(
         functools.partial(relay_kernel, bands, rows),
-        out_shape=[shape(edges, 8, LANES)] * 2,
+        out_shape=[shape(edges, 8, LANES)] * 2 + [shape(2, 8, LANES)],
         in_specs=[vmem()] * bands,
-        out_specs=[vmem()] * 2,
+        out_specs=[vmem()] * 3,
+        scratch_shapes=[pltpu.VMEM((LEVELS, LANES), jnp.float32)],
         compiler_params=params,
         cost_estimate=pl.CostEstimate(flops=RELAY_FLOPS, bytes_accessed=0, transcendentals=0),
         name="relay",
     )(*slots)
     edge_up = lax.ppermute(down, "tile", rise)
     edge_down = lax.ppermute(up, "tile", sink)
+    sides = pl.pallas_call(
+        functools.partial(corner_kernel, bands, air_state.shape[3] // LANES),
+        out_shape=[
+            shape(2 + (HALO_ROWS // 8 if k in (1, bands - 1) else 0), 8, LANES) for k in range(bands)
+        ],
+        in_specs=[vmem()] * 2,
+        out_specs=[vmem()] * bands,
+        compiler_params=params,
+        name="corners",
+    )(fire_up, fire_down)
+    sides = turn(sides)
 
     span = rows + 2 * EDGE
     values = pl.pallas_call(
@@ -650,29 +813,51 @@
         cost_estimate=pl.CostEstimate(flops=SURVEY_FLOPS, bytes_accessed=0, transcendentals=0),
         name="survey",
     )(tables, fuel_class, fire_up, fire_down)
-    fire = pltpu.VMEM((tiles + 1, span + 2 * PAD, LANES), jnp.float32)
+    padded = (tiles + 1, span + 2 * PAD, LANES)
+    fire = pltpu.VMEM(padded, jnp.float32)
     flat = pltpu.VMEM((tiles + 1, span, LANES), jnp.float32)
-    side = pltpu.VMEM((span, LANES), jnp.float32)
     atmosphere = pltpu.VMEM((4, (LEVELS + 2) * 24, LANES), jnp.float32)
-    results = pl.pallas_call(
-        functools.partial(main_kernel, bands),
-        out_shape=[shape(rows, width)] * 2 + [shape(2 * depth, 8, LANES)] * bands,
-        in_specs=[smem()] + [vmem()] * (3 + bands + 8),
-        out_specs=[vmem()] * (2 + bands),
-        scratch_shapes=[fire] * 4 + [flat] * 6 + [atmosphere] * 2 + [side] * 4 + [pltpu.VMEM((2, LEVELS, LANES), jnp.float32)],
+    level, fuel, ignite, flux, *values_side = pl.pallas_call(
+        functools.partial(first_kernel, bands),
+        out_shape=[shape(*padded)] * 3 + [shape(4, 8, LANES)] + [shape(span, LANES)] * 4,
+        in_specs=[smem()] + [vmem()] * (12 + bands),
+        out_specs=[vmem()] * 8,
+        scratch_shapes=[fire] * 2 + [flat] * 6,
         compiler_params=params,
-        name="window",
+        cost_estimate=pl.CostEstimate(flops=FIRST_FLOPS, bytes_accessed=0, transcendentals=0),
+        name="first",
     )(
         tables,
         fire_level,
         fuel_left,
         ignition,
-        *slots,
+        slots[bands - 1],
+        slots[1],
+        wind,
         fire_up,
         fire_down,
+        *sides,
+        *values,
+    )
+    results = pl.pallas_call(
+        functools.partial(main_kernel, bands),
+        out_shape=[shape(rows, width)] * 2 + [shape(2 * depth, 8, LANES)] * bands,
+        in_specs=[smem()] + [vmem()] * (4 + bands + 10),
+        out_specs=[vmem()] * (2 + bands),
+        scratch_shapes=[fire] * 3 + [flat] * 6 + [atmosphere] * 2 + [pltpu.VMEM((2, LEVELS, LANES), jnp.float32)],
+        compiler_params=params,
+        name="window",
+    )(
+        tables,
+        level,
+        fuel,
+        ignite,
+        flux,
+        *slots,
         edge_up,
         edge_down,
         *values,
+        *values_side,
     )
     level_out, fuel_out = results[:2]
     slabs = turn(results[2:])

time: 70.2 us -> 63.9 us (0.910)
  waiting for transfers between devices: 23.6 us -> 14.7 us
  starting transfers between devices: 15.3 us -> 17 us
  Pallas kernels: 29.6 us -> 30.4 us
    ppermute x1, waiting for transfers between devices: 7.42 us -> 0.01 us  [local(): edge_up = lax.ppermute(down, 'tile', rise)]
    pallas_call x0 -> x2, Pallas kernels: none -> 5.21 us  [the longest x1 5.05 us: local(): pl.pallas_call(functools.partial(first_kernel, bands), out_shape=[shape(*...]
    pallas_call x1, Pallas kernels: 22.8 us -> 18.6 us  [local(): pl.pallas_call(functools.partial(main_kernel, bands), out_shape=[shape(ro...]
    ppermute x1, waiting for transfers between devices: 4.06 us -> 0.01 us  [local(): edge_down = lax.ppermute(up, 'tile', sink)]
    ppermute x6 -> x9, waiting for transfers between devices: 12.1 us -> 14.6 us  [turn(): lax.ppermute(values[k], BANDS, [(i, (i + k) % bands) for i in range(bands)])]
    ppermute x6 -> x9, starting transfers between devices: 5.28 us -> 7.69 us  [turn(): lax.ppermute(values[k], BANDS, [(i, (i + k) % bands) for i in range(bands)])]
  transfers between devices with their start and end apart: 10 -> 13, of which waited for: 7 -> 6; matrix products, arithmetic and copies ran while one was open for 0% -> 0% of each run, Pallas kernels for 3% -> 11%
where the time goes in v4:
time: 63.9 us; the launch traced here: 63.7 us
  Pallas kernels  30.4 us (48%)
  starting transfers between devices  17 us (27%)
  waiting for transfers between devices  14.7 us (23%)
  between operations  0.85 us (1%)
  local copies, waits for them, and re-layouts  0.71 us (1%)
    pallas_call x1, Pallas kernels, local(): pl.pallas_call(functools.partial(main_kernel, bands), out_shape=[shape(ro...  18.6 us
    ppermute x9, waiting for transfers between devices, turn(): lax.ppermute(values[k], BANDS, [(i, (i + k) % bands) for i in range(bands)])  14.6 us
    ppermute x9, starting transfers between devices, turn(): lax.ppermute(values[k], BANDS, [(i, (i + k) % bands) for i in range(bands)])  7.69 us
    pallas_call x1, Pallas kernels, local(): pl.pallas_call(functools.partial(first_kernel, bands), out_shape=[shape(*...  5.05 us
    ppermute x1, starting transfers between devices, local(): edge_up = lax.ppermute(down, 'tile', rise)  3.47 us
    ppermute x1, starting transfers between devices, local(): fire_up = lax.ppermute(down, 'tile', rise)  3.21 us
    pallas_call x1, Pallas kernels, local(): pl.pallas_call(functools.partial(pack_kernel, bands), out_shape=[shape(si...  2.84 us
    pallas_call x1, Pallas kernels, local(): pl.pallas_call(functools.partial(unpack_kernel, bands), out_shape=shape(*...  1.72 us
  transfers between devices with their start and end apart: 13, of which 6 were waited for; matrix products, arithmetic and copies ran while one was open for 0% of the time, Pallas kernels for 11%

profile of v4, /device:TPU:1, one launch (start us, length us, event | category | flops | bytes accessed | tf_op | source)
XLA Modules:
  0.0 63.7 jit_solution(15550586593027942980)
XLA Ops:
  0.6 2.8 %pack.1 = (f32[67,8,128]{2,1,0:T(8,128)}, f32[47,8,128]{2,1,0:T(8,128)}, f32[67,8,128]{2,1,0:T(8,128)}, f32[5,144,128]{2,1,0:T(8,128)}, f32[5,144,128]{2,1,0:T(8,128)}) custom-call(f32[4,20,8,256]{3,2,1,0:T(8,128)} %air_ref.1, f32[80,640]{1,0:T(8,128)} %level_in.1, f32[80,640]{1,0:T(8,128)} %fuel_in.1, s32[80,640]{1,0:T(8,128)} %class_ref.1, s32[80,640]{1,0:T(8,128)} %ignite_in.1), custom_call_target="tpu_custom_call" | custom-call | tf_op jit(solution)/shard_map/pack/pallas_call | solution.py:744
  3.5 2.1 %collective-permute-start.2 = (f32[47,8,128]{2,1,0:T(8,128)}, f32[47,8,128]{2,1,0:T(8,128)S(1)}, u32[]{:S(2)}, u32[]{:S(2)}) collective-permute-start(f32[47,8,128]{2,1,0:T(8,128)} %get-tuple-element.35), channel_id=1, source_target_pairs={{0,2},{1,3},{2,0},{3,1},{4,6},{5,7},{6,4},{7,5},{8,10},{9,11},{10,... | collective-permute-start | bytes 577544 | tf_op jit(solution)/shard_map/ppermute | solution.py:775
  5.6 1.0 %collective-permute-start = (f32[67,8,128]{2,1,0:T(8,128)}, f32[67,8,128]{2,1,0:T(8,128)S(1)}, u32[]{:S(2)}, u32[]{:S(2)}) collective-permute-start(f32[67,8,128]{2,1,0:T(8,128)} %get-tuple-element.33), channel_id=1, source_target_pairs={{0,3},{1,0},{2,1},{3,2},{4,7},{5,4},{6,5},{7,6},{8,11},{9,8},{10,9... | collective-permute-start | bytes 823304 | tf_op jit(solution)/shard_map/ppermute | solution.py:775
  6.6 0.8 %collective-permute-start.1 = (f32[67,8,128]{2,1,0:T(8,128)}, f32[67,8,128]{2,1,0:T(8,128)S(1)}, u32[]{:S(2)}, u32[]{:S(2)}) collective-permute-start(f32[67,8,128]{2,1,0:T(8,128)} %get-tuple-element.34), channel_id=1, source_target_pairs={{0,1},{1,2},{2,3},{3,0},{4,5},{5,6},{6,7},{7,4},{8,9},{9,10},{10,1... | collective-permute-start | bytes 823304 | tf_op jit(solution)/shard_map/ppermute | solution.py:775
  7.3 3.2 %collective-permute-start.3 = (f32[5,144,128]{2,1,0:T(8,128)}, f32[5,144,128]{2,1,0:T(8,128)S(1)}, u32[]{:S(2)}, u32[]{:S(2)}) collective-permute-start(f32[5,144,128]{2,1,0:T(8,128)} %get-tuple-element.37), channel_id=1, source_target_pairs={{0,4},{4,8},{8,12},{1,5},{5,9},{9,13},{2,6},{6,10},{10,14},{3,7},{... | collective-permute-start | bytes 1105928 | tf_op jit(solution)/shard_map/ppermute | solution.py:778
  10.6 0.0 copy-start.9
  10.6 1.3 %collective-permute-start.4 = (f32[5,144,128]{2,1,0:T(8,128)}, f32[5,144,128]{2,1,0:T(8,128)S(1)}, u32[]{:S(2)}, u32[]{:S(2)}) collective-permute-start(f32[5,144,128]{2,1,0:T(8,128)} %get-tuple-element.38), channel_id=1, source_target_pairs={{4,0},{8,4},{12,8},{5,1},{9,5},{13,9},{6,2},{10,6},{14,10},{7,3},{... | collective-permute-start | bytes 1105928 | tf_op jit(solution)/shard_map/ppermute | solution.py:779
  11.9 0.3 keep.1.refs_0_
  12.2 4.9 %collective-permute-done.refs_3_.next_ref = f32[67,8,128]{2,1,0:T(8,128)S(1)} collective-permute-done((f32[67,8,128]{2,1,0:T(8,128)}, f32[67,8,128]{2,1,0:T(8,128)S(1)}, u32[]{:S(2)}, u32[]{:S(2)}) %collective-permute-start) | collective-permute-done | bytes 274464 | tf_op jit(solution)/shard_map/ppermute | solution.py:775
  17.1 0.2 relay.1
  17.3 3.5 %collective-permute-start.8 = (f32[94,8,128]{2,1,0:T(8,128)S(1)}, f32[94,8,128]{2,1,0:T(8,128)S(1)}, u32[]{:S(2)}, u32[]{:S(2)}) collective-permute-start(f32[94,8,128]{2,1,0:T(8,128)S(1)} %get-tuple-element.51), channel_id=1, source_target_pairs={{0,4},{4,8},{8,12},{1,5},{5,9},{9,13},{2,6},{6,10},{10,14},{3,7},{... | collective-permute-start | bytes 1155080 | tf_op jit(solution)/shard_map/ppermute | solution.py:792
  20.8 1.3 %collective-permute-start.9 = (f32[94,8,128]{2,1,0:T(8,128)S(1)}, f32[94,8,128]{2,1,0:T(8,128)S(1)}, u32[]{:S(2)}, u32[]{:S(2)}) collective-permute-start(f32[94,8,128]{2,1,0:T(8,128)S(1)} %get-tuple-element.52), channel_id=1, source_target_pairs={{4,0},{8,4},{12,8},{5,1},{9,5},{13,9},{6,2},{10,6},{14,10},{7,3},{... | collective-permute-start | bytes 1155080 | tf_op jit(solution)/shard_map/ppermute | solution.py:793
  22.1 0.0 copy-start.6
  22.1 0.0 copy-start.7
  22.1 0.6 copy-done.5
  22.7 0.0 copy-done.6
  22.7 0.0 copy-done.7
  22.8 0.1 collective-permute-done.4.down_ref.refs_1_
  22.9 0.2 corners.1
  23.1 1.2 %collective-permute-start.6 = (f32[2,8,128]{2,1,0:T(8,128)S(1)}, f32[2,8,128]{2,1,0:T(8,128)S(1)}, u32[]{:S(2)}, u32[]{:S(2)}) collective-permute-start(f32[2,8,128]{2,1,0:T(8,128)S(1)} %get-tuple-element.41), channel_id=1, source_target_pairs={{0,2},{1,3},{2,0},{3,1},{4,6},{5,7},{6,4},{7,5},{8,10},{9,11},{10,... | collective-permute-start | bytes 24584 | tf_op jit(solution)/shard_map/ppermute | solution.py:775
  24.3 1.3 %collective-permute-start.5 = (f32[19,8,128]{2,1,0:T(8,128)S(1)}, f32[19,8,128]{2,1,0:T(8,128)S(1)}, u32[]{:S(2)}, u32[]{:S(2)}) collective-permute-start(f32[19,8,128]{2,1,0:T(8,128)S(1)} %get-tuple-element.40), channel_id=1, source_target_pairs={{0,1},{1,2},{2,3},{3,0},{4,5},{5,6},{6,7},{7,4},{8,9},{9,10},{10,1... | collective-permute-start | bytes 233480 | tf_op jit(solution)/shard_map/ppermute | solution.py:775
  25.6 1.5 %survey.1 = (f32[5,160,128]{2,1,0:T(8,128)S(1)}, f32[5,160,128]{2,1,0:T(8,128)S(1)}, f32[5,160,128]{2,1,0:T(8,128)S(1)}, f32[5,160,128]{2,1,0:T(8,128)S(1)}) custom-call(f32[5,13]{1,0:T(8,128)S(1)} %stack.23.tables_ref, s32[80,640]{1,0:T(8,128)S(1)} %copy-done.1, f32[5,144,128]{2,1,0:T(8,128)S(1)} %collective-permute-done.3.up_ref.refs_0_, ...), custom_call_target="tpu_custom_call" | custom-call | flops 1000000000 | tf_op jit(solution)/shard_map/survey/pallas_call | solution.py:807
  27.1 2.5 %collective-permute-done.7.refs_5_ = f32[19,8,128]{2,1,0:T(8,128)S(1)} collective-permute-done((f32[19,8,128]{2,1,0:T(8,128)S(1)}, f32[19,8,128]{2,1,0:T(8,128)S(1)}, u32[]{:S(2)}, u32[]{:S(2)}) %collective-permute-start.7) | collective-permute-done | bytes 77856 | tf_op jit(solution)/shard_map/ppermute | solution.py:775
  29.7 5.1 %first.1 = (f32[6,176,128]{2,1,0:T(8,128)S(1)}, f32[6,176,128]{2,1,0:T(8,128)S(1)}, f32[6,176,128]{2,1,0:T(8,128)S(1)}, f32[4,8,128]{2,1,0:T(8,128)S(1)}, f32[16...) custom-call(f32[5,13]{1,0:T(8,128)S(1)} %stack.23.tables_ref, ...), custom_call_target="tpu_custom_call" | custom-call | flops 3000000000 | tf_op jit(solution)/shard_map/first/pallas_call | solution.py:820
  34.8 18.6 %window.1 = (f32[80,640]{1,0:T(8,128)}, f32[80,640]{1,0:T(8,128)}, f32[40,8,128]{2,1,0:T(8,128)S(1)}, f32[40,8,128]{2,1,0:T(8,128)S(1)}, f32[40,8,128]{2,1,0:T(8,128)S(1)}, /*index=5*/f32[40,8,128]{2,1,0:T(8,128)S(1)}) custom-call(f32[5,13]{1,0:T(8,128)S(1)} %stack.23.tables_ref, f32[6,176,128]{2,1,0:T(8,128)S(1)} %get-tuple-element.47.level_in, ...), custom_call_target="tpu_custom_call" | custom-call | tf_op jit(solution)/shard_map/window/pallas_call | solution.py:842
  53.4 0.3 collective-permute-start.10
  53.6 0.3 collective-permute-start.11
  54.0 0.8 %collective-permute-start.12 = (f32[40,8,128]{2,1,0:T(8,128)S(1)}, f32[40,8,128]{2,1,0:T(8,128)S(1)}, u32[]{:S(2)}, u32[]{:S(2)}) collective-permute-start(f32[40,8,128]{2,1,0:T(8,128)S(1)} %get-tuple-element.60), channel_id=1, source_target_pairs={{0,3},{1,0},{2,1},{3,2},{4,7},{5,4},{6,5},{7,6},{8,11},{9,8},{10,9... | collective-permute-start | bytes 491528 | tf_op jit(solution)/shard_map/ppermute | solution.py:775
  54.7 1.6 %collective-permute-done.10.refs_1_ = f32[40,8,128]{2,1,0:T(8,128)S(1)} collective-permute-done((f32[40,8,128]{2,1,0:T(8,128)S(1)}, f32[40,8,128]{2,1,0:T(8,128)S(1)}, u32[]{:S(2)}, u32[]{:S(2)}) %collective-permute-start.10) | collective-permute-done | bytes 163872 | tf_op jit(solution)/shard_map/ppermute | solution.py:775
  56.4 3.9 %collective-permute-done.11.refs_2_ = f32[40,8,128]{2,1,0:T(8,128)S(1)} collective-permute-done((f32[40,8,128]{2,1,0:T(8,128)S(1)}, f32[40,8,128]{2,1,0:T(8,128)S(1)}, u32[]{:S(2)}, u32[]{:S(2)}) %collective-permute-start.11) | collective-permute-done | bytes 163872 | tf_op jit(solution)/shard_map/ppermute | solution.py:775
  60.3 1.6 %collective-permute-done.12.refs_3_ = f32[40,8,128]{2,1,0:T(8,128)S(1)} collective-permute-done((f32[40,8,128]{2,1,0:T(8,128)S(1)}, f32[40,8,128]{2,1,0:T(8,128)S(1)}, u32[]{:S(2)}, u32[]{:S(2)}) %collective-permute-start.12) | collective-permute-done | bytes 163872 | tf_op jit(solution)/shard_map/ppermute | solution.py:775
  61.9 1.7 %unpack.1 = f32[4,20,8,256]{3,2,1,0:T(8,128)} custom-call(f32[40,8,128]{2,1,0:T(8,128)S(1)} %get-tuple-element.57.refs_0_, f32[40,8,128]{2,1,0:T(8,128)S(1)} %collective-permute-done.10.refs_1_, f32[40,8,128]{2,1,0:T(8,128)S(1)} %collective-permute-done.11.refs_2_, f32[40,8,128]{2,1,0:T(8,128)S(1)} %collective-permute-done.12.refs_3_), custom_call_target="tpu_custom_call" | custom-call | tf_op jit(solution)/shard_map/unpack/pallas_call | solution.py:864
  (25 shorter events, 0.1 us)
Async XLA Ops:
  0.6 11.2 %copy-start = (f32[4,20,8,256]{3,2,1,0:T(8,128)S(1)}, f32[4,20,8,256]{3,2,1,0:T(8,128)}, u32[]{:S(2)}) copy-start(f32[4,20,8,256]{3,2,1,0:T(8,128)} %air_ref.1) | copy-start | bytes 1966084
  3.5 8.7 %collective-permute-start.2 = (f32[47,8,128]{2,1,0:T(8,128)}, f32[47,8,128]{2,1,0:T(8,128)S(1)}, u32[]{:S(2)}, u32[]{:S(2)}) collective-permute-start(f32[47,8,128]{2,1,0:T(8,128)} %get-tuple-element.35), channel_id=1, source_target_pairs={{0,2},{1,3},{2,0},{3,1},{4,6},{5,7},{6,4},{7,5},{8,10},{9,11},{10,... | collective-permute-start | bytes 577544 | tf_op jit(solution)/shard_map/ppermute | solution.py:775
  5.6 11.5 %collective-permute-start = (f32[67,8,128]{2,1,0:T(8,128)}, f32[67,8,128]{2,1,0:T(8,128)S(1)}, u32[]{:S(2)}, u32[]{:S(2)}) collective-permute-start(f32[67,8,128]{2,1,0:T(8,128)} %get-tuple-element.33), channel_id=1, source_target_pairs={{0,3},{1,0},{2,1},{3,2},{4,7},{5,4},{6,5},{7,6},{8,11},{9,8},{10,9... | collective-permute-start | bytes 823304 | tf_op jit(solution)/shard_map/ppermute | solution.py:775
  6.6 10.5 %collective-permute-start.1 = (f32[67,8,128]{2,1,0:T(8,128)}, f32[67,8,128]{2,1,0:T(8,128)S(1)}, u32[]{:S(2)}, u32[]{:S(2)}) collective-permute-start(f32[67,8,128]{2,1,0:T(8,128)} %get-tuple-element.34), channel_id=1, source_target_pairs={{0,1},{1,2},{2,3},{3,0},{4,5},{5,6},{6,7},{7,4},{8,9},{9,10},{10,1... | collective-permute-start | bytes 823304 | tf_op jit(solution)/shard_map/ppermute | solution.py:775
  7.3 15.5 %collective-permute-start.3 = (f32[5,144,128]{2,1,0:T(8,128)}, f32[5,144,128]{2,1,0:T(8,128)S(1)}, u32[]{:S(2)}, u32[]{:S(2)}) collective-permute-start(f32[5,144,128]{2,1,0:T(8,128)} %get-tuple-element.37), channel_id=1, source_target_pairs={{0,4},{4,8},{8,12},{1,5},{5,9},{9,13},{2,6},{6,10},{10,14},{3,7},{... | collective-permute-start | bytes 1105928 | tf_op jit(solution)/shard_map/ppermute | solution.py:778
  10.6 1.6 %copy-start.9 = (s32[4]{0:T(128)S(1)}, s32[4]{0:T(128)}, u32[]{:S(2)}) copy-start(s32[4]{0:T(128)} %param.15) | copy-start | bytes 52
  10.6 12.3 %collective-permute-start.4 = (f32[5,144,128]{2,1,0:T(8,128)}, f32[5,144,128]{2,1,0:T(8,128)S(1)}, u32[]{:S(2)}, u32[]{:S(2)}) collective-permute-start(f32[5,144,128]{2,1,0:T(8,128)} %get-tuple-element.38), channel_id=1, source_target_pairs={{4,0},{8,4},{12,8},{5,1},{9,5},{13,9},{6,2},{10,6},{14,10},{7,3},{... | collective-permute-start | bytes 1105928 | tf_op jit(solution)/shard_map/ppermute | solution.py:779
  17.1 5.1 %copy-start.8 = (f32[13]{0:T(128)S(1)}, f32[13]{0:T(128)}, u32[]{:S(2)}) copy-start(f32[13]{0:T(128)} %param.19) | copy-start | bytes 160
  17.3 17.5 %collective-permute-start.8 = (f32[94,8,128]{2,1,0:T(8,128)S(1)}, f32[94,8,128]{2,1,0:T(8,128)S(1)}, u32[]{:S(2)}, u32[]{:S(2)}) collective-permute-start(f32[94,8,128]{2,1,0:T(8,128)S(1)} %get-tuple-element.51), channel_id=1, source_target_pairs={{0,4},{4,8},{8,12},{1,5},{5,9},{9,13},{2,6},{6,10},{10,14},{3,7},{... | collective-permute-start | bytes 1155080 | tf_op jit(solution)/shard_map/ppermute | solution.py:792
  20.8 14.0 %collective-permute-start.9 = (f32[94,8,128]{2,1,0:T(8,128)S(1)}, f32[94,8,128]{2,1,0:T(8,128)S(1)}, u32[]{:S(2)}, u32[]{:S(2)}) collective-permute-start(f32[94,8,128]{2,1,0:T(8,128)S(1)} %get-tuple-element.52), channel_id=1, source_target_pairs={{4,0},{8,4},{12,8},{5,1},{9,5},{13,9},{6,2},{10,6},{14,10},{7,3},{... | collective-permute-start | bytes 1155080 | tf_op jit(solution)/shard_map/ppermute | solution.py:793
  22.1 0.7 %copy-start.5 = (f32[13]{0:T(128)S(1)}, f32[13]{0:T(128)}, u32[]{:S(2)}) copy-start(f32[13]{0:T(128)} %param.16) | copy-start | bytes 160
  22.1 0.7 %copy-start.6 = (f32[13]{0:T(128)S(1)}, f32[13]{0:T(128)}, u32[]{:S(2)}) copy-start(f32[13]{0:T(128)} %param.17) | copy-start | bytes 160
  22.1 0.7 %copy-start.7 = (f32[13]{0:T(128)S(1)}, f32[13]{0:T(128)}, u32[]{:S(2)}) copy-start(f32[13]{0:T(128)} %param.18) | copy-start | bytes 160
  22.8 2.8 %copy-start.1 = (s32[80,640]{1,0:T(8,128)S(1)}, s32[80,640]{1,0:T(8,128)}, u32[]{:S(2)}) copy-start(s32[80,640]{1,0:T(8,128)} %class_ref.1) | copy-start | bytes 614404
  23.1 4.1 %collective-permute-start.6 = (f32[2,8,128]{2,1,0:T(8,128)S(1)}, f32[2,8,128]{2,1,0:T(8,128)S(1)}, u32[]{:S(2)}, u32[]{:S(2)}) collective-permute-start(f32[2,8,128]{2,1,0:T(8,128)S(1)} %get-tuple-element.41), channel_id=1, source_target_pairs={{0,2},{1,3},{2,0},{3,1},{4,6},{5,7},{6,4},{7,5},{8,10},{9,11},{10,... | collective-permute-start | bytes 24584 | tf_op jit(solution)/shard_map/ppermute | solution.py:775
  24.3 2.9 %collective-permute-start.5 = (f32[19,8,128]{2,1,0:T(8,128)S(1)}, f32[19,8,128]{2,1,0:T(8,128)S(1)}, u32[]{:S(2)}, u32[]{:S(2)}) collective-permute-start(f32[19,8,128]{2,1,0:T(8,128)S(1)} %get-tuple-element.40), channel_id=1, source_target_pairs={{0,1},{1,2},{2,3},{3,0},{4,5},{5,6},{6,7},{7,4},{8,9},{9,10},{10,1... | collective-permute-start | bytes 233480 | tf_op jit(solution)/shard_map/ppermute | solution.py:775
  25.5 4.1 %copy-start.2 = (f32[80,640]{1,0:T(8,128)S(1)}, f32[80,640]{1,0:T(8,128)}, u32[]{:S(2)}) copy-start(f32[80,640]{1,0:T(8,128)} %level_in.1) | copy-start | bytes 614404
  25.5 4.1 %copy-start.3 = (f32[80,640]{1,0:T(8,128)S(1)}, f32[80,640]{1,0:T(8,128)}, u32[]{:S(2)}) copy-start(f32[80,640]{1,0:T(8,128)} %fuel_in.1) | copy-start | bytes 614404
  25.5 4.1 %copy-start.4 = (s32[80,640]{1,0:T(8,128)S(1)}, s32[80,640]{1,0:T(8,128)}, u32[]{:S(2)}) copy-start(s32[80,640]{1,0:T(8,128)} %ignite_in.1) | copy-start | bytes 614404
  25.5 4.1 %collective-permute-start.7 = (f32[19,8,128]{2,1,0:T(8,128)S(1)}, f32[19,8,128]{2,1,0:T(8,128)S(1)}, u32[]{:S(2)}, u32[]{:S(2)}) collective-permute-start(f32[19,8,128]{2,1,0:T(8,128)S(1)} %get-tuple-element.42), channel_id=1, source_target_pairs={{0,3},{1,0},{2,1},{3,2},{4,7},{5,4},{6,5},{7,6},{8,11},{9,8},{10,9... | collective-permute-start | bytes 233480 | tf_op jit(solution)/shard_map/ppermute | solution.py:775
  53.4 3.0 %collective-permute-start.10 = (f32[40,8,128]{2,1,0:T(8,128)S(1)}, f32[40,8,128]{2,1,0:T(8,128)S(1)}, u32[]{:S(2)}, u32[]{:S(2)}) collective-permute-start(f32[40,8,128]{2,1,0:T(8,128)S(1)} %get-tuple-element.58), channel_id=1, source_target_pairs={{0,1},{1,2},{2,3},{3,0},{4,5},{5,6},{6,7},{7,4},{8,9},{9,10},{10,1... | collective-permute-start | bytes 491528 | tf_op jit(solution)/shard_map/ppermute | solution.py:775
  53.6 6.7 %collective-permute-start.11 = (f32[40,8,128]{2,1,0:T(8,128)S(1)}, f32[40,8,128]{2,1,0:T(8,128)S(1)}, u32[]{:S(2)}, u32[]{:S(2)}) collective-permute-start(f32[40,8,128]{2,1,0:T(8,128)S(1)} %get-tuple-element.59), channel_id=1, source_target_pairs={{0,2},{1,3},{2,0},{3,1},{4,6},{5,7},{6,4},{7,5},{8,10},{9,11},{10,... | collective-permute-start | bytes 491528 | tf_op jit(solution)/shard_map/ppermute | solution.py:775
  54.0 8.0 %collective-permute-start.12 = (f32[40,8,128]{2,1,0:T(8,128)S(1)}, f32[40,8,128]{2,1,0:T(8,128)S(1)}, u32[]{:S(2)}, u32[]{:S(2)}) collective-permute-start(f32[40,8,128]{2,1,0:T(8,128)S(1)} %get-tuple-element.60), channel_id=1, source_target_pairs={{0,3},{1,0},{2,1},{3,2},{4,7},{5,4},{6,5},{7,6},{8,11},{9,8},{10,9... | collective-permute-start | bytes 491528 | tf_op jit(solution)/shard_map/ppermute | solution.py:775

commit v5 on v4

--- a/solution.py
+++ b/solution.py
@@ -15,6 +15,7 @@
 NFUEL = 13
 
 LANES = 128
+vapour_lift = 0.6
 HALO = STEPS
 EDGE = HALO * REFINE
 BULK = 32
@@ -36,6 +37,7 @@
 UNROLL_AIR = 16
 UNROLL_FINAL = 10
 KEEP_FLOPS = 10**9
+UNPACK_FLOPS = 10**9
 RELAY_FLOPS = 5 * 10**9
 SURVEY_FLOPS = 10**9
 FIRST_FLOPS = 3 * 10**9
@@ -76,7 +78,7 @@
 
 
 def air_tiles(depth):
-    return 2 * depth + -(-depth // 3)
+    return 2 * depth + -(-depth // 4)
 
 
 def halo_pack(fields, above):
@@ -115,21 +117,27 @@
     turn = 64 * odd
     back = 64 - turn
     from_right = lane < 96 - turn
+    is_odd = jnp.full((8, LANES), odd, jnp.int32) == 1
     for l in range(depth):
         for p in range(2):
             first = air_ref[2 * p, l, :, pl.ds(own, LANES)]
             second = air_ref[2 * p + 1, l, :, pl.ds(own, LANES)]
-            slot[2 * l + p] = jnp.where(lane < 64, roll(first, turn, 1), roll(second, back, 1))
-    for g in range(-(-depth // 3)):
+            turned = roll(jnp.where(is_odd, first, second), 64, 1)
+            slot[2 * l + p] = jnp.where(
+                lane < 64, jnp.where(is_odd, turned, first), jnp.where(is_odd, second, turned)
+            )
+    for g in range(-(-depth // 4)):
         packed = jnp.zeros((8, LANES), jnp.float32)
-        for l in range(3 * g, min(3 * g + 3, depth)):
+        for l in range(4 * g, min(4 * g + 4, depth)):
             for f in range(4):
-                j = (l - 3 * g) * 4 + f
+                q = (l - 4 * g) * 2 + f // 2
+                at = (8 * q + 64 * (f % 2)) % LANES
                 edge = jnp.where(
                     from_right, air_ref[f, l, :, pl.ds(right, LANES)], air_ref[f, l, :, pl.ds(left, LANES)]
                 )
-                edge = roll(edge, 4 * j + back, 1)
-                here = ((lane >= 4 * j) & (lane < 4 * j + 4)) | ((lane >= 60 + 4 * j) & (lane < 64 + 4 * j))
+                edge = roll(edge, lax.rem(at + back, LANES), 1)
+                other = (at + 60) % LANES
+                here = ((lane >= at) & (lane < at + 4)) | ((lane >= other) & (lane < other + 4))
                 packed = jnp.where(here, edge, packed)
         slot[2 * depth + g] = packed
 
@@ -228,22 +236,20 @@
     weights[...] = level_weights(1.0, 1.0)
     inner = [jnp.zeros((8, LANES), jnp.float32)] * 2
     edges = jnp.zeros((8, LANES), jnp.float32)
+    level_of = ((lane + 4) & 63) >> 4
     for k in range(bands):
         first = lax.rem(band_index() - k + bands, bands) * depth
         for l in range(depth):
             inner[l % 2] = inner[l % 2] + weights[pl.ds(first + l, 1)] * slots[k][2 * l + 1]
-        for g in range(-(-depth // 3)):
-            parts = [weights[pl.ds(first + min(3 * g + n, depth - 1), 1)] for n in range(3)]
-            weight = jnp.where(
-                (lane < 16) | ((lane >= 60) & (lane < 76)),
-                parts[0],
-                jnp.where((lane < 32) | ((lane >= 76) & (lane < 92)), parts[1], parts[2]),
-            )
+        for g in range(-(-depth // 4)):
+            weight = weights[pl.ds(first + 4 * g, 1)]
+            for n in range(1, min(4, depth - 4 * g)):
+                weight = jnp.where(level_of == n, weights[pl.ds(first + 4 * g + n, 1)], weight)
             edges = edges + weight * slots[k][2 * depth + g]
     inner = inner[0] + inner[1]
-    for f in range(2):
-        halo = sum(roll(edges, 64 - 4 * (4 * n + 2 + f), 1) for n in range(3))
-        wind_ref[f] = jnp.where(lane < 64, inner if f == 0 else roll(inner, 64, 1), halo)
+    edges = sum(roll(edges, (64 - 8 * (2 * n + 1)) % LANES, 1) for n in range(4))
+    wind_ref[0] = jnp.where(lane < 64, inner, edges)
+    wind_ref[1] = roll(jnp.where(lane < 64, edges, inner), 64, 1)
 
 
 def corner_kernel(bands, lane_tiles, up_ref, down_ref, *outs):
@@ -431,13 +437,17 @@
                     square = (a * a + b * b) + (d * d + e * e)
                     steep = square * lax.rsqrt(jnp.maximum(square, 1.2e-38))
                     gx, gy = back + ahead, below + above
-                    tail = (wind_u[j, flat] * gx + wind_v[j, flat] * gy) * lax.rsqrt((gx * gx + 4.0) + gy * gy)
+                    blow_u, blow_v = wind_u[j, flat], wind_v[j, flat]
                     if s == 0:
                         speed = fire_step * value_at(0, j, t)
                         pace[j, flat] = speed
+                        blow_u, blow_v = blow_u * speed, blow_v * speed
+                        wind_u[j, flat] = blow_u
+                        wind_v[j, flat] = blow_v
                     else:
                         speed = pace[j, flat]
-                    result.append(here - (speed * (1.0 + jnp.maximum(tail, 0.0))) * steep)
+                    tail = (blow_u * gx + blow_v * gy) * lax.rsqrt((gx * gx + 4.0) + gy * gy)
+                    result.append(here - (speed + jnp.maximum(tail, 0.0)) * steep)
                 for j in range(tiles + 1):
                     unburnt = jnp.clip(result[j], -0.5, 0.5)
                     if s > 0:
@@ -472,7 +482,7 @@
                 totals.append(jnp.concatenate(total, axis=1))
         flux = dot(parts(jnp.concatenate(totals, axis=0), 1), to_columns)
         forcing = []
-        for n, gain in enumerate((heat_gain, vapour_gain)):
+        for n, gain in enumerate((heat_gain, vapour_lift * vapour_gain)):
             first, second = (flux[16 * n + 8 * half : 16 * n + 8 * half + 8] for half in range(2))
             halo, inner = swap(second, first)
             scale = air_delta * gain / (REFINE * REFINE)
@@ -592,16 +602,19 @@
                 halo = jnp.where(sub < 4, roll(below, 4, 0), above)
             return slots[k][i], halo
 
-        for g in range(-(-depth // 3)):
+        for g in range(-(-depth // 4)):
             edges = whole(2 * depth + g)
-            for l in range(3 * g, min(3 * g + 3, depth)):
+            for l in range(4 * g, min(4 * g + 4, depth)):
                 for p in range(2):
                     both = whole(2 * l + p)
-                    for f in range(2):
-                        j = (l - 3 * g) * 4 + 2 * p + f
-                        for part in range(2):
-                            inner = both[part] if f == 0 else roll(both[part], 64, 1)
-                            value = jnp.where(lane < 64, inner, roll(edges[part], 64 - 4 * j, 1))
+                    for part in range(2):
+                        edge = roll(edges[part], (64 - 8 * ((l - 4 * g) * 2 + p)) % LANES, 1)
+                        values = (
+                            jnp.where(lane < 64, both[part], edge),
+                            roll(jnp.where(lane < 64, edge, both[part]), 64, 1),
+                        )
+                        for f in range(2):
+                            value = values[f] * vapour_lift if 2 * p + f == 1 else values[f]
                             value = jnp.where(inside[part], value, 0.0)
                             put(air_a, 2 * p + f, source * depth + l, part + 1, value)
     nothing = jnp.zeros((8, LANES), jnp.float32)
@@ -621,7 +634,6 @@
     spread = air_delta * diffusion
     mixing = [jnp.where(mask, spread, 0.0) for mask in inside]
     lifting = [jnp.where(mask, 0.5 * lift_gain * air_delta, 0.0) for mask in inside]
-    lifting = [(value, 0.6 * value) for value in lifting]
     state, other = air_a, air_b
     for c in range(STEPS):
         if c == 0:
@@ -650,7 +662,7 @@
                     new = new + height * forcing[f][part]
                 else:
                     low, high = (west, east) if f == 2 else (south, north)
-                    new = new + (lifting[part][0] * (high[0] - low[0]) + lifting[part][1] * (high[1] - low[1]))
+                    new = new + lifting[part] * ((high[0] - low[0]) + (high[1] - low[1]))
                 result.append(new)
             return result
 
@@ -672,6 +684,7 @@
 
                 def final(l, carry, out=outs[k], first=first, air_step=air_step):
                     result = air_step(first + l, 0, weights[0, pl.ds(first + l, 1)])
+                    result[1] = result[1] * (1.0 / vapour_lift)
                     for p in range(2):
                         out[2 * l + p] = jnp.where(lane < 64, result[2 * p], roll(result[2 * p + 1], 64, 1))
                     return carry
@@ -683,23 +696,27 @@
         fuel_out[:, j * LANES : (j + 1) * LANES] = fuel[j, own : own + rows]
 
 
-def unpack_kernel(bands, *refs):
-    slots, out = refs[:bands], refs[bands]
+def unpack_kernel(bands, shifts, *refs):
+    out = refs[-1]
     depth = out.shape[1]
     lane = iota((8, LANES), 1)
-    for k in range(bands):
+    if len(refs) > len(shifts) + 1:
+        out[...] = refs[len(shifts)][...]
+    for k, held in zip(shifts, refs):
         source = lax.rem(band_index() - k + bands, bands)
         odd = lax.rem(source, 2)
         cols = pl.ds(pl.multiple_of((source // 2) * LANES, LANES), LANES)
         mine = (lane >= 64 * odd) & (lane < 64 * odd + 64)
 
-        def body(l, carry, slot=slots[k], odd=odd, cols=cols, mine=mine):
+        is_odd = jnp.full((8, LANES), odd, jnp.int32) == 1
+
+        def body(l, carry, slot=held, is_odd=is_odd, cols=cols, mine=mine):
             for p in range(2):
                 both = slot[2 * l + p]
-                for f in range(2):
-                    shift = 64 * odd if f == 0 else 64 - 64 * odd
+                turned = roll(both, 64, 1)
+                for f, value in enumerate((jnp.where(is_odd, turned, both), jnp.where(is_odd, both, turned))):
                     old = out[2 * p + f, l, :, cols]
-                    out[2 * p + f, l, :, cols] = jnp.where(mine, roll(both, shift, 1), old)
+                    out[2 * p + f, l, :, cols] = jnp.where(mine, value, old)
             return carry
 
         unrolled(0, depth, 10, body, 0)
@@ -861,14 +878,20 @@
     )
     level_out, fuel_out = results[:2]
     slabs = turn(results[2:])
-    air_out = pl.pallas_call(
-        functools.partial(unpack_kernel, bands),
-        out_shape=shape(*air_state.shape),
-        in_specs=[vmem()] * bands,
-        out_specs=vmem(),
-        compiler_params=params,
-        name="unpack",
-    )(*slabs)
+    air_out = []
+    for shifts in (range(2), range(2, bands)):
+        air_out = [
+            pl.pallas_call(
+                functools.partial(unpack_kernel, bands, shifts),
+                out_shape=shape(*air_state.shape),
+                in_specs=[vmem()] * (len(shifts) + len(air_out)),
+                out_specs=vmem(),
+                compiler_params=params,
+                cost_estimate=pl.CostEstimate(flops=UNPACK_FLOPS, bytes_accessed=0, transcendentals=0),
+                name=f"unpack_{shifts[0]}",
+            )(*(slabs[k] for k in shifts), *air_out)
+        ]
+    air_out = air_out[0]
     return (air_out, level_out, fuel_out)
 
 

time: 63.9 us -> 62.9 us (0.984)
  Pallas kernels: 30.4 us -> 29.7 us
    ppermute x9, waiting for transfers between devices: 14.6 us -> 13.1 us  [turn(): lax.ppermute(values[k], BANDS, [(i, (i + k) % bands) for i in range(bands)])]
    ppermute x1, waiting for transfers between devices: 0.09 us -> 1.1 us  [local(): fire_down = lax.ppermute(up, 'tile', sink)]
    pallas_call x1 -> x2, Pallas kernels: 1.72 us -> 1.6 us  [local(): pl.pallas_call(functools.partial(unpack_kernel, bands, shifts), out_shape...]
  transfers between devices with their start and end apart: 13 -> 13, of which waited for: 6 -> 6; matrix products, arithmetic and copies ran while one was open for 0% -> 0% of each run, Pallas kernels for 11% -> 12%
where the time goes in v5:
time: 62.9 us; the launch traced here: 62.7 us
  Pallas kernels  29.7 us (47%)
  starting transfers between devices  17.2 us (27%)
  waiting for transfers between devices  14.2 us (23%)
  between operations  0.85 us (1%)
  local copies, waits for them, and re-layouts  0.71 us (1%)
    pallas_call x1, Pallas kernels, local(): pl.pallas_call(functools.partial(main_kernel, bands), out_shape=[shape(ro...  18.1 us
    ppermute x9, waiting for transfers between devices, turn(): lax.ppermute(values[k], BANDS, [(i, (i + k) % bands) for i in range(bands)])  13.1 us
    ppermute x9, starting transfers between devices, turn(): lax.ppermute(values[k], BANDS, [(i, (i + k) % bands) for i in range(bands)])  7.69 us
    pallas_call x1, Pallas kernels, local(): pl.pallas_call(functools.partial(first_kernel, bands), out_shape=[shape(*...  5.05 us
    ppermute x1, starting transfers between devices, local(): edge_up = lax.ppermute(down, 'tile', rise)  3.47 us
    ppermute x1, starting transfers between devices, local(): fire_up = lax.ppermute(down, 'tile', rise)  3.34 us
    pallas_call x1, Pallas kernels, local(): pl.pallas_call(functools.partial(pack_kernel, bands), out_shape=[shape(si...  2.74 us
    pallas_call x2, Pallas kernels, local(): pl.pallas_call(functools.partial(unpack_kernel, bands, shifts), out_shape...  1.6 us
  transfers between devices with their start and end apart: 13, of which 6 were waited for; matrix products, arithmetic and copies ran while one was open for 0% of the time, Pallas kernels for 12%

profile of v5, /device:TPU:1, one launch (start us, length us, event | category | flops | bytes accessed | tf_op | source)
XLA Modules:
  0.0 62.7 jit_solution(15183917111659234129)
XLA Ops:
  0.6 2.7 %pack.1 = (f32[65,8,128]{2,1,0:T(8,128)}, f32[45,8,128]{2,1,0:T(8,128)}, f32[65,8,128]{2,1,0:T(8,128)}, f32[5,144,128]{2,1,0:T(8,128)}, f32[5,144,128]{2,1,0:T(8,128)}) custom-call(f32[4,20,8,256]{3,2,1,0:T(8,128)} %air_ref.1, f32[80,640]{1,0:T(8,128)} %level_in.1, f32[80,640]{1,0:T(8,128)} %fuel_in.1, s32[80,640]{1,0:T(8,128)} %class_ref.1, s32[80,640]{1,0:T(8,128)} %ignite_in.1), custom_call_target="tpu_custom_call" | custom-call | tf_op jit(solution)/shard_map/pack/pallas_call | solution.py:761
  3.4 2.1 %collective-permute-start.2 = (f32[45,8,128]{2,1,0:T(8,128)}, f32[45,8,128]{2,1,0:T(8,128)S(1)}, u32[]{:S(2)}, u32[]{:S(2)}) collective-permute-start(f32[45,8,128]{2,1,0:T(8,128)} %get-tuple-element.35), channel_id=1, source_target_pairs={{0,2},{1,3},{2,0},{3,1},{4,6},{5,7},{6,4},{7,5},{8,10},{9,11},{10,... | collective-permute-start | bytes 552968 | tf_op jit(solution)/shard_map/ppermute | solution.py:792
  5.5 1.0 %collective-permute-start = (f32[65,8,128]{2,1,0:T(8,128)}, f32[65,8,128]{2,1,0:T(8,128)S(1)}, u32[]{:S(2)}, u32[]{:S(2)}) collective-permute-start(f32[65,8,128]{2,1,0:T(8,128)} %get-tuple-element.33), channel_id=1, source_target_pairs={{0,3},{1,0},{2,1},{3,2},{4,7},{5,4},{6,5},{7,6},{8,11},{9,8},{10,9... | collective-permute-start | bytes 798728 | tf_op jit(solution)/shard_map/ppermute | solution.py:792
  6.4 0.8 %collective-permute-start.1 = (f32[65,8,128]{2,1,0:T(8,128)}, f32[65,8,128]{2,1,0:T(8,128)S(1)}, u32[]{:S(2)}, u32[]{:S(2)}) collective-permute-start(f32[65,8,128]{2,1,0:T(8,128)} %get-tuple-element.34), channel_id=1, source_target_pairs={{0,1},{1,2},{2,3},{3,0},{4,5},{5,6},{6,7},{7,4},{8,9},{9,10},{10,1... | collective-permute-start | bytes 798728 | tf_op jit(solution)/shard_map/ppermute | solution.py:792
  7.2 3.3 %collective-permute-start.3 = (f32[5,144,128]{2,1,0:T(8,128)}, f32[5,144,128]{2,1,0:T(8,128)S(1)}, u32[]{:S(2)}, u32[]{:S(2)}) collective-permute-start(f32[5,144,128]{2,1,0:T(8,128)} %get-tuple-element.37), channel_id=1, source_target_pairs={{0,4},{4,8},{8,12},{1,5},{5,9},{9,13},{2,6},{6,10},{10,14},{3,7},{... | collective-permute-start | bytes 1105928 | tf_op jit(solution)/shard_map/ppermute | solution.py:795
  10.6 1.3 %collective-permute-start.4 = (f32[5,144,128]{2,1,0:T(8,128)}, f32[5,144,128]{2,1,0:T(8,128)S(1)}, u32[]{:S(2)}, u32[]{:S(2)}) collective-permute-start(f32[5,144,128]{2,1,0:T(8,128)} %get-tuple-element.38), channel_id=1, source_target_pairs={{4,0},{8,4},{12,8},{5,1},{9,5},{13,9},{6,2},{10,6},{14,10},{7,3},{... | collective-permute-start | bytes 1105928 | tf_op jit(solution)/shard_map/ppermute | solution.py:796
  11.9 0.0 copy-start.5
  11.9 0.0 copy-start.7
  12.0 0.6 copy-done.5
  12.6 0.0 copy-done.6
  12.6 0.0 copy-done.7
  12.6 0.2 keep.1.refs_0_
  12.9 3.7 %collective-permute-done.refs_3_.next_ref = f32[65,8,128]{2,1,0:T(8,128)S(1)} collective-permute-done((f32[65,8,128]{2,1,0:T(8,128)}, f32[65,8,128]{2,1,0:T(8,128)S(1)}, u32[]{:S(2)}, u32[]{:S(2)}) %collective-permute-start) | collective-permute-done | bytes 266272 | tf_op jit(solution)/shard_map/ppermute | solution.py:792
  16.6 0.3 relay.1
  16.9 3.5 %collective-permute-start.8 = (f32[90,8,128]{2,1,0:T(8,128)S(1)}, f32[90,8,128]{2,1,0:T(8,128)S(1)}, u32[]{:S(2)}, u32[]{:S(2)}) collective-permute-start(f32[90,8,128]{2,1,0:T(8,128)S(1)} %get-tuple-element.51), channel_id=1, source_target_pairs={{0,4},{4,8},{8,12},{1,5},{5,9},{9,13},{2,6},{6,10},{10,14},{3,7},{... | collective-permute-start | bytes 1105928 | tf_op jit(solution)/shard_map/ppermute | solution.py:809
  20.4 0.0 copy-start.1
  20.4 1.4 %collective-permute-start.9 = (f32[90,8,128]{2,1,0:T(8,128)S(1)}, f32[90,8,128]{2,1,0:T(8,128)S(1)}, u32[]{:S(2)}, u32[]{:S(2)}) collective-permute-start(f32[90,8,128]{2,1,0:T(8,128)S(1)} %get-tuple-element.52), channel_id=1, source_target_pairs={{4,0},{8,4},{12,8},{5,1},{9,5},{13,9},{6,2},{10,6},{14,10},{7,3},{... | collective-permute-start | bytes 1105928 | tf_op jit(solution)/shard_map/ppermute | solution.py:810
  21.8 1.1 %collective-permute-done.4.down_ref.refs_1_ = f32[5,144,128]{2,1,0:T(8,128)S(1)} collective-permute-done((f32[5,144,128]{2,1,0:T(8,128)}, f32[5,144,128]{2,1,0:T(8,128)S(1)}, u32[]{:S(2)}, u32[]{:S(2)}) %collective-permute-start.4) | collective-permute-done | bytes 368672 | tf_op jit(solution)/shard_map/ppermute | solution.py:796
  22.9 0.2 corners.1
  23.1 0.7 %collective-permute-start.6 = (f32[2,8,128]{2,1,0:T(8,128)S(1)}, f32[2,8,128]{2,1,0:T(8,128)S(1)}, u32[]{:S(2)}, u32[]{:S(2)}) collective-permute-start(f32[2,8,128]{2,1,0:T(8,128)S(1)} %get-tuple-element.41), channel_id=1, source_target_pairs={{0,2},{1,3},{2,0},{3,1},{4,6},{5,7},{6,4},{7,5},{8,10},{9,11},{10,... | collective-permute-start | bytes 24584 | tf_op jit(solution)/shard_map/ppermute | solution.py:792
  23.8 1.8 %collective-permute-start.5 = (f32[19,8,128]{2,1,0:T(8,128)S(1)}, f32[19,8,128]{2,1,0:T(8,128)S(1)}, u32[]{:S(2)}, u32[]{:S(2)}) collective-permute-start(f32[19,8,128]{2,1,0:T(8,128)S(1)} %get-tuple-element.40), channel_id=1, source_target_pairs={{0,1},{1,2},{2,3},{3,0},{4,5},{5,6},{6,7},{7,4},{8,9},{9,10},{10,1... | collective-permute-start | bytes 233480 | tf_op jit(solution)/shard_map/ppermute | solution.py:792
  25.6 1.5 %survey.1 = (f32[5,160,128]{2,1,0:T(8,128)S(1)}, f32[5,160,128]{2,1,0:T(8,128)S(1)}, f32[5,160,128]{2,1,0:T(8,128)S(1)}, f32[5,160,128]{2,1,0:T(8,128)S(1)}) custom-call(f32[5,13]{1,0:T(8,128)S(1)} %stack.23.tables_ref, s32[80,640]{1,0:T(8,128)S(1)} %copy-done.1, f32[5,144,128]{2,1,0:T(8,128)S(1)} %collective-permute-done.3.up_ref.refs_0_, ...), custom_call_target="tpu_custom_call" | custom-call | flops 1000000000 | tf_op jit(solution)/shard_map/survey/pallas_call | solution.py:824
  27.2 2.5 %collective-permute-done.7.refs_5_ = f32[19,8,128]{2,1,0:T(8,128)S(1)} collective-permute-done((f32[19,8,128]{2,1,0:T(8,128)S(1)}, f32[19,8,128]{2,1,0:T(8,128)S(1)}, u32[]{:S(2)}, u32[]{:S(2)}) %collective-permute-start.7) | collective-permute-done | bytes 77856 | tf_op jit(solution)/shard_map/ppermute | solution.py:792
  29.7 5.0 %first.1 = (f32[6,176,128]{2,1,0:T(8,128)S(1)}, f32[6,176,128]{2,1,0:T(8,128)S(1)}, f32[6,176,128]{2,1,0:T(8,128)S(1)}, f32[4,8,128]{2,1,0:T(8,128)S(1)}, f32[16...) custom-call(f32[5,13]{1,0:T(8,128)S(1)} %stack.23.tables_ref, ...), custom_call_target="tpu_custom_call" | custom-call | flops 3000000000 | tf_op jit(solution)/shard_map/first/pallas_call | solution.py:837
  34.8 18.1 %window.1 = (f32[80,640]{1,0:T(8,128)}, f32[80,640]{1,0:T(8,128)}, f32[40,8,128]{2,1,0:T(8,128)S(1)}, f32[40,8,128]{2,1,0:T(8,128)S(1)}, f32[40,8,128]{2,1,0:T(8,128)S(1)}, /*index=5*/f32[40,8,128]{2,1,0:T(8,128)S(1)}) custom-call(f32[5,13]{1,0:T(8,128)S(1)} %stack.23.tables_ref, f32[6,176,128]{2,1,0:T(8,128)S(1)} %get-tuple-element.47.level_in, ...), custom_call_target="tpu_custom_call" | custom-call | tf_op jit(solution)/shard_map/window/pallas_call | solution.py:859
  52.9 0.6 collective-permute-start.10
  53.4 0.8 %collective-permute-start.11 = (f32[40,8,128]{2,1,0:T(8,128)S(1)}, f32[40,8,128]{2,1,0:T(8,128)S(1)}, u32[]{:S(2)}, u32[]{:S(2)}) collective-permute-start(f32[40,8,128]{2,1,0:T(8,128)S(1)} %get-tuple-element.58), channel_id=1, source_target_pairs={{0,3},{1,0},{2,1},{3,2},{4,7},{5,4},{6,5},{7,6},{8,11},{9,8},{10,9... | collective-permute-start | bytes 491528 | tf_op jit(solution)/shard_map/ppermute | solution.py:792
  54.2 0.9 %collective-permute-done.12.refs_1_ = f32[40,8,128]{2,1,0:T(8,128)S(1)} collective-permute-done((f32[40,8,128]{2,1,0:T(8,128)S(1)}, f32[40,8,128]{2,1,0:T(8,128)S(1)}, u32[]{:S(2)}, u32[]{:S(2)}) %collective-permute-start.12) | collective-permute-done | bytes 163872 | tf_op jit(solution)/shard_map/ppermute | solution.py:792
  55.1 0.4 unpack_0.1.refs_2_
  55.5 4.3 %collective-permute-done.10.refs_0_ = f32[40,8,128]{2,1,0:T(8,128)S(1)} collective-permute-done((f32[40,8,128]{2,1,0:T(8,128)S(1)}, f32[40,8,128]{2,1,0:T(8,128)S(1)}, u32[]{:S(2)}, u32[]{:S(2)}) %collective-permute-start.10) | collective-permute-done | bytes 163872 | tf_op jit(solution)/shard_map/ppermute | solution.py:792
  59.8 1.6 %collective-permute-done.11.refs_1_ = f32[40,8,128]{2,1,0:T(8,128)S(1)} collective-permute-done((f32[40,8,128]{2,1,0:T(8,128)S(1)}, f32[40,8,128]{2,1,0:T(8,128)S(1)}, u32[]{:S(2)}, u32[]{:S(2)}) %collective-permute-start.11) | collective-permute-done | bytes 163872 | tf_op jit(solution)/shard_map/ppermute | solution.py:792
  61.4 1.2 %unpack_2.1 = f32[4,20,8,256]{3,2,1,0:T(8,128)} custom-call(f32[40,8,128]{2,1,0:T(8,128)S(1)} %collective-permute-done.10.refs_0_, f32[40,8,128]{2,1,0:T(8,128)S(1)} %collective-permute-done.11.refs_1_, f32[4,20,8,256]{3,2,1,0:T(8,128)S(1)} %unpack_0.1.refs_2_), custom_call_target="tpu_custom_call" | custom-call | flops 1000000000 | tf_op jit(solution)/shard_map/unpack_2/pallas_call | solution.py:884
  (26 shorter events, 0.1 us)
Async XLA Ops:
  0.6 12.0 %copy-start = (f32[4,20,8,256]{3,2,1,0:T(8,128)S(1)}, f32[4,20,8,256]{3,2,1,0:T(8,128)}, u32[]{:S(2)}) copy-start(f32[4,20,8,256]{3,2,1,0:T(8,128)} %air_ref.1) | copy-start | bytes 1966084
  3.4 9.5 %collective-permute-start.2 = (f32[45,8,128]{2,1,0:T(8,128)}, f32[45,8,128]{2,1,0:T(8,128)S(1)}, u32[]{:S(2)}, u32[]{:S(2)}) collective-permute-start(f32[45,8,128]{2,1,0:T(8,128)} %get-tuple-element.35), channel_id=1, source_target_pairs={{0,2},{1,3},{2,0},{3,1},{4,6},{5,7},{6,4},{7,5},{8,10},{9,11},{10,... | collective-permute-start | bytes 552968 | tf_op jit(solution)/shard_map/ppermute | solution.py:792
  5.5 11.1 %collective-permute-start = (f32[65,8,128]{2,1,0:T(8,128)}, f32[65,8,128]{2,1,0:T(8,128)S(1)}, u32[]{:S(2)}, u32[]{:S(2)}) collective-permute-start(f32[65,8,128]{2,1,0:T(8,128)} %get-tuple-element.33), channel_id=1, source_target_pairs={{0,3},{1,0},{2,1},{3,2},{4,7},{5,4},{6,5},{7,6},{8,11},{9,8},{10,9... | collective-permute-start | bytes 798728 | tf_op jit(solution)/shard_map/ppermute | solution.py:792
  6.4 5.5 %copy-start.8 = (f32[13]{0:T(128)S(1)}, f32[13]{0:T(128)}, u32[]{:S(2)}) copy-start(f32[13]{0:T(128)} %param.19) | copy-start | bytes 160
  6.4 10.2 %collective-permute-start.1 = (f32[65,8,128]{2,1,0:T(8,128)}, f32[65,8,128]{2,1,0:T(8,128)S(1)}, u32[]{:S(2)}, u32[]{:S(2)}) collective-permute-start(f32[65,8,128]{2,1,0:T(8,128)} %get-tuple-element.34), channel_id=1, source_target_pairs={{0,1},{1,2},{2,3},{3,0},{4,5},{5,6},{6,7},{7,4},{8,9},{9,10},{10,1... | collective-permute-start | bytes 798728 | tf_op jit(solution)/shard_map/ppermute | solution.py:792
  7.2 4.7 %copy-start.9 = (s32[4]{0:T(128)S(1)}, s32[4]{0:T(128)}, u32[]{:S(2)}) copy-start(s32[4]{0:T(128)} %param.15) | copy-start | bytes 52
  7.2 14.6 %collective-permute-start.3 = (f32[5,144,128]{2,1,0:T(8,128)}, f32[5,144,128]{2,1,0:T(8,128)S(1)}, u32[]{:S(2)}, u32[]{:S(2)}) collective-permute-start(f32[5,144,128]{2,1,0:T(8,128)} %get-tuple-element.37), channel_id=1, source_target_pairs={{0,4},{4,8},{8,12},{1,5},{5,9},{9,13},{2,6},{6,10},{10,14},{3,7},{... | collective-permute-start | bytes 1105928 | tf_op jit(solution)/shard_map/ppermute | solution.py:795
  10.6 12.3 %collective-permute-start.4 = (f32[5,144,128]{2,1,0:T(8,128)}, f32[5,144,128]{2,1,0:T(8,128)S(1)}, u32[]{:S(2)}, u32[]{:S(2)}) collective-permute-start(f32[5,144,128]{2,1,0:T(8,128)} %get-tuple-element.38), channel_id=1, source_target_pairs={{4,0},{8,4},{12,8},{5,1},{9,5},{13,9},{6,2},{10,6},{14,10},{7,3},{... | collective-permute-start | bytes 1105928 | tf_op jit(solution)/shard_map/ppermute | solution.py:796
  11.9 0.7 %copy-start.5 = (f32[13]{0:T(128)S(1)}, f32[13]{0:T(128)}, u32[]{:S(2)}) copy-start(f32[13]{0:T(128)} %param.16) | copy-start | bytes 160
  11.9 0.7 %copy-start.6 = (f32[13]{0:T(128)S(1)}, f32[13]{0:T(128)}, u32[]{:S(2)}) copy-start(f32[13]{0:T(128)} %param.17) | copy-start | bytes 160
  11.9 0.7 %copy-start.7 = (f32[13]{0:T(128)S(1)}, f32[13]{0:T(128)}, u32[]{:S(2)}) copy-start(f32[13]{0:T(128)} %param.18) | copy-start | bytes 160
  16.9 17.9 %collective-permute-start.8 = (f32[90,8,128]{2,1,0:T(8,128)S(1)}, f32[90,8,128]{2,1,0:T(8,128)S(1)}, u32[]{:S(2)}, u32[]{:S(2)}) collective-permute-start(f32[90,8,128]{2,1,0:T(8,128)S(1)} %get-tuple-element.51), channel_id=1, source_target_pairs={{0,4},{4,8},{8,12},{1,5},{5,9},{9,13},{2,6},{6,10},{10,14},{3,7},{... | collective-permute-start | bytes 1105928 | tf_op jit(solution)/shard_map/ppermute | solution.py:809
  20.4 5.2 %copy-start.1 = (s32[80,640]{1,0:T(8,128)S(1)}, s32[80,640]{1,0:T(8,128)}, u32[]{:S(2)}) copy-start(s32[80,640]{1,0:T(8,128)} %class_ref.1) | copy-start | bytes 614404
  20.4 14.4 %collective-permute-start.9 = (f32[90,8,128]{2,1,0:T(8,128)S(1)}, f32[90,8,128]{2,1,0:T(8,128)S(1)}, u32[]{:S(2)}, u32[]{:S(2)}) collective-permute-start(f32[90,8,128]{2,1,0:T(8,128)S(1)} %get-tuple-element.52), channel_id=1, source_target_pairs={{4,0},{8,4},{12,8},{5,1},{9,5},{13,9},{6,2},{10,6},{14,10},{7,3},{... | collective-permute-start | bytes 1105928 | tf_op jit(solution)/shard_map/ppermute | solution.py:810
  23.1 4.1 %collective-permute-start.6 = (f32[2,8,128]{2,1,0:T(8,128)S(1)}, f32[2,8,128]{2,1,0:T(8,128)S(1)}, u32[]{:S(2)}, u32[]{:S(2)}) collective-permute-start(f32[2,8,128]{2,1,0:T(8,128)S(1)} %get-tuple-element.41), channel_id=1, source_target_pairs={{0,2},{1,3},{2,0},{3,1},{4,6},{5,7},{6,4},{7,5},{8,10},{9,11},{10,... | collective-permute-start | bytes 24584 | tf_op jit(solution)/shard_map/ppermute | solution.py:792
  23.8 3.3 %collective-permute-start.5 = (f32[19,8,128]{2,1,0:T(8,128)S(1)}, f32[19,8,128]{2,1,0:T(8,128)S(1)}, u32[]{:S(2)}, u32[]{:S(2)}) collective-permute-start(f32[19,8,128]{2,1,0:T(8,128)S(1)} %get-tuple-element.40), channel_id=1, source_target_pairs={{0,1},{1,2},{2,3},{3,0},{4,5},{5,6},{6,7},{7,4},{8,9},{9,10},{10,1... | collective-permute-start | bytes 233480 | tf_op jit(solution)/shard_map/ppermute | solution.py:792
  25.6 4.1 %copy-start.2 = (f32[80,640]{1,0:T(8,128)S(1)}, f32[80,640]{1,0:T(8,128)}, u32[]{:S(2)}) copy-start(f32[80,640]{1,0:T(8,128)} %level_in.1) | copy-start | bytes 614404
  25.6 4.1 %copy-start.3 = (f32[80,640]{1,0:T(8,128)S(1)}, f32[80,640]{1,0:T(8,128)}, u32[]{:S(2)}) copy-start(f32[80,640]{1,0:T(8,128)} %fuel_in.1) | copy-start | bytes 614404
  25.6 4.1 %copy-start.4 = (s32[80,640]{1,0:T(8,128)S(1)}, s32[80,640]{1,0:T(8,128)}, u32[]{:S(2)}) copy-start(s32[80,640]{1,0:T(8,128)} %ignite_in.1) | copy-start | bytes 614404
  25.6 4.1 %collective-permute-start.7 = (f32[19,8,128]{2,1,0:T(8,128)S(1)}, f32[19,8,128]{2,1,0:T(8,128)S(1)}, u32[]{:S(2)}, u32[]{:S(2)}) collective-permute-start(f32[19,8,128]{2,1,0:T(8,128)S(1)} %get-tuple-element.42), channel_id=1, source_target_pairs={{0,3},{1,0},{2,1},{3,2},{4,7},{5,4},{6,5},{7,6},{8,11},{9,8},{10,9... | collective-permute-start | bytes 233480 | tf_op jit(solution)/shard_map/ppermute | solution.py:792
  52.9 2.3 %collective-permute-start.12 = (f32[40,8,128]{2,1,0:T(8,128)S(1)}, f32[40,8,128]{2,1,0:T(8,128)S(1)}, u32[]{:S(2)}, u32[]{:S(2)}) collective-permute-start(f32[40,8,128]{2,1,0:T(8,128)S(1)} %get-tuple-element.60), channel_id=1, source_target_pairs={{0,1},{1,2},{2,3},{3,0},{4,5},{5,6},{6,7},{7,4},{8,9},{9,10},{10,1... | collective-permute-start | bytes 491528 | tf_op jit(solution)/shard_map/ppermute | solution.py:792
  52.9 6.9 %collective-permute-start.10 = (f32[40,8,128]{2,1,0:T(8,128)S(1)}, f32[40,8,128]{2,1,0:T(8,128)S(1)}, u32[]{:S(2)}, u32[]{:S(2)}) collective-permute-start(f32[40,8,128]{2,1,0:T(8,128)S(1)} %get-tuple-element.57), channel_id=1, source_target_pairs={{0,2},{1,3},{2,0},{3,1},{4,6},{5,7},{6,4},{7,5},{8,10},{9,11},{10,... | collective-permute-start | bytes 491528 | tf_op jit(solution)/shard_map/ppermute | solution.py:792
  53.4 8.0 %collective-permute-start.11 = (f32[40,8,128]{2,1,0:T(8,128)S(1)}, f32[40,8,128]{2,1,0:T(8,128)S(1)}, u32[]{:S(2)}, u32[]{:S(2)}) collective-permute-start(f32[40,8,128]{2,1,0:T(8,128)S(1)} %get-tuple-element.58), channel_id=1, source_target_pairs={{0,3},{1,0},{2,1},{3,2},{4,7},{5,4},{6,5},{7,6},{8,11},{9,8},{10,9... | collective-permute-start | bytes 491528 | tf_op jit(solution)/shard_map/ppermute | solution.py:792
